TPU v7x, 32 devices: a whole 2x2x4 slice. The times are simulated.
32 devices in a mesh: dp: 2 (over x), mp: 4 (over y, core), width: 4 (over z).
Axes of the slice: x: 2, y: 2, z: 4, core: 2. Of those that a mesh axis runs over, the one named last changes fastest.
Arguments:
- tokens: bfloat16 [16, 1024, 512], P(('dp', 'width'), 'mp'), may hold values from -6 to 6
- segments: int32 [16, 1024], P(('dp', 'width')), may hold values from -1 to 7, as said below
- cotangent: bfloat16 [16, 1024, 512], P(('dp', 'width'), 'mp'), may hold values from -6 to 6
- norm_gains: bfloat16 [2, 2, 512], P(None, None, ('dp', 'width')), may hold values from 0.5 to 1.5
- biases: bfloat16 [2, 4, 512], P(None, None, ('dp', 'width')), may hold values from -3 to 3
- w_qkv: bfloat16 [2, 512, 3, 512], P(None, ('dp', 'width'), None, 'mp'), may hold values from -0.375 to 0.375
- w_out: bfloat16 [2, 512, 512], P(None, 'mp', ('dp', 'width')), may hold values from -3 to 3
- w_gate: bfloat16 [2, 2, 512, 512], P(None, None, ('dp', 'width'), 'mp'), may hold values from -0.25 to 0.25
- w_up: bfloat16 [2, 512, 2048], P(None, ('dp', 'width'), 'mp'), may hold values from -0.25 to 0.25
- w_down: bfloat16 [2, 2048, 512], P(None, 'mp', ('dp', 'width')), may hold values from -0.125 to 0.125
Outputs:
- output: float32 [16, 1024, 512], P(('dp', 'width'), 'mp')
- d_tokens: float32 [16, 1024, 512], P(('dp', 'width'), 'mp')
- d_norm_gains: float32 [2, 2, 512], P(None, None, ('dp', 'width'))
- d_norm_biases: float32 [2, 2, 512], P(None, None, ('dp', 'width'))
- d_gate_biases: float32 [2, 2, 512], P(None, None, ('dp', 'width'))
- d_w_qkv: float32 [2, 512, 3, 512], P(None, ('dp', 'width'), None, 'mp')
- d_w_out: float32 [2, 512, 512], P(None, 'mp', ('dp', 'width'))
- d_w_gate: float32 [2, 2, 512, 512], P(None, None, ('dp', 'width'), 'mp')
- d_w_up: float32 [2, 512, 2048], P(None, ('dp', 'width'), 'mp')
- d_w_down: float32 [2, 2048, 512], P(None, 'mp', ('dp', 'width'))
Inputs may be any that keep to these rules, and one draw needn't show every extreme that they name: `segments`: ids never fall along a packed row; -1 marks padding, which fills the end of a row. Of the 2 rows of one index of dp and width, one, chosen by the seed, is a single sequence of 1024 positions; every other row holds sequences 0 to 7, each of 32 to 64 positions, then padding.
All inputs are finite; a program needn't handle non-finite values.
Results may differ from a plain program's by a relative error of at most 0.025.
Values may be sent and summed in bfloat16 or wider, within the bound.
No kernel may reach another device: no remote copies, remote signals or barrier semaphores. Data moves between devices by JAX's collectives and lax.ppermute only.
A program may use at most 192 MiB of HBM per device.

v0:
```python
import functools

import jax
import jax.numpy as jnp
from jax import lax
from jax.experimental import pallas as pl
from jax.experimental.pallas import tpu as pltpu
from jax.sharding import PartitionSpec as P

HEAD_DIM = 64
LANE = 128
NORM_EPS = 1e-05
SPAN = 256
CHUNK = 64

VALUES_MB = {
    "attend": 6,
    "second": 10,
    "second_back": 10,
    "attend_back": 8,
    "first_back": 6,
    "weight_grad": 8,
    "relay": 1,
    "stack": 2,
    "add": 2,
    "pack": 2,
    "finish": 4,
}

KERNEL_US = {
    "attend": 8,
    "second": 12,
    "second_back": 10,
    "attend_back": 9,
    "first_back": 4,
    "weight_grad": 8,
    "relay": 1,
    "stack": 0.1,
    "add": 1,
    "pack": 10,
    "finish": 2,
}

F32 = jnp.float32
BF16 = jnp.bfloat16


def nn(a, b):
    return jnp.dot(a, b, preferred_element_type=F32)


def nt(a, b):
    return lax.dot_general(a, b, (((1,), (1,)), ((), ())), preferred_element_type=F32)


def tn(a, b):
    return lax.dot_general(a, b, (((0,), (0,)), ((), ())), preferred_element_type=F32)


def sds(shape, dtype):
    return jax.ShapeDtypeStruct(shape, dtype)


class Late:
    def __init__(self, array):
        self.array = array


class Copies:
    def __init__(self, pairs, first_out, sems):
        self.first_out = first_out
        self.all = [
            (ref, pltpu.make_async_copy(*pair, sems.at[i]))
            for i, (ref, *pair) in enumerate(pairs)
        ]
        self.waiting = []
        self.unsent = list(self.all[first_out:])
        for ref, copy in self.all[:first_out]:
            copy.start()
            self.waiting.append((ref, copy))

    def need(self, *refs):
        for ref in refs:
            for i, entry in enumerate(self.waiting):
                if entry[0] is ref:
                    entry[1].wait()
                    del self.waiting[i]
                    break

    def send(self, *refs):
        for ref in refs:
            for i, entry in enumerate(self.unsent):
                if entry[0] is ref:
                    entry[1].start()
                    del self.unsent[i]
                    break

    def finish(self):
        for _, copy in self.waiting:
            copy.wait()
        for _, copy in self.unsent:
            copy.start()
        for _, copy in self.all[self.first_out :]:
            copy.wait()


class Chain:
    def __init__(self):
        self.token = None
        self.copies = None


ORDER = Chain()


def need(*refs):
    ORDER.copies.need(*refs)


def send(*refs):
    ORDER.copies.send(*refs)


def in_hbm(a):
    return pltpu.with_memory_space_constraint(a, pltpu.HBM)


def size_of(a):
    return a.size * a.dtype.itemsize


def call(body, name, out_shape, args, smem=0, parts=(), scratch=(), after=()):
    after = list(after) + ([] if ORDER.token is None else [ORDER.token])
    late_in = [i for i, a in enumerate(args) if isinstance(a, Late)]
    late_out = [i for i, o in enumerate(out_shape) if isinstance(o, Late)]
    args = [in_hbm(a.array) if isinstance(a, Late) else a for a in args]
    out_shape = [o.array if isinstance(o, Late) else o for o in out_shape]
    parts = [in_hbm(a) for a in parts]
    hbm, vmem = (pl.BlockSpec(memory_space=space) for space in (pltpu.HBM, pltpu.VMEM))
    specs = [pl.BlockSpec(memory_space=pltpu.SMEM)] * smem
    specs += [hbm if i in late_in else vmem for i in range(smem, len(args))]
    specs += [hbm] * len(parts)
    specs += [pl.BlockSpec(memory_space=pl.ANY)] * len(after)
    used = len(args) + len(parts)
    given = used + len(after)
    outs = len(out_shape)
    late = [args[i] for i in late_in] + [out_shape[i] for i in late_out]
    room = [pltpu.VMEM(a.shape, a.dtype) for a in late]
    sems = [pltpu.SemaphoreType.DMA((len(late),))] if late else []

    def inner(*refs):
        ins, results = list(refs[:used]), list(refs[given : given + outs])
        rest = refs[given + outs + 1 :]
        own = rest[: len(scratch)]
        places = rest[len(scratch) : len(scratch) + len(late)]
        pairs = []
        for i, place in zip(late_in, places):
            pairs.append((place, ins[i], place))
            ins[i] = place
        for i, place in zip(late_out, places[len(late_in) :]):
            pairs.append((place, place, results[i]))
            results[i] = place
        copies = ORDER.copies = Copies(pairs, len(late_in), rest[-1] if late else None)
        body(*ins, *results, *own)
        copies.finish()

    nbytes = sum(size_of(a) for a in args + out_shape)
    for s in scratch:
        if hasattr(s, "shape") and len(s.shape) > 1:
            nbytes += size_of(jax.ShapeDtypeStruct(s.shape, s.dtype))
    *result, ORDER.token = pl.pallas_call(
        inner,
        name=name,
        out_shape=[
            pltpu.HBM(o.shape, o.dtype) if i in late_out else o for i, o in enumerate(out_shape)
        ]
        + [sds((8, LANE), F32)],
        in_specs=specs,
        out_specs=[hbm if i in late_out else vmem for i in range(outs)]
        + [pl.BlockSpec(memory_space=pl.ANY)],
        scratch_shapes=list(scratch) + room + sems,
        cost_estimate=pl.CostEstimate(
            flops=int(5 * KERNEL_US[name] * 1.1e9),
            bytes_accessed=int(5 * KERNEL_US[name] * 3.6e6),
            transcendentals=0,
        ),
        compiler_params=pltpu.CompilerParams(
            vmem_limit_bytes=int(1.02 * nbytes) + VALUES_MB[name] * 2**20
        ),
    )(*args, *parts, *after)
    return result


def col(start):
    return pl.multiple_of(start, LANE)


class Parts:
    def __init__(self, arrays, order, first_rows, rows):
        self.arrays = arrays
        self.order = order
        self.first_rows = first_rows if isinstance(first_rows, list) else [first_rows] * len(arrays)
        self.rows = rows

    def open(self, refs, me_ref, dst, sem, chunks, own_only=False):
        if self.order is None:
            rows = pl.ds(self.first_rows[0], self.rows)
            src = refs[0].at[:, rows, :]
            if own_only:
                src = refs[0].at[pl.ds(me_ref[0] * chunks, chunks), rows, :]
            pltpu.make_async_copy(src, dst, sem).start()
            return Blocks(dst, sem, chunks, 0, 0)
        for ref, first_row, (mx, dx) in zip(refs, self.first_rows, self.order):
            rows = pl.ds(first_row, self.rows)
            at = pl.ds((0 if own_only else mx * chunks) + dx, ref.shape[0])
            pltpu.make_async_copy(ref.at[:, rows, :], dst.at[at], sem).start()
        return Blocks(dst, sem, chunks, 0 if own_only else me_ref[0], me_ref[1])


def others(wd, wu):
    return [a for a in wu.arrays if not any(a is b for b in wd.arrays)]


def shared(wd, wu, d_refs, refs):
    more = iter(refs)
    found, count = [], 0
    for a in wu.arrays:
        at = [i for i, b in enumerate(wd.arrays) if a is b]
        count += not at
        found.append(d_refs[at[0]] if at else next(more))
    return found, refs[count:]


class Blocks:
    def __init__(self, ref, sem, chunks, turn_m, turn_d):
        self.ref, self.sem, self.chunks = ref, sem, chunks
        self.turn_m, self.turn_d = turn_m, turn_d

    def wait(self):
        pltpu.make_async_copy(self.ref, self.ref, self.sem).wait()

    def place(self, m, d):
        if isinstance(self.turn_d, int):
            return m * self.chunks + d
        return jnp.bitwise_xor(m, self.turn_m) * self.chunks + jnp.bitwise_xor(d, self.turn_d)

    def block(self, m, b, lo=0, hi=None):
        rows = pl.ds(b * CHUNK, CHUNK)
        hi = self.chunks if hi is None else hi
        return jnp.concatenate([self.ref[self.place(m, d), rows, :] for d in range(lo, hi)], axis=0)

    def wide(self, which, lo=0, hi=None):
        return jnp.concatenate([self.block(m, b, lo, hi) for m, b in which], axis=1)

    def params(self, first_row, layer):
        rows = slice(first_row + 8 * layer, first_row + 8 * layer + 8)
        share = LANE // CHUNK
        tiles = []
        for i in range(self.chunks // share):
            tile = self.ref[self.place(0, i * share), rows, :].astype(F32)
            for j in range(1, share):
                tile += self.ref[self.place(0, i * share + j), rows, :].astype(F32)
            tiles.append(tile)
        return jnp.concatenate(tiles, axis=1)


def norm_parts(x):
    mean = jnp.mean(x, axis=1, keepdims=True)
    centred = x - mean
    rstd = lax.rsqrt(jnp.mean(centred * centred, axis=1, keepdims=True) + NORM_EPS)
    return centred * rstd, rstd


def sigmoid(v):
    return 1.0 / (1.0 + jnp.exp(-v))


def rows_at(me_ref, at, part):
    return pl.ds(pl.multiple_of(me_ref[2 + at] * part, part), part)


def seg_bounds(seg_ref, row, q_at, q_spans):
    first_id = seg_ref[row, q_at * SPAN]
    first_id = jnp.where(first_id < 0, 1 << 20, first_id)
    low = jnp.int32(0)
    for kb in range(q_spans - 1):
        last_id = seg_ref[row, (kb + 1) * SPAN - 1]
        last_id = jnp.where(last_id < 0, 1 << 20, last_id)
        low += jnp.where((kb < q_at) & (last_id < first_id), 1, 0)
    return low


def allowed_t(segc_ref, segr_ref, row, k0, q0, spans):
    keys = spans * SPAN
    seg_k = segc_ref[pl.ds(k0, keys), :]
    seg_q = segr_ref[row, :, pl.ds(q0, SPAN)]
    same = jnp.concatenate([seg_k == seg_q[:, :LANE], seg_k == seg_q[:, LANE:]], axis=1)
    tri = lax.broadcasted_iota(jnp.int32, (SPAN, SPAN), 0) <= (
        lax.broadcasted_iota(jnp.int32, (SPAN, SPAN), 1)
    )
    if spans == 1:
        return same & tri
    return jnp.concatenate([same[: keys - SPAN], same[keys - SPAN :] & tri], axis=0)


def attend_body(
    wq, layer, norm_here, mp_size, chunks, batch, me_ref, seg_ref, segr_ref, *refs
):
    given = mp_size if norm_here else mp_size * batch
    t_refs, refs = refs[:given], refs[given:]
    w_refs, refs = refs[: len(wq.arrays)], refs[len(wq.arrays) :]
    qkv_ref, lse_ref = refs[:2]
    o_refs, refs = [refs[2], refs[3], refs[4].at[0], refs[4].at[1]], refs[5:]
    if norm_here:
        par_ref, n_refs, refs = refs[0], refs[1 : 1 + mp_size * batch], refs[1 + mp_size * batch :]
    w_scr, o_scr, segc_ref, sem = refs
    part = o_refs[0].shape[1]
    me_m = me_ref[0]
    w = wq.open(w_refs, me_ref, w_scr, sem, chunks, own_only=True)
    w.wait()
    if norm_here:
        for l in range(par_ref.shape[0]):
            par_ref[l] = w.params(3 * CHUNK, l)
    weights = w.wide([(0, 0), (0, 1), (0, 2)])
    q_spans = qkv_ref.shape[1] // SPAN
    for r in range(batch):
        for mx in range(mp_size):
            at = pl.ds(pl.multiple_of(jnp.bitwise_xor(me_m, mx) * part, part), part)
            if norm_here:
                xhat, _ = norm_parts(t_refs[mx][me_ref[2 + r]].astype(F32))
                n = (xhat * par_ref[layer, 0:1] + par_ref[layer, 2:3]).astype(BF16)
                n_refs[r * mp_size + mx][...] = n
                send(n_refs[r * mp_size + mx])
            else:
                n = t_refs[mx * batch + r][...]
            qkv_ref[r, at, :] = nn(n, weights).astype(BF16)
    send(qkv_ref)

    for r in range(batch):
        length = qkv_ref.shape[1]
        segc_ref[pl.ds(r * length, length), :] = jnp.broadcast_to(segr_ref[r], (LANE, length)).T

    def step(i, carry):
        r, q_at = i // q_spans, i % q_spans
        low = seg_bounds(seg_ref, r, q_at, q_spans)
        q0 = pl.multiple_of(q_at * SPAN, SPAN)
        k0 = pl.multiple_of(low * SPAN, SPAN)
        k_abs = pl.multiple_of((r * q_spans + low) * SPAN, SPAN)
        for spans in range(1, q_spans + 1):

            @pl.when(q_at - low + 1 == spans)
            def _():
                keys = spans * SPAN
                mask = allowed_t(segc_ref, segr_ref, r, k_abs, q0, spans)
                outs = []
                for h in range(2):
                    lo = h * HEAD_DIM
                    q = qkv_ref[r, pl.ds(q0, SPAN), lo : lo + HEAD_DIM] * jnp.asarray(
                        HEAD_DIM**-0.5, BF16
                    )
                    k = qkv_ref[r, pl.ds(k0, keys), 128 + lo : 128 + lo + HEAD_DIM]
                    v = qkv_ref[r, pl.ds(k0, keys), 256 + lo : 256 + lo + HEAD_DIM]
                    s = jnp.where(mask, nt(k, q), -1e30)
                    top = jnp.max(s, axis=0, keepdims=True)
                    p = jnp.exp(s - top)
                    total = jnp.sum(p, axis=0, keepdims=True)
                    lse_ref[r * 2 + h, :, pl.ds(q0, SPAN)] = top + jnp.log(total)
                    outs.append(tn(v, p.astype(BF16)) / total)
                o_scr[r, pl.ds(q0, SPAN), :] = jnp.concatenate(outs, axis=0).T.astype(BF16)

        return carry

    lax.fori_loop(0, batch * q_spans, step, 0)
    for mx in range(mp_size):
        at = pl.multiple_of(jnp.bitwise_xor(me_m, mx) * part, part)
        for r in range(batch):
            o_refs[mx][r] = o_scr[r, pl.ds(at, part), :]


def attend(me, segs, t_parts, wq, layer, layers, norm_here, chunks):
    seg, segr = segs
    batch, length = seg.shape
    mp_size = 4
    part, model = t_parts[0].shape[-2:]
    out = [sds((batch, length, 384), BF16), sds((batch * 2, 1, length), F32)]
    if norm_here:
        out = [Late(o) for o in out]
    out += [sds((batch, part, LANE), BF16)] * 2 + [sds((2, batch, part, LANE), BF16)]
    if norm_here:
        out += [sds((layers, 8, model), F32)] + [Late(sds((part, model), BF16))] * mp_size * batch
    return call(
        functools.partial(attend_body, wq, layer, norm_here, mp_size, chunks, batch),
        "attend",
        out,
        [me, seg, segr] + t_parts,
        smem=2,
        parts=wq.arrays,
        scratch=[
            pltpu.VMEM((chunks, wq.rows, LANE), BF16),
            pltpu.VMEM((batch, length, LANE), BF16),
            pltpu.VMEM((batch * length, LANE), F32),
            pltpu.SemaphoreType.DMA,
        ],
    )


def second_body(
    wd, wu, layer, mp_size, chunks, batch, has_next, me_ref, x_ref, par_ref, *refs
):
    n_refs, refs = refs[:batch], refs[batch:]
    t_refs, refs = refs[:mp_size], refs[mp_size:]
    t_refs = [t_refs[0], t_refs[1], t_refs[2].at[0], t_refs[3].at[1]]
    d_refs, refs = refs[: len(wd.arrays)], refs[len(wd.arrays) :]
    u_refs, refs = shared(wd, wu, d_refs, refs)
    att_ref, s1_ref, mid_ref, n2_ref, s2_ref, act_ref, slope_ref, out_ref = refs[:8]
    refs = refs[8:]
    if has_next:
        next_refs, refs = refs[:batch], refs[batch:]
    n_scr, d_scr, u_scr, d_sem, u_sem = refs
    w_d = wd.open(d_refs, me_ref, d_scr, d_sem, chunks)
    w_u = wu.open(u_refs, me_ref, u_scr, u_sem, chunks)
    me_m = me_ref[0]
    part = n_refs[0].shape[0]
    par = par_ref.at[layer]
    for r in range(batch):
        for mx in range(mp_size):
            m = jnp.bitwise_xor(me_m, mx)
            att_ref[rows_at(me_ref, r, part), pl.ds(col(m * LANE), LANE)] = t_refs[mx][r]
    send(att_ref)
    need(*n_refs)
    for r in range(batch):
        n_scr[rows_at(me_ref, r, part), :] = n_refs[r][...]
    n = n_scr[...]
    every = range(mp_size)
    w_d.wait()
    s1 = sigmoid(nn(n, w_d.wide([(m, 0) for m in every])) + par[3:4])
    s1_ref[...] = s1
    send(s1_ref)
    need(x_ref)
    mid = (
        x_ref[...].astype(F32)
        + nt(att_ref[...], w_d.wide([(m, 1) for m in every]))
        + s1 * n.astype(F32)
    )
    mid_ref[...] = mid
    send(mid_ref)
    xhat, _ = norm_parts(mid)
    n2_ref[...] = (xhat * par[1:2] + par[4:5]).astype(BF16)
    send(n2_ref)
    w_u.wait()
    s2_ref[...] = sigmoid(nn(n2_ref[...], w_u.wide([(m, 0) for m in every])) + par[5:6])
    send(s2_ref)
    ff_blocks = act_ref.shape[1] // (mp_size * LANE)
    for m in every:
        for b in range(0, ff_blocks, 2):
            at = (m * ff_blocks + b) * LANE
            cols = slice(at, at + 2 * LANE)
            hidden = nn(n2_ref[...], w_u.wide([(m, 1 + b), (m, 2 + b)]))
            square = hidden * hidden
            inner = 0.7978845608 + (0.7978845608 * 0.044715) * square
            th = jnp.tanh(hidden * inner)
            half = 0.5 + 0.5 * th
            act = hidden * half
            act_ref[:, cols] = act.astype(BF16)
            slope = half + act * (1.0 - th) * (3.0 * inner - 2 * 0.7978845608)
            slope_ref[:, cols] = slope.astype(BF16)
    send(act_ref, slope_ref)
    share = chunks // 2
    for j in range(2):
        cols = slice(j * share * CHUNK, (j + 1) * share * CHUNK)
        down = [(m, 2 + b) for m in every for b in range(ff_blocks)]
        out_ref[:, cols] = (
            mid_ref[:, cols]
            + s2_ref[:, cols] * n2_ref[:, cols].astype(F32)
            + nt(act_ref[...], w_d.wide(down, j * share, (j + 1) * share))
        )
    send(out_ref)
    if has_next:
        xhat, _ = norm_parts(out_ref[...])
        n_scr[...] = (xhat * par_ref[layer + 1, 0:1] + par_ref[layer + 1, 2:3]).astype(BF16)
        for r in range(batch):
            next_refs[r][...] = n_scr[rows_at(me_ref, r, part), :]


def second(me, x, par, n_rows, t_parts, wd, wu, layer, chunks, ff, has_next, after=()):
    rows, model = x.shape
    mp_size = len(t_parts)
    out = [
        sds((rows, model), BF16),
        sds((rows, model), F32),
        sds((rows, model), F32),
        sds((rows, model), BF16),
        sds((rows, model), F32),
        sds((rows, ff), BF16),
        sds((rows, ff), BF16),
        sds((rows, model), F32),
    ]
    out = [Late(o) for o in out]
    if has_next:
        out += [sds(n_rows[0].shape, BF16)] * len(n_rows)
    return call(
        functools.partial(
            second_body, wd, wu, layer, mp_size, chunks, len(n_rows), has_next
        ),
        "second",
        out,
        [me, Late(x), par] + [Late(n) for n in n_rows] + t_parts,
        smem=1,
        parts=wd.arrays + others(wd, wu),
        scratch=[
            pltpu.VMEM((rows, model), BF16),
            pltpu.VMEM((chunks * mp_size, wd.rows, LANE), BF16),
            pltpu.VMEM((chunks * mp_size, wu.rows, LANE), BF16),
            pltpu.SemaphoreType.DMA,
            pltpu.SemaphoreType.DMA,
        ],
        after=after,
    )


def norm_back(x, gain, d_normed):
    xhat, rstd = norm_parts(x)
    e = d_normed * gain
    mean_e = jnp.mean(e, axis=1, keepdims=True)
    mean_ex = jnp.mean(e * xhat, axis=1, keepdims=True)
    d_gain = jnp.sum(d_normed * xhat, axis=0, keepdims=True)
    d_bias = jnp.sum(d_normed, axis=0, keepdims=True)
    return (e - mean_e - xhat * mean_ex) * rstd, d_gain, d_bias


def second_back_body(
    wd, wu, layer, mp_size, chunks, batch, me_ref, g_ref, mid_ref, n2_ref, s2_ref, slope_ref,
    par_ref, *refs
):
    d_refs, refs = refs[: len(wd.arrays)], refs[len(wd.arrays) :]
    u_refs, refs = shared(wd, wu, d_refs, refs)
    b2_ref, dcomb_ref, gmid_ref, b1_ref, sums_ref = refs[:5]
    refs = refs[5:]
    o_refs, refs = [refs[0], refs[1], refs[2].at[0], refs[2].at[1]], refs[3:]
    o_scr, d_scr, u_scr, d_sem, u_sem = refs
    w_d = wd.open(d_refs, me_ref, d_scr, d_sem, chunks)
    w_u = wu.open(u_refs, me_ref, u_scr, u_sem, chunks)
    ff = slope_ref.shape[1]
    model = g_ref.shape[1]
    ff_m = ff // mp_size
    ff_blocks = ff_m // LANE
    stride = LANE + ff_m
    part = g_ref.shape[0] // batch
    me_m = me_ref[0]
    every = range(mp_size)
    g = g_ref[...]
    b2_ref[...] = g.astype(BF16)
    need(n2_ref, s2_ref)
    s2 = s2_ref[...]
    b2f = b2_ref[...].astype(F32)
    d_z2 = (b2f * n2_ref[...].astype(F32) * s2 * (1.0 - s2)).astype(BF16)
    sums_ref[2:3, :] = jnp.sum(d_z2.astype(F32), axis=0, keepdims=True)
    for m in every:
        dcomb_ref[:, m * stride : m * stride + LANE] = d_z2[:, m * LANE : (m + 1) * LANE]
    w_d.wait()
    need(slope_ref)
    for m in every:
        for b in range(0, ff_blocks, 2):
            at = m * ff_m + b * LANE
            d_act = nn(b2_ref[...], w_d.wide([(m, 2 + b), (m, 3 + b)]))
            slope = slope_ref[:, at : at + 2 * LANE].astype(F32)
            at = m * stride + (1 + b) * LANE
            dcomb_ref[:, at : at + 2 * LANE] = (d_act * slope).astype(BF16)
    w_u.wait()
    share = chunks // 2
    cols_of = [(m, b) for m in every for b in range(1 + ff_blocks)]
    for j in range(2):
        cols = slice(j * share * CHUNK, (j + 1) * share * CHUNK)
        gmid_ref[:, cols] = b2_ref[:, cols].astype(F32) * s2_ref[:, cols] + nt(
            dcomb_ref[...], w_u.wide(cols_of, j * share, (j + 1) * share)
        )
    need(mid_ref)
    d_mid, d_gain, d_bias = norm_back(mid_ref[...], par_ref[layer, 1:2], gmid_ref[...])
    sums_ref[0:1, :] = d_gain
    sums_ref[1:2, :] = d_bias
    sums_ref[3:8, :] = jnp.zeros((5, model), F32)
    g_mid = g_ref[...] + d_mid
    gmid_ref[...] = g_mid
    b1_ref[...] = g_mid.astype(BF16)
    for mx in every:
        m = jnp.bitwise_xor(me_m, mx)
        o_scr[...] = nn(b1_ref[...], w_d.block(m, 1)).astype(BF16)
        for r in range(batch):
            o_refs[mx][r] = o_scr[rows_at(me_ref, r, part), :]


def second_back(me, g, mid, n2, s2, slope, par, wd, wu, layer, mp_size, chunks, batch, after=()):
    rows, model = g.shape
    ff = slope.shape[1]
    out = [
        sds((rows, model), BF16),
        sds((rows, ff + LANE * mp_size), BF16),
        sds((rows, model), F32),
        sds((rows, model), BF16),
        sds((8, model), F32),
    ]
    out += [sds((batch, rows // batch, LANE), BF16)] * 2
    out += [sds((2, batch, rows // batch, LANE), BF16)]
    return call(
        functools.partial(second_back_body, wd, wu, layer, mp_size, chunks, batch),
        "second_back",
        out,
        [me, g, Late(mid), Late(n2), Late(s2), Late(slope), par],
        smem=1,
        parts=wd.arrays + others(wd, wu),
        scratch=[
            pltpu.VMEM((rows, LANE), BF16),
            pltpu.VMEM((chunks * mp_size, wd.rows, LANE), BF16),
            pltpu.VMEM((chunks * mp_size, wu.rows, LANE), BF16),
            pltpu.SemaphoreType.DMA,
            pltpu.SemaphoreType.DMA,
        ],
        after=after,
    )


def attend_back_body(wq, row, mp_size, chunks, last, me_ref, seg_ref, segr_ref, *refs):
    qkv_ref, lse_ref = refs[:2]
    d_in, refs = refs[2 : 2 + mp_size], refs[2 + mp_size :]
    d_in = [d_in[0].at[row], d_in[1].at[row], d_in[2].at[0, row], d_in[3].at[1, row]]
    n_refs, refs = refs[:mp_size], refs[mp_size:]
    if last:
        before_ref, refs = refs[0], refs[1:]
    w_refs, refs = refs[: len(wq.arrays)], refs[len(wq.arrays) :]
    keep_ref, send_ref, dw_ref = refs[:3]
    w_scr, do_scr, dqkv_scr, dk_scr, dv_scr, segc_ref, sem = refs[3:]
    w = wq.open(w_refs, me_ref, w_scr, sem, chunks, own_only=True)
    length = qkv_ref.shape[1]
    part = d_in[0].shape[0]
    me_m, me_d = me_ref[0], me_ref[1]
    for mx in range(mp_size):
        at = pl.multiple_of(jnp.bitwise_xor(me_m, mx) * part, part)
        do_scr[pl.ds(at, part), :] = d_in[mx][...]
    dqkv_scr[...] = jnp.zeros_like(dqkv_scr)
    dk_scr[...] = jnp.zeros_like(dk_scr)
    segc_ref[...] = jnp.broadcast_to(segr_ref[row], (LANE, length)).T
    dv_scr[...] = jnp.zeros_like(dv_scr)
    q_spans = length // SPAN

    def step(q_at, carry):
        low = seg_bounds(seg_ref, row, q_at, q_spans)
        real = seg_ref[row, q_at * SPAN] >= 0
        q0 = pl.multiple_of(q_at * SPAN, SPAN)
        k0 = pl.multiple_of(low * SPAN, SPAN)
        for spans in range(1, q_spans + 1):

            @pl.when(real & (q_at - low + 1 == spans))
            def _():
                keys = spans * SPAN
                mask = allowed_t(segc_ref, segr_ref, row, k0, q0, spans)
                dqs, dks, dvs = [], [], []
                for h in range(2):
                    lo = h * HEAD_DIM
                    q = qkv_ref[row, pl.ds(q0, SPAN), lo : lo + HEAD_DIM] * jnp.asarray(
                        HEAD_DIM**-0.5, BF16
                    )
                    k = qkv_ref[row, pl.ds(k0, keys), 128 + lo : 128 + lo + HEAD_DIM]
                    v = qkv_ref[row, pl.ds(k0, keys), 256 + lo : 256 + lo + HEAD_DIM]
                    do = do_scr[pl.ds(q0, SPAN), lo : lo + HEAD_DIM]
                    lse = lse_ref[row * 2 + h, :, pl.ds(q0, SPAN)]
                    p = jnp.where(mask, jnp.exp(nt(k, q) - lse), 0.0)
                    dvs.append(nn(p.astype(BF16), do))
                    dp = nt(v, do)
                    delta = jnp.sum(p * dp, axis=0, keepdims=True)
                    ds = (p * (dp - delta)).astype(BF16)
                    dks.append(nn(ds, q))
                    dqs.append(tn(k, ds))
                dqkv_scr[pl.ds(q0, SPAN), 0:128] = (
                    jnp.concatenate(dqs, axis=0).T * HEAD_DIM**-0.5
                ).astype(BF16)
                dk_scr[pl.ds(k0, keys), :] += jnp.concatenate(dks, axis=1)
                dv_scr[pl.ds(k0, keys), :] += jnp.concatenate(dvs, axis=1)

        return carry

    lax.fori_loop(0, q_spans, step, 0)
    dqkv_scr[:, 128:256] = dk_scr[...].astype(BF16)
    dqkv_scr[:, 256:384] = dv_scr[...].astype(BF16)
    w.wait()
    weights = w.wide([(0, 0), (0, 1), (0, 2)])
    need(*n_refs)
    grad = jnp.zeros((n_refs[0].shape[1], 384), F32)
    if last:
        grad = before_ref[...]
    for mx in range(mp_size):
        at = pl.multiple_of(jnp.bitwise_xor(me_m, mx) * part, part)
        d_here = dqkv_scr[pl.ds(at, part), :]
        d_n = nt(d_here, weights).astype(BF16)
        (send_ref if mx % 2 else keep_ref)[mx // 2] = d_n
        grad += tn(n_refs[mx][...], d_here)
    if not last:
        dw_ref[...] = grad
        return
    grad = grad.astype(BF16)
    for d in range(chunks):
        for b in range(3):
            dw_ref[jnp.bitwise_xor(d, me_d), b * CHUNK : (b + 1) * CHUNK, :] = grad[
                d * CHUNK : (d + 1) * CHUNK, b * LANE : (b + 1) * LANE
            ]


def attend_back(
    me, seg, segr, qkv, lse, d_parts, n_parts, wq, row, chunks, before=None, after=()
):
    mp_size = len(d_parts)
    length = seg.shape[1]
    part, model = n_parts[0].shape
    last = before is not None
    out = [sds((mp_size // 2, part, model), BF16)] * 2
    out += [sds((chunks, 3 * CHUNK, LANE), BF16) if last else sds((model, 384), F32)]
    return call(
        functools.partial(attend_back_body, wq, row, mp_size, chunks, last),
        "attend_back",
        out,
        [me, seg, segr, qkv, lse]
        + d_parts
        + [Late(n) for n in n_parts]
        + ([before] if last else []),
        smem=2,
        parts=wq.arrays,
        scratch=[
            pltpu.VMEM((chunks, wq.rows, LANE), BF16),
            pltpu.VMEM((length, LANE), BF16),
            pltpu.VMEM((length, 384), BF16),
            pltpu.VMEM((length, LANE), F32),
            pltpu.VMEM((length, LANE), F32),
            pltpu.VMEM((length, LANE), F32),
            pltpu.SemaphoreType.DMA,
        ],
        after=after,
    )


def first_back_body(
    layer, batch, me_ref, x_ref, gmid_ref, local_ref, par_ref, sums2_ref, sums1_ref, *refs
):
    kept, got = refs[:batch], refs[batch : 2 * batch]
    g_ref, sums_ref = refs[2 * batch :]
    part = kept[0].shape[0]
    for r in range(batch):
        at = rows_at(me_ref, r, part)
        g_ref[at, :] = local_ref[at, :] + kept[r][...].astype(F32) + got[r][...].astype(F32)
    need(x_ref)
    d_x, d_gain, d_bias = norm_back(x_ref[...].astype(F32), par_ref[layer, 0:1], g_ref[...])
    g_ref[...] = gmid_ref[...] + d_x
    sums_ref[0:1, :] = d_gain
    sums_ref[1:2, :] = sums2_ref[0:1, :]
    sums_ref[2:3, :] = d_bias
    sums_ref[3:4, :] = sums1_ref[0:1, :]
    sums_ref[4:5, :] = sums2_ref[1:2, :]
    sums_ref[5:6, :] = sums2_ref[2:3, :]
    sums_ref[6:8, :] = sums2_ref[6:8, :]


def first_back(me, x, gmid, local, par, sums2, sums1, kept, got, layer, after=()):
    rows, model = x.shape
    return call(
        functools.partial(first_back_body, layer, len(kept)),
        "first_back",
        [sds((rows, model), F32), sds((8, model), F32)],
        [me, Late(x), gmid, local, par, sums2, sums1] + kept + got,
        smem=1,
        after=after,
    )


def put_blocks(outs, mx, me_d, chunks, at_block, res, mp_first=False):
    half = chunks // 2
    for d in range(chunks):
        at = jnp.bitwise_xor(d, me_d)
        if mp_first:
            at = (mx // 2) * chunks + at
        else:
            at = (at // half) * chunks + (mx // 2) * half + at % half
        for b in range(res.shape[1] // LANE):
            rows = slice((at_block + b) * CHUNK, (at_block + b + 1) * CHUNK)
            outs[mx % 2][at, rows, :] = res[d * CHUNK : (d + 1) * CHUNK, b * LANE : (b + 1) * LANE]


def weight_grad_body(
    wd, mp_size, chunks, batch, mp_first, me_ref, n2_ref, dcomb_ref, b1_ref, b2_ref, att_ref,
    act_ref, s1_ref, *refs
):
    n_refs, refs = refs[:batch], refs[batch:]
    d_refs, refs = refs[: len(wd.arrays)], refs[len(wd.arrays) :]
    ups, downs, (local_ref, sums_ref), refs = refs[:2], refs[2:4], refs[4:6], refs[6:]
    w_scr, left, n_left, b1_left, z_scr, sem = refs
    w = wd.open(d_refs, me_ref, w_scr, sem, chunks)
    me_m, me_d = me_ref[0], me_ref[1]
    every = range(mp_size)
    need(n2_ref)
    left[...] = n2_ref[...].T
    stride = dcomb_ref.shape[1] // mp_size
    for mx in every:
        m = jnp.bitwise_xor(me_m, mx)
        res = nn(left[...], dcomb_ref[:, pl.ds(col(m * stride), stride)])
        put_blocks(ups, mx, me_d, chunks, 0, res.astype(BF16), mp_first)
    need(s1_ref, *n_refs)
    for r in range(batch):
        z_scr[rows_at(me_ref, r, n_refs[r].shape[0]), :] = n_refs[r][...]
    n = z_scr[...]
    n_left[...] = n.T
    b1f = b1_ref[...].astype(F32)
    s1 = s1_ref[...]
    d_z1 = (b1f * n.astype(F32) * s1 * (1.0 - s1)).astype(BF16)
    z_scr[...] = d_z1
    sums_ref[0:1, :] = jnp.sum(d_z1.astype(F32), axis=0, keepdims=True)
    sums_ref[1:8, :] = jnp.zeros((7, sums_ref.shape[1]), F32)
    b1_left[...] = b1_ref[...].T
    left[...] = b2_ref[...].T
    w.wait()
    local_ref[...] = b1f * s1 + nt(d_z1, w.wide([(m, 0) for m in every]))
    need(att_ref, act_ref)
    ff_m = act_ref.shape[1] // mp_size
    for mx in every:
        m = jnp.bitwise_xor(me_m, mx)
        cols = pl.ds(col(m * LANE), LANE)
        put_blocks(downs, mx, me_d, chunks, 0, nn(n_left[...], z_scr[:, cols]).astype(BF16))
        put_blocks(downs, mx, me_d, chunks, 1, nn(b1_left[...], att_ref[:, cols]).astype(BF16))
        res = nn(left[...], act_ref[:, pl.ds(col(m * ff_m), ff_m)])
        put_blocks(downs, mx, me_d, chunks, 2, res.astype(BF16))


def weight_grad(
    me, n2, dcomb, b1, b2, att, act, s1, n_rows, wd, mp_size, chunks, mp_first, after=()
):
    rows, model = b1.shape
    gates = Parts(wd.arrays, wd.order, wd.first_rows, CHUNK)
    height = dcomb.shape[1] // mp_size // LANE * CHUNK
    return call(
        functools.partial(weight_grad_body, gates, mp_size, chunks, len(n_rows), mp_first),
        "weight_grad",
        [sds((mp_size // 2 * chunks, height, LANE), BF16)] * 2
        + [sds((mp_size // 2 * chunks, wd.rows, LANE), BF16)] * 2
        + [sds((rows, model), F32), sds((8, model), F32)],
        [me, Late(n2), dcomb, b1, b2, Late(att), Late(act), Late(s1)]
        + [Late(n) for n in n_rows],
        smem=1,
        parts=wd.arrays,
        scratch=[pltpu.VMEM((chunks * mp_size, CHUNK, LANE), BF16)]
        + [pltpu.VMEM((model, rows), BF16)] * 3
        + [pltpu.VMEM((rows, model), BF16), pltpu.SemaphoreType.DMA],
        after=after,
    )


def swap(value, axis, size, bits):
    return lax.ppermute(value, axis, [(i, i ^ bits) for i in range(size)])


def add_body(count, *refs):
    left, right = refs[:2]
    outs = refs[2:]
    size = outs[0].shape[0]

    def step(i, carry):
        for part, out in enumerate(outs):
            at = part * size + i
            out[i] = (left[at].astype(F32) + right[at].astype(F32)).astype(BF16)
        return carry

    lax.fori_loop(0, size, step, 0)


def add(left, right, count):
    shape = (left.shape[0] // count,) + left.shape[1:]
    return call(
        functools.partial(add_body, count),
        "add",
        [sds(shape, BF16)] * count,
        [left, right],
    )


def join_body(count, has_sums, me_ref, *refs):
    pairs = [(refs[2 * i], refs[2 * i + 1]) for i in range(count)]
    refs = refs[2 * count :]
    if has_sums:
        sums_ref, refs = refs[0], refs[1:]
    for k, out in enumerate(refs):
        at = 0
        for left, right in pairs:
            rows = left.shape[1]
            out[at : at + rows, :] = (left[k].astype(F32) + right[k].astype(F32)).astype(BF16)
            at += rows
        if has_sums:
            tile = jnp.bitwise_xor(me_ref[1], k) // (LANE // CHUNK)
            out[at:, :] = sums_ref[:, pl.ds(col(tile * LANE), LANE)].astype(BF16)


def join(me, pairs, sums=None):
    width = 4
    rows = sum(p[0].shape[1] for p in pairs) + (0 if sums is None else sums.shape[0])
    flat = [a for pair in pairs for a in pair]
    return call(
        functools.partial(join_body, len(pairs), sums is not None),
        "add",
        [sds((rows, LANE), BF16)] * width,
        [me] + flat + ([] if sums is None else [sums]),
        smem=1,
    )


def total_body(*refs):
    value = refs[0][...].astype(F32)
    for ref in refs[1:-1]:
        value += ref[...].astype(F32)
    refs[-1][...] = value


def total(parts):
    return call(total_body, "add", [sds(parts[0].shape, F32)], parts)[0]


def stack_body(cuts, *refs):
    ins, outs = refs[: -len(cuts)], refs[-len(cuts) :]
    for i, ref in enumerate(ins):
        at = 0
        for out, rows in zip(outs, cuts):
            out[i] = ref[at : at + rows, :]
            at += rows


def stack(arrays, cuts=None, after=()):
    cuts = cuts or [arrays[0].shape[0]]
    return call(
        functools.partial(stack_body, cuts),
        "stack",
        [sds((len(arrays), rows, LANE), BF16) for rows in cuts],
        arrays,
        after=after,
    )


def copy_body(rows, *refs):
    half = len(refs) // 2
    for (first, count), a_ref, b_ref in zip(rows, refs[:half], refs[half:]):
        b_ref[...] = a_ref[:, first : first + count, :]


def copied(*pieces):
    return call(
        functools.partial(copy_body, [p[1:] for p in pieces]),
        "stack",
        [sds((a.shape[0], count, a.shape[2]), a.dtype) for a, _, count in pieces],
        [p[0] for p in pieces],
    )


def relay_body(*refs):
    pass


def relay(arrays, name="relay"):
    call(relay_body, name, [], [], after=arrays)


def pack_q_body(per, me_ref, qkv_ref, par_ref, out_ref):
    for c in range(3):
        out_ref[c * per : (c + 1) * per, :] = qkv_ref[c]
    rows = jnp.concatenate([par_ref[...].astype(F32)] * (LANE // per), axis=1)
    share = lax.broadcasted_iota(jnp.int32, rows.shape, 1) // per
    mine = jnp.where(share == me_ref[1] % (LANE // per), rows, 0.0)
    out_ref[3 * per :, :] = mine.astype(BF16)


def pack_q(me, qkv, params):
    per = qkv.shape[1]
    return call(
        functools.partial(pack_q_body, per),
        "pack",
        [sds((3 * per + params.shape[0], LANE), BF16)],
        [me, qkv, params],
        smem=1,
    )[0]


def pack_body(layer, with_q, qkv_ref, gate_ref, out_ref, up_ref, down_ref, shard_ref):
    per = gate_ref.shape[2]
    at = 0
    if with_q:
        for c in range(3):
            shard_ref[at : at + per, :] = qkv_ref[layer, c]
            at += per
    refs = (gate_ref.at[layer, 0], out_ref.at[layer], down_ref.at[layer])
    for ref in refs + (gate_ref.at[layer, 1], up_ref.at[layer]):
        for b in range(ref.shape[1] // LANE):
            shard_ref[at : at + per, :] = ref[:, b * LANE : (b + 1) * LANE]
            at += per


def pack(layer, with_q, w_qkv, w_gate, w_out, w_up, w_down):
    per = w_gate.shape[2]
    cols = 2 * w_gate.shape[3] + w_out.shape[2] + w_up.shape[2] + w_down.shape[2]
    rows = (cols // LANE + 3 * with_q) * per
    return call(
        functools.partial(pack_body, layer, with_q),
        "pack",
        [sds((rows, LANE), BF16)],
        [w_qkv, w_gate, w_out, w_up, w_down],
    )[0]


def finish_body(counts, names, me_ref, *refs):
    ins, outs = refs[: sum(counts)], refs[sum(counts) :]
    d_qkv, d_out, d_gate, d_up, d_down, d_gains, d_norm_biases, d_gate_biases = outs
    per = CHUNK
    at = 0
    for count, pieces in zip(counts, names):
        value = ins[at][...].astype(F32)
        for ref in ins[at + 1 : at + count]:
            value += ref[...].astype(F32)
        at += count
        row = 0
        for name, l in pieces:
            if name == "p":
                low, high = value[row:, :CHUNK], value[row:, CHUNK:]
                value = jnp.where(me_ref[1] % 2 == 0, low, high)
                for i in range(value.shape[0] // 8):
                    for out, first in ((d_gains, 0), (d_norm_biases, 2), (d_gate_biases, 3)):
                        step = 1 if out is d_gains else 2
                        for j in range(2):
                            at_row = 8 * i + first + j * step
                            out[i, j : j + 1, :] = value[at_row : at_row + 1]
                continue
            blocks = {"q": 3, "u": 1 + d_up.shape[2] // LANE, "d": 2 + d_down.shape[2] // LANE}
            for b in range(blocks[name]):
                block = value[row : row + per]
                row += per
                if name == "q":
                    d_qkv[l, b] = block
                elif name == "u" and b == 0:
                    d_gate[l, 1] = block
                elif name == "u":
                    d_up[l, :, (b - 1) * LANE : b * LANE] = block
                elif b == 0:
                    d_gate[l, 0] = block
                elif b == 1:
                    d_out[l] = block
                else:
                    d_down[l, :, (b - 2) * LANE : (b - 1) * LANE] = block


def finish(me, layers, ff_m, groups):
    shapes = [(3, CHUNK, LANE), (CHUNK, LANE), (2, CHUNK, LANE), (CHUNK, ff_m), (CHUNK, ff_m)]
    out = [sds((layers,) + shape, F32) for shape in shapes] + [sds((layers, 2, CHUNK), F32)] * 3
    return call(
        functools.partial(finish_body, [len(g[0]) for g in groups], [g[1] for g in groups]),
        "finish",
        out,
        [me] + [a for g in groups for a in g[0]],
        smem=1,
    )


def solution(mesh):
    dp_size, mp_size, width_size = (mesh.shape[a] for a in ("dp", "mp", "width"))
    all_axes = ("mp", "dp", "width")
    direct = (dp_size, mp_size, width_size) == (2, 4, 4)

    def mp_swap(value, bits):
        return swap(value, "mp", mp_size, bits)

    def dp_swap(value):
        return swap(value, "dp", dp_size, 1)

    def spread(value):
        return [value, mp_swap(value, 1), mp_swap(value, 2)]

    def spread_last(values):
        return values + [mp_swap(values[2], 1)]

    def exchange(own, near, far):
        far = mp_swap(far, 2)
        return [own, mp_swap(near, 1), far, mp_swap(far, 1)]

    def send_width(value):
        return [value] + [swap(value, "width", width_size, k) for k in range(1, width_size)]

    def swap_width(values):
        return [values[0]] + [
            swap(values[k], "width", width_size, k) for k in range(1, width_size)
        ]

    def on_device(
        tokens, segments, cotangent, norm_gains, biases, w_qkv, w_out, w_gate, w_up, w_down
    ):
        ORDER.token = None
        batch, part, model = tokens.shape
        layers = w_qkv.shape[0]
        per = w_qkv.shape[1]
        chunks = model // CHUNK
        half = chunks // 2
        ff_m = w_up.shape[2]
        ff_blocks = ff_m // LANE
        ff = ff_m * mp_size
        me_m = lax.axis_index("mp")
        me_d = lax.axis_index("dp") * width_size + lax.axis_index("width")
        rows = [jnp.where(segments[0, -1] < 0, 0, batch - 1)]
        rows += [batch - 1 - rows[0]] if batch == 2 else []
        me = jnp.stack([me_m, me_d] + rows).astype(jnp.int32)
        me_pack, me_att = me, me
        if not direct:
            me_pack = jnp.stack([0 * me_m, 0 * me_d] + rows).astype(jnp.int32)
            me_att = jnp.stack([me_m, 0 * me_d] + rows).astype(jnp.int32)

        def blocks_of(matrix):
            return jnp.swapaxes(matrix.reshape(per, -1, LANE), 0, 1).reshape(-1, LANE)

        qkv_t, out_t, down_t = (jnp.swapaxes(w, 1, 2) for w in (w_qkv, w_out, w_down))
        params = jnp.concatenate([norm_gains, biases], axis=1)
        params = jnp.pad(params, ((0, 0), (0, 2), (0, 0))).reshape(layers * 8, per)

        def param_block():
            rows = jnp.concatenate([params] * (LANE // per), axis=1)
            share = lax.broadcasted_iota(jnp.int32, rows.shape, 1) // per
            return jnp.where(share == me_d % (LANE // per), rows, 0)

        q_rows, d_rows, u_rows = 3 * CHUNK, (2 + ff_blocks) * CHUNK, (1 + ff_blocks) * CHUNK

        def shard(l, q):
            mats = [w_gate[l, 0], out_t[l], blocks_of(down_t[l]), w_gate[l, 1], blocks_of(w_up[l])]
            return jnp.concatenate(([qkv_t[l].reshape(-1, LANE)] if q else []) + mats, axis=0)

        def gather_whole(shard, extra):
            full = lax.all_gather(shard, all_axes, axis=0, tiled=False)
            if per == CHUNK:
                return full
            count = (shard.shape[0] - extra) // per
            full = full.reshape(mp_size, chunks, CHUNK // per, shard.shape[0], LANE)
            mats = full[:, :, :, : count * per]
            mats = mats.reshape(mp_size, chunks, CHUNK // per, count, per, LANE)
            mats = jnp.swapaxes(mats, 2, 3).reshape(mp_size * chunks, count * CHUNK, LANE)
            if not extra:
                return mats
            pars = jnp.sum(full[:, :, :, count * per :].astype(F32), axis=2).astype(BF16)
            return jnp.concatenate([mats, pars.reshape(mp_size * chunks, extra, LANE)], axis=1)

        def reduce_whole(even, odd):
            full = jnp.stack([even, odd], axis=1)
            full = full.reshape(2, mp_size // 2, half, 2, -1, CHUNK // per, per, LANE)
            full = jnp.transpose(full, (1, 3, 0, 2, 5, 4, 6, 7)).reshape(-1, LANE).astype(F32)
            return lax.psum_scatter(full, all_axes, scatter_dimension=0, tiled=True)

        def reduce_q_whole(grad):
            full = grad.reshape(chunks, -1, CHUNK // per, per, LANE)
            full = jnp.swapaxes(full, 1, 2).reshape(-1, LANE).astype(F32)
            return lax.psum_scatter(full, ("dp", "width"), scatter_dimension=0, tiled=True)

        seg = jnp.where(rows[0] == 0, segments, segments[::-1]) if batch == 2 else segments
        segs = (seg, seg[:, None, :].astype(F32))

        q_all = q_rows + layers * 8
        weights = [None] * layers
        if direct:
            mats = (qkv_t, w_gate, out_t, w_up, down_t)
            q_steps = send_width(pack_q(me, qkv_t[0], params))
            t_all = spread(tokens)
            w_steps = send_width(pack(0, False, *mats))
            relay([], "pack")
            (q_base,) = stack(q_steps)
            t_far = copied((t_all[2], 0, part))[0]
            wq = Parts([q_base, dp_swap(q_base)], [(0, 0), (0, 4)], 0, q_all)
            (base,) = stack(w_steps)
            got = {(0, 0): base, (0, 4): dp_swap(base), (2, 0): mp_swap(base, 2)}
            later = send_width(pack(1, True, *mats))
            relay([wq.arrays[1]])
            t_all = t_all + [mp_swap(t_far, 1)]
        else:
            t_all = spread_last(spread(tokens))
            q_sh = jnp.concatenate([qkv_t[0].reshape(-1, LANE), param_block()], axis=0)
            wq = Parts([gather_whole(q_sh, layers * 8)], None, 0, q_all)
            full = gather_whole(shard(0, False), 0)
            wd, wu = Parts([full], None, 0, d_rows), Parts([full], None, d_rows, u_rows)
            for l in range(1, layers):
                full = gather_whole(shard(l, True), 0)
                weights[l] = (
                    Parts([full], None, 0, q_rows),
                    Parts([full], None, q_rows, d_rows),
                    Parts([full], None, q_rows + d_rows, u_rows),
                )

        def last_step(got):
            d_last, u_last = copied((got[2, 0], 0, d_rows), (got[0, 4], d_rows, u_rows))
            return dp_swap(d_last), mp_swap(u_last, 2)

        def two_pieces(got, lasts):
            for m, d in list(got):
                got[m + 1, d] = mp_swap(got[m, d], 1)
            arrays, order = list(got.values()), list(got) + [(2, 4), (3, 4)]
            lasts = copied(*[(a, 0, a.shape[1]) for a in lasts])
            d_all, u_all = (arrays + [a, mp_swap(a, 1)] for a in lasts)
            return (
                Parts(d_all, order, 0, d_rows),
                Parts(u_all, order, [d_rows] * len(arrays) + [0, 0], u_rows),
            )

        x = tokens.reshape(batch * part, model)
        par = None
        saved = []
        t_parts = t_all
        for l in range(layers):
            if l and direct:
                wq = wq_next
            elif l:
                wq, wd, wu = weights[l]
            qkv, lse, own, near, far, *rest = attend(
                me, segs, t_parts, wq, l, layers, l == 0, chunks
            )
            kept = (qkv, lse)
            if l == 0:
                par = rest[0]
                n_parts = [rest[1 + r * mp_size : 1 + (r + 1) * mp_size] for r in range(batch)]
            else:
                n_parts = [t_parts[r::batch] for r in range(batch)]
            o_parts = exchange(own, near, far)
            if direct:
                if l == 0:
                    relay([got[0, 4], got[2, 0]] + later[1:])
                    lasts = last_step(got)
                    relay([o_parts[2]])
                wd, wu = two_pieces(got, lasts)
                if l == 0:
                    q_base, base = stack(later, [q_rows, d_rows + u_rows])
                    wq_next = Parts([q_base, dp_swap(q_base)], [(0, 0), (0, 4)], 0, q_rows)
                    got = {(0, 0): base, (0, 4): dp_swap(base), (2, 0): mp_swap(base, 2)}
                else:
                    wq = wq_next
                weights[l] = (wq, wd, wu)
            elif l == 0:
                weights[0] = (wq, wd, wu)
            n_rows = [n_parts[r][0] for r in range(batch)]
            att, s1, mid, n2, s2, act, slope, out, *following = second(
                me, x, par, n_rows, o_parts, wd, wu, l, chunks, ff, l + 1 < layers
            )
            saved.append((x, n_parts, kept, att, s1, mid, n2, s2, act, slope))
            x = out
            if following:
                t_rows = [spread(n) for n in following]
                if direct:
                    relay([got[0, 4], got[2, 0], wq_next.arrays[1]] + [t[2] for t in t_rows])
                    lasts = last_step(got)
                t_rows = [spread_last(t) for t in t_rows]
                t_parts = [t_rows[r][mx] for mx in range(mp_size) for r in range(batch)]
        output = x.reshape(batch, part, model)

        own = lax.dynamic_slice_in_dim(segments, me_m * part, part, 1)
        g = cotangent.astype(F32) * (own >= 0).astype(F32)[:, :, None]
        g = g.reshape(batch * part, model)
        reduced = [None] * layers
        all_sums = [None] * layers
        moving = {}

        def reduce_2(name, mp_first=False):
            if name in moving:
                keep, send = add(*moving[name], 2)
                moving[name] = (keep, mp_swap(send, 2) if mp_first else dp_swap(send))

        def reduce_3(name, mp_first=False):
            if name in moving:
                keep, send = add(*moving[name], 2)
                moving[name] = (keep, dp_swap(send) if mp_first else mp_swap(send, 2))

        def reduce_4(names, sums=None):
            if direct:
                pairs = [moving.pop(name) for name in names]
                moving[names[0]] = swap_width(join(me, pairs, sums))

        def reduce_5(name):
            return total(moving.pop(name)) if direct else None

        for l in reversed(range(layers)):
            wq, wd, wu = weights[l]
            x, n_parts, kept, att, s1, mid, n2, s2, act, slope = saved[l]
            n_rows = [n_parts[r][0] for r in range(batch)]
            final, first_of_two = l == 0, l + 1 < layers
            b2, dcomb, gmid, b1, sums2, *o_parts = second_back(
                me, g, mid, n2, s2, slope, par, wd, wu, l, mp_size, chunks, batch
            )
            d_parts = exchange(*o_parts)
            if first_of_two:
                reduce_4([("q", l + 1), ("u", l + 1)])
            reduce_3(("d", l + 1))
            *grads, local, sums1 = weight_grad(
                me_pack, n2, dcomb, b1, b2, att, act, s1, n_rows, wd, mp_size, chunks,
                final and direct,
            )
            relay([d_parts[2]])
            if direct:
                moving["u", l] = (grads[0], mp_swap(grads[1], 1))
                moving["d", l] = (grads[2], mp_swap(grads[3], 1))
            keeps, gots = [], []
            q_grad = None
            for r in range(batch):
                keep, send, q_grad = attend_back(
                    me_att, *segs, *kept, d_parts, n_parts[r], wq, r, chunks, q_grad
                )
                if r == 0:
                    if first_of_two:
                        reduce_4([("d", l + 1)])
                    reduce_2(("d", l))
                    reduce_2(("u", l), final)
                    if first_of_two:
                        moving["q", l + 1] = [reduce_5(("q", l + 1))] if direct else None
                else:
                    reduce_3(("u", l), final)
                    if final:
                        reduce_3(("d", l))
                keep, send = add(keep, mp_swap(send, 1), 2)
                keeps.append(keep.reshape(keep.shape[1:]))
                gots.append(mp_swap(send, 2).reshape(keep.shape[1:]))
            if direct and first_of_two:
                moving["d", l + 1] = [reduce_5(("d", l + 1))]
            if direct:
                moving["q", l] = (q_grad[:half], dp_swap(q_grad[half:]))
                if final:
                    reduce_4([("u", l)])
            g, all_sums[l] = first_back(me, x, gmid, local, par, sums2, sums1, keeps, gots, l)
            if direct and final:
                reduce_4([("q", l), ("d", l)])
                moving["u", l] = [reduce_5(("u", l))]
            if not direct:
                reduced[l] = (reduce_q_whole(q_grad), reduce_whole(*grads[:2]), reduce_whole(*grads[2:]))
        d_tokens = g.reshape(batch, part, model)
        sums = jnp.concatenate(all_sums, axis=0)
        if direct:
            sums = sums + mp_swap(sums, 1)
            sums = sums + mp_swap(sums, 2)
            sums = sums + dp_swap(sums)
            moving["p", 0] = swap_width(join(me, [], sums))
            groups = [
                (moving["q", 1], [("q", 1), ("u", 1)]),
                (moving["d", 1], [("d", 1)]),
                (moving["u", 0], [("u", 0)]),
                (moving["q", 0], [("q", 0), ("d", 0)]),
                (moving["p", 0], [("p", 0)]),
            ]
            stacked = finish(me, layers, ff_m, groups)
            stacked, small = stacked[:5], stacked[5:]
        else:
            params = lax.dynamic_slice_in_dim(lax.psum(sums, all_axes), me_d * per, per, 1)
            params = params.reshape(layers, 8, per)
            small = [params[:, 0:2], params[:, 2:6:2], params[:, 3:6:2]]

        def unblocks(rows, count):
            return jnp.swapaxes(rows.reshape(count, per, LANE), 0, 1).reshape(per, count * LANE)

        if not direct:
            grads = []
            for q_sum, up_sum, down_sum in reduced:
                grads.append(
                    (
                        q_sum.reshape(3, per, LANE),
                        down_sum[per : 2 * per],
                        jnp.stack([down_sum[:per], up_sum[:per]]),
                        unblocks(up_sum[per:], ff_blocks),
                        unblocks(down_sum[2 * per :], ff_blocks),
                    )
                )
            stacked = [jnp.stack([grads[l][i] for l in range(layers)]) for i in range(5)]
        for i in (0, 1, 4):
            stacked[i] = jnp.swapaxes(stacked[i], 1, 2)
        return (
            output,
            d_tokens,
            *small,
            *stacked,
        )

    placed = (
        P(("dp", "width"), "mp", None),
        P(("dp", "width"), None),
        P(("dp", "width"), "mp", None),
        P(None, None, ("dp", "width")),
        P(None, None, ("dp", "width")),
        P(None, ("dp", "width"), None, "mp"),
        P(None, "mp", ("dp", "width")),
        P(None, None, ("dp", "width"), "mp"),
        P(None, ("dp", "width"), "mp"),
        P(None, "mp", ("dp", "width")),
    )
    return jax.shard_map(
        on_device,
        mesh=mesh,
        in_specs=placed,
        out_specs=(
            placed[0],
            placed[0],
            placed[3],
            placed[3],
            placed[3],
            placed[5],
            placed[6],
            placed[7],
            placed[8],
            placed[9],
        ),
        check_vma=False,
    )
```

profile of v0, /device:TPU:0, one launch (start us, length us, event | category | flops | bytes accessed | tf_op | source)
XLA Modules:
  0.0 308.2 jit_solution(17718932600485488676)
XLA Ops:
  0.6 1.3 slice.18
  4.8 5.1 %collective-permute-start.4 = (bf16[208,128]{1,0:T(8,128)(2,1)S(1)}, bf16[208,128]{1,0:T(8,128)(2,1)S(1)}, u32[]{:S(2)}, u32[]{:S(2)}) collective-permute-start(bf16[208,128]{1,0:T(8,128)(2,1)S(1)} %get-tuple-element.207.refs_0_), channel_id=1, source_target_pairs={{0,3},{1,2},{2,1},{3,0},{4,7},{5,6},{6,5},{7,4},{8,11},{9,10},{10,... | collective-permute-start | bytes 159752 | tf_op jit(solution)/shard_map/ppermute | solution.py:853
  10.6 3.8 %collective-permute-start.9 = (bf16[704,128]{1,0:T(8,128)(2,1)S(1)}, bf16[704,128]{1,0:T(8,128)(2,1)S(1)}, u32[]{:S(2)}, u32[]{:S(2)}) collective-permute-start(bf16[704,128]{1,0:T(8,128)(2,1)S(1)} %get-tuple-element.213.refs_0_), channel_id=1, source_target_pairs={{0,3},{1,2},{2,1},{3,0},{4,7},{5,6},{6,5},{7,4},{8,11},{9,10},{10,... | collective-permute-start | bytes 540680 | tf_op jit(solution)/shard_map/ppermute | solution.py:853
  14.4 1.5 collective-permute-start.1
  16.9 5.1 %collective-permute-done.3.refs_2_ = bf16[208,128]{1,0:T(8,128)(2,1)S(1)} collective-permute-done((bf16[208,128]{1,0:T(8,128)(2,1)S(1)}, bf16[208,128]{1,0:T(8,128)(2,1)S(1)}, u32[]{:S(2)}, u32[]{:S(2)}) %collective-permute-start.3) | collective-permute-done | bytes 53280 | tf_op jit(solution)/shard_map/ppermute | solution.py:853
  22.2 4.7 %collective-permute-done.1.refs_0_.refs_5_ = bf16[2,256,512]{2,1,0:T(8,128)(2,1)S(1)} collective-permute-done((bf16[2,256,512]{2,1,0:T(8,128)(2,1)S(1)}, bf16[2,256,512]{2,1,0:T(8,128)(2,1)S(1)}, u32[]{:S(2)}, u32[]{:S(2)}) %collective-permute-start.1) | collective-permute-done | bytes 524320 | tf_op jit(solution)/shard_map/ppermute | solution.py:853
  27.0 1.5 collective-permute-start.6
  28.6 1.6 collective-permute-done.8.refs_2_
  31.4 1.5 collective-permute-start.20
  32.9 2.9 collective-permute-start.18
  35.9 1.4 collective-permute-start.14
  37.3 1.5 collective-permute-start.13
  38.8 14.2 %attend.2 = (bf16[2,1024,384]{2,1,0:T(8,128)(2,1)}, f32[4,1,1024]{2,1,0:T(1,128)}, bf16[2,256,128]{2,1,0:T(8,128)(2,1)S(1)}, bf16[2,256,128]{2,1,0:T(8,128)(2,1)...) custom-call(s32[4]{0:T(128)S(1)} %copy-done.8, ...), custom_call_target="tpu_custom_call" | custom-call | flops 44000002048 | bytes 144000000 | tf_op jit(solution)/shard_map/attend/pallas_call | solution.py:171
  53.9 1.4 collective-permute-start.11
  56.6 8.7 %collective-permute-done.11.refs_0_.refs_7_ = bf16[2,2,256,128]{3,2,1,0:T(8,128)(2,1)S(1)} collective-permute-done((bf16[2,2,256,128]{3,2,1,0:T(8,128)(2,1)S(1)}, bf16[2,2,256,128]{3,2,1,0:T(8,128)(2,1)S(1)}, u32[]{:S(2)}, u32[]{:S(2)}) %collective-permute-start.11) | collective-permute-done | bytes 262176 | tf_op jit(solution)/shard_map/ppermute | solution.py:853
  67.6 2.3 collective-permute-done.12.refs_8_
  70.5 1.7 collective-permute-start.32
  73.3 10.7 %second.2 = (bf16[512,512]{1,0:T(8,128)(2,1)}, f32[512,512]{1,0:T(8,128)}, f32[512,512]{1,0:T(8,128)}, bf16[512,512]{1,0:T(8,128)(2,1)}, f32[512,512]{1,0:T(8,12...) custom-call(s32[4]{0:T(128)S(1)} %copy-done.8, ...), custom_call_target="tpu_custom_call" | custom-call | flops 65999998976 | bytes 216000000 | tf_op jit(solution)/shard_map/second/pallas_call | solution.py:171
  84.4 1.7 collective-permute-start.28
  86.6 5.7 %collective-permute-done.31.refs_2_.refs_12_.refs_14_.refs_15_ = bf16[4,192,128]{2,1,0:T(8,128)(2,1)S(1)} collective-permute-done((bf16[4,192,128]{2,1,0:T(8,128)(2,1)S(1)}, bf16[4,192,128]{2,1,0:T(8,128)(2,1)S(1)}, u32[]{:S(2)}, u32[]{:S(2)}) %collective-permute-start.31) | collective-permute-done | bytes 196640 | tf_op jit(solution)/shard_map/ppermute | solution.py:853
  92.3 2.8 collective-permute-done.27.refs_3_.refs_7_.refs_11_
  95.1 4.5 %collective-permute-done.28.refs_4_.refs_8_.refs_11_ = bf16[256,512]{1,0:T(8,128)(2,1)S(1)} collective-permute-done((bf16[256,512]{1,0:T(8,128)(2,1)S(1)}, bf16[256,512]{1,0:T(8,128)(2,1)S(1)}, u32[]{:S(2)}, u32[]{:S(2)}) %collective-permute-start.28) | collective-permute-done | bytes 262176 | tf_op jit(solution)/shard_map/ppermute | solution.py:853
  100.3 1.7 collective-permute-start.41
  103.3 13.4 %attend.3 = (bf16[2,1024,384]{2,1,0:T(8,128)(2,1)S(1)}, f32[4,1,1024]{2,1,0:T(1,128)S(1)}, bf16[2,256,128]{2,1,0:T(8,128)(2,1)S(1)}, bf16[2,256,128]{2,1,0:T(8,1...) custom-call(s32[4]{0:T(128)S(1)} %copy-done.8, s32[2,1024]{1,0:T(2,128)S(1)} %get-tuple-element.405.refs_1_, ...), custom_call_target="tpu_custom_call" | custom-call | flops 44000002048 | bytes 144000000 | tf_op jit(solution)/shard_map/attend/pallas_call | solution.py:171
  116.8 1.3 collective-permute-start.35
  120.4 4.9 %collective-permute-done.35.refs_7_ = bf16[2,2,256,128]{3,2,1,0:T(8,128)(2,1)S(1)} collective-permute-done((bf16[2,2,256,128]{3,2,1,0:T(8,128)(2,1)}, bf16[2,2,256,128]{3,2,1,0:T(8,128)(2,1)S(1)}, u32[]{:S(2)}, u32[]{:S(2)}) %collective-permute-start.35) | collective-permute-done | bytes 262176 | tf_op jit(solution)/shard_map/ppermute | solution.py:853
  125.4 1.4 collective-permute-done.36.refs_8_
  127.6 10.8 %second.3 = (bf16[512,512]{1,0:T(8,128)(2,1)}, f32[512,512]{1,0:T(8,128)}, f32[512,512]{1,0:T(8,128)}, bf16[512,512]{1,0:T(8,128)(2,1)}, f32[512,512]{1,0:T(8,12...) custom-call(s32[4]{0:T(128)S(1)} %copy-done.8, ...), custom_call_target="tpu_custom_call" | custom-call | flops 65999998976 | bytes 216000000 | tf_op jit(solution)/shard_map/second/pallas_call | solution.py:171
  138.4 8.9 %second_back.2 = (bf16[512,512]{1,0:T(8,128)(2,1)S(1)}, bf16[512,2560]{1,0:T(8,128)(2,1)S(1)}, f32[512,512]{1,0:T(8,128)S(1)}, bf16[512,512]{1,0:T(8,128)(2,1)S(...) custom-call(s32[4]{0:T(128)S(1)} %copy-done.8, ...), custom_call_target="tpu_custom_call" | custom-call | flops 54999998464 | bytes 180000000 | tf_op jit(solution)/shard_map/second_back/pallas_call | solution.py:171
  147.5 1.3 collective-permute-start.45
  148.8 7.3 %weight_grad.2 = (bf16[16,320,128]{2,1,0:T(8,128)(2,1)S(1)}, bf16[16,320,128]{2,1,0:T(8,128)(2,1)S(1)}, bf16[16,384,128]{2,1,0:T(8,128)(2,1)S(1)}, bf16[16,384,1...) custom-call(s32[4]{0:T(128)S(1)} %copy-done.8, ...), custom_call_target="tpu_custom_call" | custom-call | flops 44000002048 | bytes 144000000 | tf_op jit(solution)/shard_map/weight_grad/pallas_call | solution.py:171
  156.8 5.0 %collective-permute-done.46.refs_8_ = bf16[2,2,256,128]{3,2,1,0:T(8,128)(2,1)S(1)} collective-permute-done((bf16[2,2,256,128]{3,2,1,0:T(8,128)(2,1)S(1)}, bf16[2,2,256,128]{3,2,1,0:T(8,128)(2,1)S(1)}, u32[]{:S(2)}, u32[]{:S(2)}) %collective-permute-start.46) | collective-permute-done | bytes 262176 | tf_op jit(solution)/shard_map/ppermute | solution.py:853
  161.9 5.1 %attend_back.4 = (bf16[2,256,512]{2,1,0:T(8,128)(2,1)S(1)}, bf16[2,256,512]{2,1,0:T(8,128)(2,1)S(1)}, f32[512,384]{1,0:T(8,128)S(1)}, f32[8,128]{1,0:T(8,128)S(1)}) custom-call(s32[4]{0:T(128)S(1)} %copy-done.8, s32[2,1024]{1,0:T(2,128)S(1)} %copy-done.5, f32[2,1,1024]{2,1,0:T(1,128)S(1)} %copy-done.2, bf16[2,1024,384]{2,1,0:T(8,128)(2,1)S(1)} %copy-done.38, ...), custom_call_target="tpu_custom_call" | custom-call | flops 49500000256 | bytes 162000000 | tf_op jit(solution)/shard_map/attend_back/pallas_call | solution.py:171
  169.1 9.6 %attend_back.5 = (bf16[2,256,512]{2,1,0:T(8,128)(2,1)S(1)}, bf16[2,256,512]{2,1,0:T(8,128)(2,1)S(1)}, bf16[8,192,128]{2,1,0:T(8,128)(2,1)S(1)}, f32[8,128]{1,0:T(8,128)S(1)}) custom-call(s32[4]{0:T(128)S(1)} %copy-done.8, s32[2,1024]{1,0:T(2,128)S(1)} %copy-done.5, f32[2,1,1024]{2,1,0:T(1,128)S(1)} %copy-done.2, bf16[2,1024,384]{2,1,0:T(8,128)(2,1)S(1)} %copy-done.38, ...), custom_call_target="tpu_custom_call" | custom-call | flops 49500000256 | bytes 162000000 | tf_op jit(solution)/shard_map/attend_back/pallas_call | solution.py:171
  178.9 1.3 collective-permute-start.52
  180.2 4.9 %collective-permute-done.51.refs_1_ = bf16[8,320,128]{2,1,0:T(8,128)(2,1)S(1)} collective-permute-done((bf16[8,320,128]{2,1,0:T(8,128)(2,1)S(1)}, bf16[8,320,128]{2,1,0:T(8,128)(2,1)S(1)}, u32[]{:S(2)}, u32[]{:S(2)}) %collective-permute-start.51) | collective-permute-done | bytes 655392 | tf_op jit(solution)/shard_map/ppermute | solution.py:853
  186.5 1.5 collective-permute-start.55
  189.8 5.1 %collective-permute-done.53 = bf16[1,256,512]{2,1,0:T(8,128)(2,1)S(1)} collective-permute-done((bf16[1,256,512]{2,1,0:T(8,128)(2,1)S(1)}, bf16[1,256,512]{2,1,0:T(8,128)(2,1)S(1)}, u32[]{:S(2)}, u32[]{:S(2)}) %collective-permute-start.53) | collective-permute-done | bytes 262176 | tf_op jit(solution)/shard_map/ppermute | solution.py:853
  194.9 2.5 first_back.2
  197.4 8.9 %second_back.3 = (bf16[512,512]{1,0:T(8,128)(2,1)S(1)}, bf16[512,2560]{1,0:T(8,128)(2,1)S(1)}, f32[512,512]{1,0:T(8,128)S(1)}, bf16[512,512]{1,0:T(8,128)(2,1)S(...) custom-call(s32[4]{0:T(128)S(1)} %copy-done.8, ...), custom_call_target="tpu_custom_call" | custom-call | flops 54999998464 | bytes 180000000 | tf_op jit(solution)/shard_map/second_back/pallas_call | solution.py:171
  208.9 2.6 collective-permute-start.62
  211.7 1.3 collective-permute-start.66
  212.9 7.1 %weight_grad.3 = (bf16[16,320,128]{2,1,0:T(8,128)(2,1)S(1)}, bf16[16,320,128]{2,1,0:T(8,128)(2,1)S(1)}, bf16[16,384,128]{2,1,0:T(8,128)(2,1)S(1)}, bf16[16,384,1...) custom-call(s32[4]{0:T(128)S(1)} %copy-done.8, ...), custom_call_target="tpu_custom_call" | custom-call | flops 44000002048 | bytes 144000000 | tf_op jit(solution)/shard_map/weight_grad/pallas_call | solution.py:171
  221.8 5.6 %attend_back.6 = (bf16[2,256,512]{2,1,0:T(8,128)(2,1)S(1)}, bf16[2,256,512]{2,1,0:T(8,128)(2,1)S(1)}, f32[512,384]{1,0:T(8,128)S(1)}, f32[8,128]{1,0:T(8,128)S(1)}) custom-call(s32[4]{0:T(128)S(1)} %copy-done.8, s32[2,1024]{1,0:T(2,128)S(1)} %copy-done.6, f32[2,1,1024]{2,1,0:T(1,128)S(1)} %copy-done.3, bf16[2,1024,384]{2,1,0:T(8,128)(2,1)S(1)} %copy-done.36, ...), custom_call_target="tpu_custom_call" | custom-call | flops 49500000256 | bytes 162000000 | tf_op jit(solution)/shard_map/attend_back/pallas_call | solution.py:171
  230.3 3.2 %collective-permute-start.74 = (bf16[384,128]{1,0:T(8,128)(2,1)S(1)}, bf16[384,128]{1,0:T(8,128)(2,1)S(1)}, u32[]{:S(2)}, u32[]{:S(2)}) collective-permute-start(bf16[384,128]{1,0:T(8,128)(2,1)S(1)} %get-tuple-element.366), channel_id=1, source_target_pairs={{0,2},{1,3},{2,0},{3,1},{4,6},{5,7},{6,4},{7,5},{8,10},{9,11},{10,... | collective-permute-start | bytes 294920 | tf_op jit(solution)/shard_map/ppermute | solution.py:853
  236.6 1.5 collective-permute-start.68
  238.2 9.6 %attend_back.7 = (bf16[2,256,512]{2,1,0:T(8,128)(2,1)S(1)}, bf16[2,256,512]{2,1,0:T(8,128)(2,1)S(1)}, bf16[8,192,128]{2,1,0:T(8,128)(2,1)S(1)}, f32[8,128]{1,0:T(8,128)S(1)}) custom-call(s32[4]{0:T(128)S(1)} %copy-done.8, s32[2,1024]{1,0:T(2,128)S(1)} %copy-done.6, f32[2,1,1024]{2,1,0:T(1,128)S(1)} %copy-done.3, bf16[2,1024,384]{2,1,0:T(8,128)(2,1)S(1)} %copy-done.36, ...), custom_call_target="tpu_custom_call" | custom-call | flops 49500000256 | bytes 162000000 | tf_op jit(solution)/shard_map/attend_back/pallas_call | solution.py:171
  247.8 3.5 %collective-permute-done.69.refs_1_ = bf16[8,320,128]{2,1,0:T(8,128)(2,1)S(1)} collective-permute-done((bf16[8,320,128]{2,1,0:T(8,128)(2,1)S(1)}, bf16[8,320,128]{2,1,0:T(8,128)(2,1)S(1)}, u32[]{:S(2)}, u32[]{:S(2)}) %collective-permute-start.69) | collective-permute-done | bytes 655392 | tf_op jit(solution)/shard_map/ppermute | solution.py:853
  251.4 3.3 %collective-permute-done.68.refs_1_ = bf16[8,384,128]{2,1,0:T(8,128)(2,1)S(1)} collective-permute-done((bf16[8,384,128]{2,1,0:T(8,128)(2,1)S(1)}, bf16[8,384,128]{2,1,0:T(8,128)(2,1)S(1)}, u32[]{:S(2)}, u32[]{:S(2)}) %collective-permute-start.68) | collective-permute-done | bytes 786464 | tf_op jit(solution)/shard_map/ppermute | solution.py:853
  256.2 1.6 collective-permute-start.79
  260.6 7.0 %collective-permute-done.72.refs_2_ = bf16[4,320,128]{2,1,0:T(8,128)(2,1)S(1)} collective-permute-done((bf16[4,320,128]{2,1,0:T(8,128)(2,1)S(1)}, bf16[4,320,128]{2,1,0:T(8,128)(2,1)S(1)}, u32[]{:S(2)}, u32[]{:S(2)}) %collective-permute-start.72) | collective-permute-done | bytes 327712 | tf_op jit(solution)/shard_map/ppermute | solution.py:853
  268.2 1.4 collective-permute-done.71
  269.6 3.3 %first_back.3 = (f32[512,512]{1,0:T(8,128)}, f32[8,512]{1,0:T(8,128)S(1)}, f32[8,128]{1,0:T(8,128)S(1)}) custom-call(s32[4]{0:T(128)S(1)} %copy-done.8, bf16[512,512]{1,0:T(8,128)(2,1)} %bitcast.32, f32[512,512]{1,0:T(8,128)S(1)} %get-tuple-element.300.refs_2_, f32[512,512]{1,0:T(8,128)S(1)} %get-tuple-element.315.refs_3_, f32[2,8,512]{2,1,0:T(8,128)S(1)} %copy-done.40, ...), custom_call_target="tpu_custom_call" | custom-call | flops 22000001024 | bytes 72000000 | tf_op jit(solution)/shard_map/first_back/pallas_call | solution.py:171
  275.4 2.7 collective-permute-done.85
  278.1 1.4 collective-permute-start.86
  279.5 2.1 collective-permute-start.76
  282.8 1.9 collective-permute-start.78
  285.9 2.0 collective-permute-start.82
  288.0 1.9 collective-permute-start.83
  291.2 8.2 %collective-permute-start.87 = (bf16[16,128]{1,0:T(8,128)(2,1)S(1)}, bf16[16,128]{1,0:T(8,128)(2,1)S(1)}, u32[]{:S(2)}, u32[]{:S(2)}) collective-permute-start(bf16[16,128]{1,0:T(8,128)(2,1)S(1)} %get-tuple-element.392), channel_id=1, source_target_pairs={{0,1},{1,0},{2,3},{3,2},{4,5},{5,4},{6,7},{7,6},{8,9},{9,8},{10,11... | collective-permute-start | bytes 12296 | tf_op jit(solution)/shard_map/ppermute | solution.py:853
  299.4 1.6 collective-permute-done.87.refs_9_
  301.9 2.1 collective-permute-done.88.refs_10_
  303.9 2.5 collective-permute-done.89.refs_11_
  306.5 1.5 finish.1
  (295 shorter events, 46.2 us)
Async XLA Ops:
  4.8 12.0 %collective-permute-start.4 = (bf16[208,128]{1,0:T(8,128)(2,1)S(1)}, bf16[208,128]{1,0:T(8,128)(2,1)S(1)}, u32[]{:S(2)}, u32[]{:S(2)}) collective-permute-start(bf16[208,128]{1,0:T(8,128)(2,1)S(1)} %get-tuple-element.207.refs_0_), channel_id=1, source_target_pairs={{0,3},{1,2},{2,1},{3,0},{4,7},{5,6},{6,5},{7,4},{8,11},{9,10},{10,... | collective-permute-start | bytes 159752 | tf_op jit(solution)/shard_map/ppermute | solution.py:853
  9.9 12.2 %collective-permute-start.3 = (bf16[208,128]{1,0:T(8,128)(2,1)S(1)}, bf16[208,128]{1,0:T(8,128)(2,1)S(1)}, u32[]{:S(2)}, u32[]{:S(2)}) collective-permute-start(bf16[208,128]{1,0:T(8,128)(2,1)S(1)} %get-tuple-element.207.refs_0_), channel_id=1, source_target_pairs={{0,2},{1,3},{2,0},{3,1},{4,6},{5,7},{6,4},{7,5},{8,10},{9,11},{10,... | collective-permute-start | bytes 159752 | tf_op jit(solution)/shard_map/ppermute | solution.py:853
  9.9 12.2 %collective-permute-start.2 = (bf16[208,128]{1,0:T(8,128)(2,1)S(1)}, bf16[208,128]{1,0:T(8,128)(2,1)S(1)}, u32[]{:S(2)}, u32[]{:S(2)}) collective-permute-start(bf16[208,128]{1,0:T(8,128)(2,1)S(1)} %get-tuple-element.207.refs_0_), channel_id=1, source_target_pairs={{0,1},{1,0},{2,3},{3,2},{4,5},{5,4},{6,7},{7,6},{8,9},{9,8},{10,11... | collective-permute-start | bytes 159752 | tf_op jit(solution)/shard_map/ppermute | solution.py:853
  10.6 17.9 %collective-permute-start.9 = (bf16[704,128]{1,0:T(8,128)(2,1)S(1)}, bf16[704,128]{1,0:T(8,128)(2,1)S(1)}, u32[]{:S(2)}, u32[]{:S(2)}) collective-permute-start(bf16[704,128]{1,0:T(8,128)(2,1)S(1)} %get-tuple-element.213.refs_0_), channel_id=1, source_target_pairs={{0,3},{1,2},{2,1},{3,0},{4,7},{5,6},{6,5},{7,4},{8,11},{9,10},{10,... | collective-permute-start | bytes 540680 | tf_op jit(solution)/shard_map/ppermute | solution.py:853
  14.4 12.5 %collective-permute-start.1 = (bf16[2,256,512]{2,1,0:T(8,128)(2,1)S(1)}, bf16[2,256,512]{2,1,0:T(8,128)(2,1)S(1)}, u32[]{:S(2)}, u32[]{:S(2)}) collective-permute-start(bf16[2,256,512]{2,1,0:T(8,128)(2,1)S(1)} %copy-done.15), channel_id=1, source_target_pairs={{0,8},{4,12},{8,0},{12,4},{1,9},{5,13},{9,1},{13,5},{2,10},{6,14},... | collective-permute-start | bytes 1572872 | tf_op jit(solution)/shard_map/ppermute | solution.py:853
  16.8 13.4 %collective-permute-start.8 = (bf16[704,128]{1,0:T(8,128)(2,1)S(1)}, bf16[704,128]{1,0:T(8,128)(2,1)S(1)}, u32[]{:S(2)}, u32[]{:S(2)}) collective-permute-start(bf16[704,128]{1,0:T(8,128)(2,1)S(1)} %get-tuple-element.213.refs_0_), channel_id=1, source_target_pairs={{0,2},{1,3},{2,0},{3,1},{4,6},{5,7},{6,4},{7,5},{8,10},{9,11},{10,... | collective-permute-start | bytes 540680 | tf_op jit(solution)/shard_map/ppermute | solution.py:853
  22.1 9.2 %collective-permute-start.7 = (bf16[704,128]{1,0:T(8,128)(2,1)S(1)}, bf16[704,128]{1,0:T(8,128)(2,1)S(1)}, u32[]{:S(2)}, u32[]{:S(2)}) collective-permute-start(bf16[704,128]{1,0:T(8,128)(2,1)S(1)} %get-tuple-element.213.refs_0_), channel_id=1, source_target_pairs={{0,1},{1,0},{2,3},{3,2},{4,5},{5,4},{6,7},{7,6},{8,9},{9,8},{10,11... | collective-permute-start | bytes 540680 | tf_op jit(solution)/shard_map/ppermute | solution.py:853
  22.1 13.7 %collective-permute-start = (bf16[2,256,512]{2,1,0:T(8,128)(2,1)S(1)}, bf16[2,256,512]{2,1,0:T(8,128)(2,1)S(1)}, u32[]{:S(2)}, u32[]{:S(2)}) collective-permute-start(bf16[2,256,512]{2,1,0:T(8,128)(2,1)S(1)} %copy-done.15), channel_id=1, source_target_pairs={{0,4},{4,0},{8,12},{12,8},{1,5},{5,1},{9,13},{13,9},{2,6},{6,2},{1... | collective-permute-start | bytes 1572872 | tf_op jit(solution)/shard_map/ppermute | solution.py:853
  28.5 8.8 %collective-permute-start.5 = (bf16[2,256,512]{2,1,0:T(8,128)(2,1)S(1)}, bf16[2,256,512]{2,1,0:T(8,128)(2,1)S(1)}, u32[]{:S(2)}, u32[]{:S(2)}) collective-permute-start(bf16[2,256,512]{2,1,0:T(8,128)(2,1)S(1)} %get-tuple-element.211), channel_id=1, source_target_pairs={{0,4},{4,0},{8,12},{12,8},{1,5},{5,1},{9,13},{13,9},{2,6},{6,2},{1... | collective-permute-start | bytes 1572872 | tf_op jit(solution)/shard_map/ppermute | solution.py:853
  31.4 21.6 %collective-permute-start.20 = (bf16[896,128]{1,0:T(8,128)(2,1)S(1)}, bf16[896,128]{1,0:T(8,128)(2,1)S(1)}, u32[]{:S(2)}, u32[]{:S(2)}) collective-permute-start(bf16[896,128]{1,0:T(8,128)(2,1)S(1)} %get-tuple-element.224.refs_0_), channel_id=1, source_target_pairs={{0,3},{1,2},{2,1},{3,0},{4,7},{5,6},{6,5},{7,4},{8,11},{9,10},{10,... | collective-permute-start | bytes 688136 | tf_op jit(solution)/shard_map/ppermute | solution.py:853
  32.9 20.1 %collective-permute-start.19 = (bf16[896,128]{1,0:T(8,128)(2,1)S(1)}, bf16[896,128]{1,0:T(8,128)(2,1)S(1)}, u32[]{:S(2)}, u32[]{:S(2)}) collective-permute-start(bf16[896,128]{1,0:T(8,128)(2,1)S(1)} %get-tuple-element.224.refs_0_), channel_id=1, source_target_pairs={{0,2},{1,3},{2,0},{3,1},{4,6},{5,7},{6,4},{7,5},{8,10},{9,11},{10,... | collective-permute-start | bytes 688136 | tf_op jit(solution)/shard_map/ppermute | solution.py:853
  32.9 20.1 %collective-permute-start.18 = (bf16[896,128]{1,0:T(8,128)(2,1)S(1)}, bf16[896,128]{1,0:T(8,128)(2,1)S(1)}, u32[]{:S(2)}, u32[]{:S(2)}) collective-permute-start(bf16[896,128]{1,0:T(8,128)(2,1)S(1)} %get-tuple-element.224.refs_0_), channel_id=1, source_target_pairs={{0,1},{1,0},{2,3},{3,2},{4,5},{5,4},{6,7},{7,6},{8,9},{9,8},{10,11... | collective-permute-start | bytes 688136 | tf_op jit(solution)/shard_map/ppermute | solution.py:853
  35.9 17.2 %collective-permute-start.14 = (bf16[4,704,128]{2,1,0:T(8,128)(2,1)S(1)}, bf16[4,704,128]{2,1,0:T(8,128)(2,1)S(1)}, u32[]{:S(2)}, u32[]{:S(2)}) collective-permute-start(bf16[4,704,128]{2,1,0:T(8,128)(2,1)S(1)} %get-tuple-element.223.refs_9_.refs_7_.refs_10_), channel_id=1, source_target_pairs={{0,8},{4,12},{8,0},{12,4},{1,9},{5,13},{9,1},{13,5},{2,10},{6,14},... | collective-permute-start | bytes 2162696 | tf_op jit(solution)/shard_map/ppermute | solution.py:853
  37.3 15.8 %collective-permute-start.13 = (bf16[4,704,128]{2,1,0:T(8,128)(2,1)S(1)}, bf16[4,704,128]{2,1,0:T(8,128)(2,1)S(1)}, u32[]{:S(2)}, u32[]{:S(2)}) collective-permute-start(bf16[4,704,128]{2,1,0:T(8,128)(2,1)S(1)} %get-tuple-element.223.refs_9_.refs_7_.refs_10_), channel_id=1, source_target_pairs={{0,16},{16,0},{1,17},{17,1},{2,18},{18,2},{3,19},{19,3},{4,20},{20... | collective-permute-start | bytes 2162696 | tf_op jit(solution)/shard_map/ppermute | solution.py:853
  53.2 12.1 %collective-permute-start.22 = (bf16[4,320,128]{2,1,0:T(8,128)(2,1)S(1)}, bf16[4,320,128]{2,1,0:T(8,128)(2,1)S(1)}, u32[]{:S(2)}, u32[]{:S(2)}) collective-permute-start(bf16[4,320,128]{2,1,0:T(8,128)(2,1)S(1)} %get-tuple-element.227), channel_id=1, source_target_pairs={{0,8},{4,12},{8,0},{12,4},{1,9},{5,13},{9,1},{13,5},{2,10},{6,14},... | collective-permute-start | bytes 983048 | tf_op jit(solution)/shard_map/ppermute | solution.py:853
  53.9 11.4 %collective-permute-start.11 = (bf16[2,2,256,128]{3,2,1,0:T(8,128)(2,1)S(1)}, bf16[2,2,256,128]{3,2,1,0:T(8,128)(2,1)S(1)}, u32[]{:S(2)}, u32[]{:S(2)}) collective-permute-start(bf16[2,2,256,128]{3,2,1,0:T(8,128)(2,1)S(1)} %get-tuple-element.222), channel_id=1, source_target_pairs={{0,8},{4,12},{8,0},{12,4},{1,9},{5,13},{9,1},{13,5},{2,10},{6,14},... | collective-permute-start | bytes 786440 | tf_op jit(solution)/shard_map/ppermute | solution.py:853
  55.3 12.2 %collective-permute-start.15 = (bf16[4,704,128]{2,1,0:T(8,128)(2,1)S(1)}, bf16[4,704,128]{2,1,0:T(8,128)(2,1)S(1)}, u32[]{:S(2)}, u32[]{:S(2)}) collective-permute-start(bf16[4,704,128]{2,1,0:T(8,128)(2,1)S(1)} %get-tuple-element.223.refs_9_.refs_7_.refs_10_), channel_id=1, source_target_pairs={{0,4},{4,0},{8,12},{12,8},{1,5},{5,1},{9,13},{13,9},{2,6},{6,2},{1... | collective-permute-start | bytes 2162696 | tf_op jit(solution)/shard_map/ppermute | solution.py:853
  55.3 11.7 %collective-permute-start.10 = (bf16[2,256,128]{2,1,0:T(8,128)(2,1)S(1)}, bf16[2,256,128]{2,1,0:T(8,128)(2,1)S(1)}, u32[]{:S(2)}, u32[]{:S(2)}) collective-permute-start(bf16[2,256,128]{2,1,0:T(8,128)(2,1)S(1)} %get-tuple-element.221), channel_id=1, source_target_pairs={{0,4},{4,0},{8,12},{12,8},{1,5},{5,1},{9,13},{13,9},{2,6},{6,2},{1... | collective-permute-start | bytes 393224 | tf_op jit(solution)/shard_map/ppermute | solution.py:853
  55.8 11.0 %collective-permute-start.21 = (bf16[4,384,128]{2,1,0:T(8,128)(2,1)S(1)}, bf16[4,384,128]{2,1,0:T(8,128)(2,1)S(1)}, u32[]{:S(2)}, u32[]{:S(2)}) collective-permute-start(bf16[4,384,128]{2,1,0:T(8,128)(2,1)S(1)} %get-tuple-element.226), channel_id=1, source_target_pairs={{0,16},{16,0},{1,17},{17,1},{2,18},{18,2},{3,19},{19,3},{4,20},{20... | collective-permute-start | bytes 1179656 | tf_op jit(solution)/shard_map/ppermute | solution.py:853
  69.9 29.7 %collective-permute-start.33 = (bf16[4,704,128]{2,1,0:T(8,128)(2,1)S(1)}, bf16[4,704,128]{2,1,0:T(8,128)(2,1)S(1)}, u32[]{:S(2)}, u32[]{:S(2)}) collective-permute-start(bf16[4,704,128]{2,1,0:T(8,128)(2,1)S(1)} %get-tuple-element.237.refs_9_.refs_7_.refs_10_), channel_id=1, source_target_pairs={{0,16},{16,0},{1,17},{17,1},{2,18},{18,2},{3,19},{19,3},{4,20},{20... | collective-permute-start | bytes 2162696 | tf_op jit(solution)/shard_map/ppermute | solution.py:853
  70.5 29.7 %collective-permute-start.32 = (bf16[4,704,128]{2,1,0:T(8,128)(2,1)S(1)}, bf16[4,704,128]{2,1,0:T(8,128)(2,1)S(1)}, u32[]{:S(2)}, u32[]{:S(2)}) collective-permute-start(bf16[4,704,128]{2,1,0:T(8,128)(2,1)S(1)} %get-tuple-element.237.refs_9_.refs_7_.refs_10_), channel_id=1, source_target_pairs={{0,8},{4,12},{8,0},{12,4},{1,9},{5,13},{9,1},{13,5},{2,10},{6,14},... | collective-permute-start | bytes 2162696 | tf_op jit(solution)/shard_map/ppermute | solution.py:853
  84.0 11.1 %collective-permute-start.27 = (bf16[256,512]{1,0:T(8,128)(2,1)S(1)}, bf16[256,512]{1,0:T(8,128)(2,1)S(1)}, u32[]{:S(2)}, u32[]{:S(2)}) collective-permute-start(bf16[256,512]{1,0:T(8,128)(2,1)S(1)} %get-tuple-element.234.refs_3_.refs_8_.refs_9_), channel_id=1, source_target_pairs={{0,8},{4,12},{8,0},{12,4},{1,9},{5,13},{9,1},{13,5},{2,10},{6,14},... | collective-permute-start | bytes 786440 | tf_op jit(solution)/shard_map/ppermute | solution.py:853
  84.4 15.2 %collective-permute-start.28 = (bf16[256,512]{1,0:T(8,128)(2,1)S(1)}, bf16[256,512]{1,0:T(8,128)(2,1)S(1)}, u32[]{:S(2)}, u32[]{:S(2)}) collective-permute-start(bf16[256,512]{1,0:T(8,128)(2,1)S(1)} %get-tuple-element.235.refs_4_.refs_9_), channel_id=1, source_target_pairs={{0,8},{4,12},{8,0},{12,4},{1,9},{5,13},{9,1},{13,5},{2,10},{6,14},... | collective-permute-start | bytes 786440 | tf_op jit(solution)/shard_map/ppermute | solution.py:853
  92.3 25.9 %collective-permute-start.37 = (bf16[4,704,128]{2,1,0:T(8,128)(2,1)S(1)}, bf16[4,704,128]{2,1,0:T(8,128)(2,1)S(1)}, u32[]{:S(2)}, u32[]{:S(2)}) collective-permute-start(bf16[4,704,128]{2,1,0:T(8,128)(2,1)S(1)} %get-tuple-element.237.refs_9_.refs_7_.refs_10_), channel_id=1, source_target_pairs={{0,4},{4,0},{8,12},{12,8},{1,5},{5,1},{9,13},{13,9},{2,6},{6,2},{1... | collective-permute-start | bytes 2162696 | tf_op jit(solution)/shard_map/ppermute | solution.py:853
  100.3 16.4 %collective-permute-start.41 = (bf16[4,320,128]{2,1,0:T(8,128)(2,1)S(1)}, bf16[4,320,128]{2,1,0:T(8,128)(2,1)S(1)}, u32[]{:S(2)}, u32[]{:S(2)}) collective-permute-start(bf16[4,320,128]{2,1,0:T(8,128)(2,1)S(1)} %get-tuple-element.244), channel_id=1, source_target_pairs={{0,8},{4,12},{8,0},{12,4},{1,9},{5,13},{9,1},{13,5},{2,10},{6,14},... | collective-permute-start | bytes 983048 | tf_op jit(solution)/shard_map/ppermute | solution.py:853
  102.0 16.0 %collective-permute-start.40 = (bf16[4,384,128]{2,1,0:T(8,128)(2,1)S(1)}, bf16[4,384,128]{2,1,0:T(8,128)(2,1)S(1)}, u32[]{:S(2)}, u32[]{:S(2)}) collective-permute-start(bf16[4,384,128]{2,1,0:T(8,128)(2,1)S(1)} %get-tuple-element.243), channel_id=1, source_target_pairs={{0,16},{16,0},{1,17},{17,1},{2,18},{18,2},{3,19},{19,3},{4,20},{20... | collective-permute-start | bytes 1179656 | tf_op jit(solution)/shard_map/ppermute | solution.py:853
  102.6 24.2 %collective-permute-start.38 = (bf16[4,704,128]{2,1,0:T(8,128)(2,1)S(1)}, bf16[4,704,128]{2,1,0:T(8,128)(2,1)}, u32[]{:S(2)}, u32[]{:S(2)}) collective-permute-start(bf16[4,704,128]{2,1,0:T(8,128)(2,1)S(1)} %collective-permute-done.33.refs_0_.refs_1_.refs_10_.refs_8_.refs_11_), channel_id=1, source_target_pairs={{0,4},{4,0},{8,12},{12,8},{1,5},{5,1},{9,13},{13,9},{2,6},{6,2},{1... | collective-permute-start | bytes 2162696 | tf_op jit(solution)/shard_map/ppermute | solution.py:853
  102.7 24.1 %collective-permute-start.39 = (bf16[4,704,128]{2,1,0:T(8,128)(2,1)S(1)}, bf16[4,704,128]{2,1,0:T(8,128)(2,1)}, u32[]{:S(2)}, u32[]{:S(2)}) collective-permute-start(bf16[4,704,128]{2,1,0:T(8,128)(2,1)S(1)} %collective-permute-done.32.refs_1_.refs_0_.refs_11_.refs_9_.refs_12_), channel_id=1, source_target_pairs={{0,4},{4,0},{8,12},{12,8},{1,5},{5,1},{9,13},{13,9},{2,6},{6,2},{1... | collective-permute-start | bytes 2162696 | tf_op jit(solution)/shard_map/ppermute | solution.py:853
  116.8 8.5 %collective-permute-start.35 = (bf16[2,2,256,128]{3,2,1,0:T(8,128)(2,1)}, bf16[2,2,256,128]{3,2,1,0:T(8,128)(2,1)S(1)}, u32[]{:S(2)}, u32[]{:S(2)}) collective-permute-start(bf16[2,2,256,128]{3,2,1,0:T(8,128)(2,1)} %get-tuple-element.242), channel_id=1, source_target_pairs={{0,8},{4,12},{8,0},{12,4},{1,9},{5,13},{9,1},{13,5},{2,10},{6,14},... | collective-permute-start | bytes 786440 | tf_op jit(solution)/shard_map/ppermute | solution.py:853
  119.1 7.7 %collective-permute-start.42 = (bf16[4,384,128]{2,1,0:T(8,128)(2,1)S(1)}, bf16[4,384,128]{2,1,0:T(8,128)(2,1)}, u32[]{:S(2)}, u32[]{:S(2)}) collective-permute-start(bf16[4,384,128]{2,1,0:T(8,128)(2,1)S(1)} %get-tuple-element.246.refs_15_.refs_13_.refs_16_), channel_id=1, source_target_pairs={{0,4},{4,0},{8,12},{12,8},{1,5},{5,1},{9,13},{13,9},{2,6},{6,2},{1... | collective-permute-start | bytes 1179656 | tf_op jit(solution)/shard_map/ppermute | solution.py:853
  147.3 9.5 %collective-permute-start.44 = (bf16[2,256,128]{2,1,0:T(8,128)(2,1)S(1)}, bf16[2,256,128]{2,1,0:T(8,128)(2,1)S(1)}, u32[]{:S(2)}, u32[]{:S(2)}) collective-permute-start(bf16[2,256,128]{2,1,0:T(8,128)(2,1)S(1)} %get-tuple-element.269), channel_id=1, source_target_pairs={{0,4},{4,0},{8,12},{12,8},{1,5},{5,1},{9,13},{13,9},{2,6},{6,2},{1... | collective-permute-start | bytes 393224 | tf_op jit(solution)/shard_map/ppermute | solution.py:853
  147.5 9.2 %collective-permute-start.45 = (bf16[2,2,256,128]{3,2,1,0:T(8,128)(2,1)S(1)}, bf16[2,2,256,128]{3,2,1,0:T(8,128)(2,1)S(1)}, u32[]{:S(2)}, u32[]{:S(2)}) collective-permute-start(bf16[2,2,256,128]{3,2,1,0:T(8,128)(2,1)S(1)} %get-tuple-element.270), channel_id=1, source_target_pairs={{0,8},{4,12},{8,0},{12,4},{1,9},{5,13},{9,1},{13,5},{2,10},{6,14},... | collective-permute-start | bytes 786440 | tf_op jit(solution)/shard_map/ppermute | solution.py:853
  156.1 11.4 %collective-permute-start.48 = (bf16[16,320,128]{2,1,0:T(8,128)(2,1)S(1)}, bf16[16,320,128]{2,1,0:T(8,128)(2,1)S(1)}, u32[]{:S(2)}, u32[]{:S(2)}) collective-permute-start(bf16[16,320,128]{2,1,0:T(8,128)(2,1)S(1)} %get-tuple-element.275), channel_id=1, source_target_pairs={{0,4},{4,0},{8,12},{12,8},{1,5},{5,1},{9,13},{13,9},{2,6},{6,2},{1... | collective-permute-start | bytes 3932168 | tf_op jit(solution)/shard_map/ppermute | solution.py:853
  156.3 10.9 %collective-permute-start.49 = (bf16[16,384,128]{2,1,0:T(8,128)(2,1)S(1)}, bf16[16,384,128]{2,1,0:T(8,128)(2,1)S(1)}, u32[]{:S(2)}, u32[]{:S(2)}) collective-permute-start(bf16[16,384,128]{2,1,0:T(8,128)(2,1)S(1)} %get-tuple-element.277), channel_id=1, source_target_pairs={{0,4},{4,0},{8,12},{12,8},{1,5},{5,1},{9,13},{13,9},{2,6},{6,2},{1... | collective-permute-start | bytes 4718600 | tf_op jit(solution)/shard_map/ppermute | solution.py:853
  167.9 17.1 %collective-permute-start.51 = (bf16[8,320,128]{2,1,0:T(8,128)(2,1)S(1)}, bf16[8,320,128]{2,1,0:T(8,128)(2,1)S(1)}, u32[]{:S(2)}, u32[]{:S(2)}) collective-permute-start(bf16[8,320,128]{2,1,0:T(8,128)(2,1)S(1)} %get-tuple-element.287), channel_id=1, source_target_pairs={{0,16},{16,0},{1,17},{17,1},{2,18},{18,2},{3,19},{19,3},{4,20},{20... | collective-permute-start | bytes 1966088 | tf_op jit(solution)/shard_map/ppermute | solution.py:853
  178.9 10.9 %collective-permute-start.52 = (bf16[1,256,512]{2,1,0:T(8,128)(2,1)S(1)}, bf16[1,256,512]{2,1,0:T(8,128)(2,1)S(1)}, u32[]{:S(2)}, u32[]{:S(2)}) collective-permute-start(bf16[1,256,512]{2,1,0:T(8,128)(2,1)S(1)} %get-tuple-element.291), channel_id=1, source_target_pairs={{0,8},{4,12},{8,0},{12,4},{1,9},{5,13},{9,1},{13,5},{2,10},{6,14},... | collective-permute-start | bytes 786440 | tf_op jit(solution)/shard_map/ppermute | solution.py:853
  185.6 9.3 %collective-permute-start.53 = (bf16[1,256,512]{2,1,0:T(8,128)(2,1)S(1)}, bf16[1,256,512]{2,1,0:T(8,128)(2,1)S(1)}, u32[]{:S(2)}, u32[]{:S(2)}) collective-permute-start(bf16[1,256,512]{2,1,0:T(8,128)(2,1)S(1)} %get-tuple-element.292), channel_id=1, source_target_pairs={{0,8},{4,12},{8,0},{12,4},{1,9},{5,13},{9,1},{13,5},{2,10},{6,14},... | collective-permute-start | bytes 786440 | tf_op jit(solution)/shard_map/ppermute | solution.py:853
  186.5 20.8 %collective-permute-start.55 = (bf16[4,192,128]{2,1,0:T(8,128)(2,1)S(1)}, bf16[4,192,128]{2,1,0:T(8,128)(2,1)S(1)}, u32[]{:S(2)}, u32[]{:S(2)}) collective-permute-start(bf16[4,192,128]{2,1,0:T(8,128)(2,1)S(1)} %get-tuple-element.408), channel_id=1, source_target_pairs={{0,16},{16,0},{1,17},{17,1},{2,18},{18,2},{3,19},{19,3},{4,20},{20... | collective-permute-start | bytes 589832 | tf_op jit(solution)/shard_map/ppermute | solution.py:853
  188.0 23.5 %collective-permute-start.54 = (bf16[8,384,128]{2,1,0:T(8,128)(2,1)S(1)}, bf16[8,384,128]{2,1,0:T(8,128)(2,1)S(1)}, u32[]{:S(2)}, u32[]{:S(2)}) collective-permute-start(bf16[8,384,128]{2,1,0:T(8,128)(2,1)S(1)} %get-tuple-element.308), channel_id=1, source_target_pairs={{0,16},{16,0},{1,17},{17,1},{2,18},{18,2},{3,19},{19,3},{4,20},{20... | collective-permute-start | bytes 2359304 | tf_op jit(solution)/shard_map/ppermute | solution.py:853
  188.6 18.7 %collective-permute-start.56 = (bf16[4,320,128]{2,1,0:T(8,128)(2,1)S(1)}, bf16[4,320,128]{2,1,0:T(8,128)(2,1)S(1)}, u32[]{:S(2)}, u32[]{:S(2)}) collective-permute-start(bf16[4,320,128]{2,1,0:T(8,128)(2,1)S(1)} %get-tuple-element.311), channel_id=1, source_target_pairs={{0,8},{4,12},{8,0},{12,4},{1,9},{5,13},{9,1},{13,5},{2,10},{6,14},... | collective-permute-start | bytes 983048 | tf_op jit(solution)/shard_map/ppermute | solution.py:853
  206.3 13.9 %collective-permute-start.57 = (bf16[2,256,128]{2,1,0:T(8,128)(2,1)S(1)}, bf16[2,256,128]{2,1,0:T(8,128)(2,1)S(1)}, u32[]{:S(2)}, u32[]{:S(2)}) collective-permute-start(bf16[2,256,128]{2,1,0:T(8,128)(2,1)S(1)} %get-tuple-element.321), channel_id=1, source_target_pairs={{0,4},{4,0},{8,12},{12,8},{1,5},{5,1},{9,13},{13,9},{2,6},{6,2},{1... | collective-permute-start | bytes 393224 | tf_op jit(solution)/shard_map/ppermute | solution.py:853
  206.4 13.7 %collective-permute-start.58 = (bf16[2,2,256,128]{3,2,1,0:T(8,128)(2,1)S(1)}, bf16[2,2,256,128]{3,2,1,0:T(8,128)(2,1)S(1)}, u32[]{:S(2)}, u32[]{:S(2)}) collective-permute-start(bf16[2,2,256,128]{3,2,1,0:T(8,128)(2,1)S(1)} %get-tuple-element.322), channel_id=1, source_target_pairs={{0,8},{4,12},{8,0},{12,4},{1,9},{5,13},{9,1},{13,5},{2,10},{6,14},... | collective-permute-start | bytes 786440 | tf_op jit(solution)/shard_map/ppermute | solution.py:853
  207.9 22.4 %collective-permute-start.61 = (bf16[512,128]{1,0:T(8,128)(2,1)S(1)}, bf16[512,128]{1,0:T(8,128)(2,1)S(1)}, u32[]{:S(2)}, u32[]{:S(2)}) collective-permute-start(bf16[512,128]{1,0:T(8,128)(2,1)S(1)} %get-tuple-element.330), channel_id=1, source_target_pairs={{0,1},{1,0},{2,3},{3,2},{4,5},{5,4},{6,7},{7,6},{8,9},{9,8},{10,11... | collective-permute-start | bytes 393224 | tf_op jit(solution)/shard_map/ppermute | solution.py:853
  208.9 24.6 %collective-permute-start.62 = (bf16[512,128]{1,0:T(8,128)(2,1)S(1)}, bf16[512,128]{1,0:T(8,128)(2,1)S(1)}, u32[]{:S(2)}, u32[]{:S(2)}) collective-permute-start(bf16[512,128]{1,0:T(8,128)(2,1)S(1)} %get-tuple-element.331), channel_id=1, source_target_pairs={{0,2},{1,3},{2,0},{3,1},{4,6},{5,7},{6,4},{7,5},{8,10},{9,11},{10,... | collective-permute-start | bytes 393224 | tf_op jit(solution)/shard_map/ppermute | solution.py:853
  211.7 15.7 %collective-permute-start.66 = (bf16[4,384,128]{2,1,0:T(8,128)(2,1)S(1)}, bf16[4,384,128]{2,1,0:T(8,128)(2,1)S(1)}, u32[]{:S(2)}, u32[]{:S(2)}) collective-permute-start(bf16[4,384,128]{2,1,0:T(8,128)(2,1)S(1)} %get-tuple-element.338), channel_id=1, source_target_pairs={{0,8},{4,12},{8,0},{12,4},{1,9},{5,13},{9,1},{13,5},{2,10},{6,14},... | collective-permute-start | bytes 1179656 | tf_op jit(solution)/shard_map/ppermute | solution.py:853
  220.2 9.6 %collective-permute-start.64 = (bf16[16,320,128]{2,1,0:T(8,128)(2,1)S(1)}, bf16[16,320,128]{2,1,0:T(8,128)(2,1)S(1)}, u32[]{:S(2)}, u32[]{:S(2)}) collective-permute-start(bf16[16,320,128]{2,1,0:T(8,128)(2,1)S(1)} %get-tuple-element.334), channel_id=1, source_target_pairs={{0,4},{4,0},{8,12},{12,8},{1,5},{5,1},{9,13},{13,9},{2,6},{6,2},{1... | collective-permute-start | bytes 3932168 | tf_op jit(solution)/shard_map/ppermute | solution.py:853
  227.4 8.2 %collective-permute-start.63 = (bf16[512,128]{1,0:T(8,128)(2,1)S(1)}, bf16[512,128]{1,0:T(8,128)(2,1)S(1)}, u32[]{:S(2)}, u32[]{:S(2)}) collective-permute-start(bf16[512,128]{1,0:T(8,128)(2,1)S(1)} %get-tuple-element.332), channel_id=1, source_target_pairs={{0,3},{1,2},{2,1},{3,0},{4,7},{5,6},{6,5},{7,4},{8,11},{9,10},{10,... | collective-permute-start | bytes 393224 | tf_op jit(solution)/shard_map/ppermute | solution.py:853
  229.1 28.8 %collective-permute-start.73 = (bf16[384,128]{1,0:T(8,128)(2,1)S(1)}, bf16[384,128]{1,0:T(8,128)(2,1)S(1)}, u32[]{:S(2)}, u32[]{:S(2)}) collective-permute-start(bf16[384,128]{1,0:T(8,128)(2,1)S(1)} %get-tuple-element.365), channel_id=1, source_target_pairs={{0,1},{1,0},{2,3},{3,2},{4,5},{5,4},{6,7},{7,6},{8,9},{9,8},{10,11... | collective-permute-start | bytes 294920 | tf_op jit(solution)/shard_map/ppermute | solution.py:853
  230.3 28.2 %collective-permute-start.74 = (bf16[384,128]{1,0:T(8,128)(2,1)S(1)}, bf16[384,128]{1,0:T(8,128)(2,1)S(1)}, u32[]{:S(2)}, u32[]{:S(2)}) collective-permute-start(bf16[384,128]{1,0:T(8,128)(2,1)S(1)} %get-tuple-element.366), channel_id=1, source_target_pairs={{0,2},{1,3},{2,0},{3,1},{4,6},{5,7},{6,4},{7,5},{8,10},{9,11},{10,... | collective-permute-start | bytes 294920 | tf_op jit(solution)/shard_map/ppermute | solution.py:853
  233.5 25.8 %collective-permute-start.75 = (bf16[384,128]{1,0:T(8,128)(2,1)S(1)}, bf16[384,128]{1,0:T(8,128)(2,1)S(1)}, u32[]{:S(2)}, u32[]{:S(2)}) collective-permute-start(bf16[384,128]{1,0:T(8,128)(2,1)S(1)} %get-tuple-element.367), channel_id=1, source_target_pairs={{0,3},{1,2},{2,1},{3,0},{4,7},{5,6},{6,5},{7,4},{8,11},{9,10},{10,... | collective-permute-start | bytes 294920 | tf_op jit(solution)/shard_map/ppermute | solution.py:853
  235.6 15.6 %collective-permute-start.69 = (bf16[8,320,128]{2,1,0:T(8,128)(2,1)S(1)}, bf16[8,320,128]{2,1,0:T(8,128)(2,1)S(1)}, u32[]{:S(2)}, u32[]{:S(2)}) collective-permute-start(bf16[8,320,128]{2,1,0:T(8,128)(2,1)S(1)} %get-tuple-element.355), channel_id=1, source_target_pairs={{0,8},{4,12},{8,0},{12,4},{1,9},{5,13},{9,1},{13,5},{2,10},{6,14},... | collective-permute-start | bytes 1966088 | tf_op jit(solution)/shard_map/ppermute | solution.py:853
  236.6 18.2 %collective-permute-start.68 = (bf16[8,384,128]{2,1,0:T(8,128)(2,1)S(1)}, bf16[8,384,128]{2,1,0:T(8,128)(2,1)S(1)}, u32[]{:S(2)}, u32[]{:S(2)}) collective-permute-start(bf16[8,384,128]{2,1,0:T(8,128)(2,1)S(1)} %get-tuple-element.353), channel_id=1, source_target_pairs={{0,16},{16,0},{1,17},{17,1},{2,18},{18,2},{3,19},{19,3},{4,20},{20... | collective-permute-start | bytes 2359304 | tf_op jit(solution)/shard_map/ppermute | solution.py:853
  254.8 13.4 %collective-permute-start.70 = (bf16[1,256,512]{2,1,0:T(8,128)(2,1)S(1)}, bf16[1,256,512]{2,1,0:T(8,128)(2,1)S(1)}, u32[]{:S(2)}, u32[]{:S(2)}) collective-permute-start(bf16[1,256,512]{2,1,0:T(8,128)(2,1)S(1)} %get-tuple-element.360), channel_id=1, source_target_pairs={{0,8},{4,12},{8,0},{12,4},{1,9},{5,13},{9,1},{13,5},{2,10},{6,14},... | collective-permute-start | bytes 786440 | tf_op jit(solution)/shard_map/ppermute | solution.py:853
  256.2 28.5 %collective-permute-start.79 = (bf16[4,192,128]{2,1,0:T(8,128)(2,1)S(1)}, bf16[4,192,128]{2,1,0:T(8,128)(2,1)S(1)}, u32[]{:S(2)}, u32[]{:S(2)}) collective-permute-start(bf16[4,192,128]{2,1,0:T(8,128)(2,1)S(1)} %get-tuple-element.406), channel_id=1, source_target_pairs={{0,16},{16,0},{1,17},{17,1},{2,18},{18,2},{3,19},{19,3},{4,20},{20... | collective-permute-start | bytes 589832 | tf_op jit(solution)/shard_map/ppermute | solution.py:853
  257.9 9.7 %collective-permute-start.72 = (bf16[4,320,128]{2,1,0:T(8,128)(2,1)S(1)}, bf16[4,320,128]{2,1,0:T(8,128)(2,1)S(1)}, u32[]{:S(2)}, u32[]{:S(2)}) collective-permute-start(bf16[4,320,128]{2,1,0:T(8,128)(2,1)S(1)} %get-tuple-element.363), channel_id=1, source_target_pairs={{0,16},{16,0},{1,17},{17,1},{2,18},{18,2},{3,19},{19,3},{4,20},{20... | collective-permute-start | bytes 983048 | tf_op jit(solution)/shard_map/ppermute | solution.py:853
  258.5 11.1 %collective-permute-start.71 = (bf16[1,256,512]{2,1,0:T(8,128)(2,1)S(1)}, bf16[1,256,512]{2,1,0:T(8,128)(2,1)S(1)}, u32[]{:S(2)}, u32[]{:S(2)}) collective-permute-start(bf16[1,256,512]{2,1,0:T(8,128)(2,1)S(1)} %get-tuple-element.361), channel_id=1, source_target_pairs={{0,8},{4,12},{8,0},{12,4},{1,9},{5,13},{9,1},{13,5},{2,10},{6,14},... | collective-permute-start | bytes 786440 | tf_op jit(solution)/shard_map/ppermute | solution.py:853
  259.3 25.4 %collective-permute-start.80 = (bf16[4,384,128]{2,1,0:T(8,128)(2,1)S(1)}, bf16[4,384,128]{2,1,0:T(8,128)(2,1)S(1)}, u32[]{:S(2)}, u32[]{:S(2)}) collective-permute-start(bf16[4,384,128]{2,1,0:T(8,128)(2,1)S(1)} %get-tuple-element.380), channel_id=1, source_target_pairs={{0,8},{4,12},{8,0},{12,4},{1,9},{5,13},{9,1},{13,5},{2,10},{6,14},... | collective-permute-start | bytes 1179656 | tf_op jit(solution)/shard_map/ppermute | solution.py:853
  279.5 8.4 %collective-permute-start.76 = (bf16[320,128]{1,0:T(8,128)(2,1)S(1)}, bf16[320,128]{1,0:T(8,128)(2,1)S(1)}, u32[]{:S(2)}, u32[]{:S(2)}) collective-permute-start(bf16[320,128]{1,0:T(8,128)(2,1)S(1)} %get-tuple-element.375), channel_id=1, source_target_pairs={{0,1},{1,0},{2,3},{3,2},{4,5},{5,4},{6,7},{7,6},{8,9},{9,8},{10,11... | collective-permute-start | bytes 245768 | tf_op jit(solution)/shard_map/ppermute | solution.py:853
  281.7 8.9 %collective-permute-start.77 = (bf16[320,128]{1,0:T(8,128)(2,1)S(1)}, bf16[320,128]{1,0:T(8,128)(2,1)S(1)}, u32[]{:S(2)}, u32[]{:S(2)}) collective-permute-start(bf16[320,128]{1,0:T(8,128)(2,1)S(1)} %get-tuple-element.376), channel_id=1, source_target_pairs={{0,2},{1,3},{2,0},{3,1},{4,6},{5,7},{6,4},{7,5},{8,10},{9,11},{10,... | collective-permute-start | bytes 245768 | tf_op jit(solution)/shard_map/ppermute | solution.py:853
  282.8 7.8 %collective-permute-start.78 = (bf16[320,128]{1,0:T(8,128)(2,1)S(1)}, bf16[320,128]{1,0:T(8,128)(2,1)S(1)}, u32[]{:S(2)}, u32[]{:S(2)}) collective-permute-start(bf16[320,128]{1,0:T(8,128)(2,1)S(1)} %get-tuple-element.377), channel_id=1, source_target_pairs={{0,3},{1,2},{2,1},{3,0},{4,7},{5,6},{6,5},{7,4},{8,11},{9,10},{10,... | collective-permute-start | bytes 245768 | tf_op jit(solution)/shard_map/ppermute | solution.py:853
  285.4 21.1 %collective-permute-start.81 = (bf16[576,128]{1,0:T(8,128)(2,1)S(1)}, bf16[576,128]{1,0:T(8,128)(2,1)S(1)}, u32[]{:S(2)}, u32[]{:S(2)}) collective-permute-start(bf16[576,128]{1,0:T(8,128)(2,1)S(1)} %get-tuple-element.385), channel_id=1, source_target_pairs={{0,1},{1,0},{2,3},{3,2},{4,5},{5,4},{6,7},{7,6},{8,9},{9,8},{10,11... | collective-permute-start | bytes 442376 | tf_op jit(solution)/shard_map/ppermute | solution.py:853
  285.9 20.5 %collective-permute-start.82 = (bf16[576,128]{1,0:T(8,128)(2,1)S(1)}, bf16[576,128]{1,0:T(8,128)(2,1)S(1)}, u32[]{:S(2)}, u32[]{:S(2)}) collective-permute-start(bf16[576,128]{1,0:T(8,128)(2,1)S(1)} %get-tuple-element.386), channel_id=1, source_target_pairs={{0,2},{1,3},{2,0},{3,1},{4,6},{5,7},{6,4},{7,5},{8,10},{9,11},{10,... | collective-permute-start | bytes 442376 | tf_op jit(solution)/shard_map/ppermute | solution.py:853
  288.0 18.5 %collective-permute-start.83 = (bf16[576,128]{1,0:T(8,128)(2,1)S(1)}, bf16[576,128]{1,0:T(8,128)(2,1)S(1)}, u32[]{:S(2)}, u32[]{:S(2)}) collective-permute-start(bf16[576,128]{1,0:T(8,128)(2,1)S(1)} %get-tuple-element.387), channel_id=1, source_target_pairs={{0,3},{1,2},{2,1},{3,0},{4,7},{5,6},{6,5},{7,4},{8,11},{9,10},{10,... | collective-permute-start | bytes 442376 | tf_op jit(solution)/shard_map/ppermute | solution.py:853
  291.2 9.8 %collective-permute-start.87 = (bf16[16,128]{1,0:T(8,128)(2,1)S(1)}, bf16[16,128]{1,0:T(8,128)(2,1)S(1)}, u32[]{:S(2)}, u32[]{:S(2)}) collective-permute-start(bf16[16,128]{1,0:T(8,128)(2,1)S(1)} %get-tuple-element.392), channel_id=1, source_target_pairs={{0,1},{1,0},{2,3},{3,2},{4,5},{5,4},{6,7},{7,6},{8,9},{9,8},{10,11... | collective-permute-start | bytes 12296 | tf_op jit(solution)/shard_map/ppermute | solution.py:853
  (81 other events, 659.5 us)
where the time goes:
time: 314 us; the launch traced here: 308 us
  Pallas kernels  126 us (40%)
  waiting for transfers between devices  87.1 us (28%)
  starting transfers between devices  85.1 us (27%)
  local copies, waits for them, and re-layouts  5.84 us (2%)
    pallas_call x53, Pallas kernels, call(): pl.pallas_call(inner, name=name, out_shape=[pltpu.HBM(o.shape, o.dtype) i...  126 us
    ppermute x90, waiting for transfers between devices, swap(): return lax.ppermute(value, axis, [(i, i ^ bits) for i in range(size)])  87.1 us
    ppermute x90, starting transfers between devices, swap(): return lax.ppermute(value, axis, [(i, i ^ bits) for i in range(size)])  85.1 us
  transfers between devices with their start and end apart: 90, of which 27 were waited for; matrix products, arithmetic and copies ran while one was open for 0% of the time, Pallas kernels for 34%

commit v1 on v0

--- a/solution.py
+++ b/solution.py
@@ -21,6 +21,7 @@
     "first_back": 6,
     "weight_grad": 8,
     "relay": 1,
+    "sum": 2,
     "stack": 2,
     "add": 2,
     "pack": 2,
@@ -35,6 +36,7 @@
     "first_back": 4,
     "weight_grad": 8,
     "relay": 1,
+    "sum": 0.1,
     "stack": 0.1,
     "add": 1,
     "pack": 10,
@@ -539,7 +541,6 @@
     o_refs, refs = [refs[0], refs[1], refs[2].at[0], refs[2].at[1]], refs[3:]
     o_scr, d_scr, u_scr, d_sem, u_sem = refs
     w_d = wd.open(d_refs, me_ref, d_scr, d_sem, chunks)
-    w_u = wu.open(u_refs, me_ref, u_scr, u_sem, chunks)
     ff = slope_ref.shape[1]
     model = g_ref.shape[1]
     ff_m = ff // mp_size
@@ -558,6 +559,7 @@
     for m in every:
         dcomb_ref[:, m * stride : m * stride + LANE] = d_z2[:, m * LANE : (m + 1) * LANE]
     w_d.wait()
+    w_u = wu.open(u_refs, me_ref, u_scr, u_sem, chunks)
     need(slope_ref)
     for m in every:
         for b in range(0, ff_blocks, 2):
@@ -867,11 +869,11 @@
     lax.fori_loop(0, size, step, 0)
 
 
-def add(left, right, count):
+def add(left, right, count, name="add"):
     shape = (left.shape[0] // count,) + left.shape[1:]
     return call(
         functools.partial(add_body, count),
-        "add",
+        name,
         [sds(shape, BF16)] * count,
         [left, right],
     )
@@ -893,13 +895,13 @@
             out[at:, :] = sums_ref[:, pl.ds(col(tile * LANE), LANE)].astype(BF16)
 
 
-def join(me, pairs, sums=None):
+def join(me, pairs, sums=None, name="add"):
     width = 4
     rows = sum(p[0].shape[1] for p in pairs) + (0 if sums is None else sums.shape[0])
     flat = [a for pair in pairs for a in pair]
     return call(
         functools.partial(join_body, len(pairs), sums is not None),
-        "add",
+        name,
         [sds((rows, LANE), BF16)] * width,
         [me] + flat + ([] if sums is None else [sums]),
         smem=1,
@@ -913,8 +915,8 @@
     refs[-1][...] = value
 
 
-def total(parts):
-    return call(total_body, "add", [sds(parts[0].shape, F32)], parts)[0]
+def total(parts, name="add"):
+    return call(total_body, name, [sds(parts[0].shape, F32)], parts)[0]
 
 
 def stack_body(cuts, *refs):
@@ -960,23 +962,30 @@
     call(relay_body, name, [], [], after=arrays)
 
 
-def pack_q_body(per, me_ref, qkv_ref, par_ref, out_ref):
+def pack_q_body(me_ref, qkv_ref, gains_ref, biases_ref, out_ref, scr):
+    per = qkv_ref.shape[2]
     for c in range(3):
-        out_ref[c * per : (c + 1) * per, :] = qkv_ref[c]
-    rows = jnp.concatenate([par_ref[...].astype(F32)] * (LANE // per), axis=1)
-    share = lax.broadcasted_iota(jnp.int32, rows.shape, 1) // per
-    mine = jnp.where(share == me_ref[1] % (LANE // per), rows, 0.0)
+        out_ref[c * per : (c + 1) * per, :] = qkv_ref[0, c]
+    scr[...] = jnp.zeros_like(scr)
+    for l in range(gains_ref.shape[0]):
+        for first, ref in ((0, gains_ref), (2, biases_ref)):
+            rows = slice(8 * l + first, 8 * l + first + ref.shape[1])
+            for lane in range(0, LANE, per):
+                scr[rows, lane : lane + per] = ref[l].astype(F32)
+    share = lax.broadcasted_iota(jnp.int32, scr.shape, 1) // per
+    mine = jnp.where(share == me_ref[1] % (LANE // per), scr[...], 0.0)
     out_ref[3 * per :, :] = mine.astype(BF16)
 
 
-def pack_q(me, qkv, params):
-    per = qkv.shape[1]
+def pack_q(me, qkv, gains, biases):
+    per, rows = qkv.shape[2], 8 * gains.shape[0]
     return call(
-        functools.partial(pack_q_body, per),
+        pack_q_body,
         "pack",
-        [sds((3 * per + params.shape[0], LANE), BF16)],
-        [me, qkv, params],
+        [sds((3 * per + rows, LANE), BF16)],
+        [me, qkv, gains, biases],
         smem=1,
+        scratch=[pltpu.VMEM((rows, LANE), F32)],
     )[0]
 
 
@@ -1113,10 +1122,10 @@
             return jnp.swapaxes(matrix.reshape(per, -1, LANE), 0, 1).reshape(-1, LANE)
 
         qkv_t, out_t, down_t = (jnp.swapaxes(w, 1, 2) for w in (w_qkv, w_out, w_down))
-        params = jnp.concatenate([norm_gains, biases], axis=1)
-        params = jnp.pad(params, ((0, 0), (0, 2), (0, 0))).reshape(layers * 8, per)
 
         def param_block():
+            params = jnp.concatenate([norm_gains, biases], axis=1)
+            params = jnp.pad(params, ((0, 0), (0, 2), (0, 0))).reshape(layers * 8, per)
             rows = jnp.concatenate([params] * (LANE // per), axis=1)
             share = lax.broadcasted_iota(jnp.int32, rows.shape, 1) // per
             return jnp.where(share == me_d % (LANE // per), rows, 0)
@@ -1159,7 +1168,7 @@
         weights = [None] * layers
         if direct:
             mats = (qkv_t, w_gate, out_t, w_up, down_t)
-            q_steps = send_width(pack_q(me, qkv_t[0], params))
+            q_steps = send_width(pack_q(me, qkv_t, norm_gains, biases))
             t_all = spread(tokens)
             w_steps = send_width(pack(0, False, *mats))
             relay([], "pack")
@@ -1263,16 +1272,16 @@
 
         def reduce_3(name, mp_first=False):
             if name in moving:
-                keep, send = add(*moving[name], 2)
+                keep, send = add(*moving[name], 2, "sum" if mp_first or name == ("d", 0) else "add")
                 moving[name] = (keep, dp_swap(send) if mp_first else mp_swap(send, 2))
 
         def reduce_4(names, sums=None):
             if direct:
                 pairs = [moving.pop(name) for name in names]
-                moving[names[0]] = swap_width(join(me, pairs, sums))
+                moving[names[0]] = swap_width(join(me, pairs, sums, "sum" if names[0][1] == 0 else "add"))
 
         def reduce_5(name):
-            return total(moving.pop(name)) if direct else None
+            return total(moving.pop(name), "sum" if name[1] == 0 else "add") if direct else None
 
         for l in reversed(range(layers)):
             wq, wd, wu = weights[l]

time: 314 us -> 306 us (0.975)
  starting transfers between devices: 85.1 us -> 80.8 us
    ppermute x90, starting transfers between devices: 85.1 us -> 80.8 us  [swap(): return lax.ppermute(value, axis, [(i, i ^ bits) for i in range(size)])]
where the time goes in v1:
time: 306 us; the launch traced here: 301 us
  Pallas kernels  125 us (41%)
  waiting for transfers between devices  84.3 us (28%)
  starting transfers between devices  80.8 us (26%)
  local copies, waits for them, and re-layouts  7.28 us (2%)
    pallas_call x53, Pallas kernels, call(): pl.pallas_call(inner, name=name, out_shape=[pltpu.HBM(o.shape, o.dtype) i...  125 us
    ppermute x90, waiting for transfers between devices, swap(): return lax.ppermute(value, axis, [(i, i ^ bits) for i in range(size)])  84.3 us
    ppermute x90, starting transfers between devices, swap(): return lax.ppermute(value, axis, [(i, i ^ bits) for i in range(size)])  80.8 us
  transfers between devices with their start and end apart: 90, of which 27 were waited for; matrix products, arithmetic and copies ran while one was open for 0% of the time, Pallas kernels for 34%

profile of v1, /device:TPU:0, one launch (start us, length us, event | category | flops | bytes accessed | tf_op | source)
XLA Modules:
  0.0 300.6 jit_solution(1744926740288174379)
XLA Ops:
  0.6 1.3 slice.15
  5.6 5.1 %collective-permute-start.4 = (bf16[208,128]{1,0:T(8,128)(2,1)S(1)}, bf16[208,128]{1,0:T(8,128)(2,1)S(1)}, u32[]{:S(2)}, u32[]{:S(2)}) collective-permute-start(bf16[208,128]{1,0:T(8,128)(2,1)S(1)} %get-tuple-element.207.refs_0_), channel_id=1, source_target_pairs={{0,3},{1,2},{2,1},{3,0},{4,7},{5,6},{6,5},{7,4},{8,11},{9,10},{10,... | collective-permute-start | bytes 159752 | tf_op jit(solution)/shard_map/ppermute | solution.py:855
  11.4 3.8 %collective-permute-start.9 = (bf16[704,128]{1,0:T(8,128)(2,1)S(1)}, bf16[704,128]{1,0:T(8,128)(2,1)S(1)}, u32[]{:S(2)}, u32[]{:S(2)}) collective-permute-start(bf16[704,128]{1,0:T(8,128)(2,1)S(1)} %get-tuple-element.213.refs_0_), channel_id=1, source_target_pairs={{0,3},{1,2},{2,1},{3,0},{4,7},{5,6},{6,5},{7,4},{8,11},{9,10},{10,... | collective-permute-start | bytes 540680 | tf_op jit(solution)/shard_map/ppermute | solution.py:855
  15.2 1.5 collective-permute-start.1
  17.7 5.1 %collective-permute-done.3.refs_2_ = bf16[208,128]{1,0:T(8,128)(2,1)S(1)} collective-permute-done((bf16[208,128]{1,0:T(8,128)(2,1)S(1)}, bf16[208,128]{1,0:T(8,128)(2,1)S(1)}, u32[]{:S(2)}, u32[]{:S(2)}) %collective-permute-start.3) | collective-permute-done | bytes 53280 | tf_op jit(solution)/shard_map/ppermute | solution.py:855
  23.0 4.7 %collective-permute-done.1.refs_0_.refs_5_ = bf16[2,256,512]{2,1,0:T(8,128)(2,1)S(1)} collective-permute-done((bf16[2,256,512]{2,1,0:T(8,128)(2,1)S(1)}, bf16[2,256,512]{2,1,0:T(8,128)(2,1)S(1)}, u32[]{:S(2)}, u32[]{:S(2)}) %collective-permute-start.1) | collective-permute-done | bytes 524320 | tf_op jit(solution)/shard_map/ppermute | solution.py:855
  27.8 1.5 collective-permute-start.6
  29.4 1.6 collective-permute-done.8.refs_2_
  32.2 1.5 collective-permute-start.20
  33.7 2.9 collective-permute-start.18
  36.7 1.4 collective-permute-start.14
  38.1 1.5 collective-permute-start.13
  39.6 14.1 %attend.2 = (bf16[2,1024,384]{2,1,0:T(8,128)(2,1)}, f32[4,1,1024]{2,1,0:T(1,128)}, bf16[2,256,128]{2,1,0:T(8,128)(2,1)S(1)}, bf16[2,256,128]{2,1,0:T(8,128)(2,1)...) custom-call(s32[4]{0:T(128)S(1)} %copy-done.7, ...), custom_call_target="tpu_custom_call" | custom-call | flops 44000002048 | bytes 144000000 | tf_op jit(solution)/shard_map/attend/pallas_call | solution.py:173
  54.6 1.4 collective-permute-start.11
  57.4 8.6 %collective-permute-done.11.refs_0_.refs_7_ = bf16[2,2,256,128]{3,2,1,0:T(8,128)(2,1)S(1)} collective-permute-done((bf16[2,2,256,128]{3,2,1,0:T(8,128)(2,1)S(1)}, bf16[2,2,256,128]{3,2,1,0:T(8,128)(2,1)S(1)}, u32[]{:S(2)}, u32[]{:S(2)}) %collective-permute-start.11) | collective-permute-done | bytes 262176 | tf_op jit(solution)/shard_map/ppermute | solution.py:855
  68.3 2.3 collective-permute-done.12.refs_8_
  71.3 1.7 collective-permute-start.32
  74.1 10.7 %second.2 = (bf16[512,512]{1,0:T(8,128)(2,1)}, f32[512,512]{1,0:T(8,128)}, f32[512,512]{1,0:T(8,128)}, bf16[512,512]{1,0:T(8,128)(2,1)}, f32[512,512]{1,0:T(8,12...) custom-call(s32[4]{0:T(128)S(1)} %copy-done.7, ...), custom_call_target="tpu_custom_call" | custom-call | flops 65999998976 | bytes 216000000 | tf_op jit(solution)/shard_map/second/pallas_call | solution.py:173
  85.2 1.7 collective-permute-start.28
  87.4 5.6 %collective-permute-done.31.refs_2_.refs_12_.refs_14_.refs_15_ = bf16[4,192,128]{2,1,0:T(8,128)(2,1)S(1)} collective-permute-done((bf16[4,192,128]{2,1,0:T(8,128)(2,1)S(1)}, bf16[4,192,128]{2,1,0:T(8,128)(2,1)S(1)}, u32[]{:S(2)}, u32[]{:S(2)}) %collective-permute-start.31) | collective-permute-done | bytes 196640 | tf_op jit(solution)/shard_map/ppermute | solution.py:855
  93.0 2.9 collective-permute-done.27.refs_3_.refs_7_.refs_11_
  96.0 4.5 %collective-permute-done.28.refs_4_.refs_8_.refs_11_ = bf16[256,512]{1,0:T(8,128)(2,1)S(1)} collective-permute-done((bf16[256,512]{1,0:T(8,128)(2,1)S(1)}, bf16[256,512]{1,0:T(8,128)(2,1)S(1)}, u32[]{:S(2)}, u32[]{:S(2)}) %collective-permute-start.28) | collective-permute-done | bytes 262176 | tf_op jit(solution)/shard_map/ppermute | solution.py:855
  101.1 1.7 collective-permute-start.41
  104.1 13.4 %attend.3 = (bf16[2,1024,384]{2,1,0:T(8,128)(2,1)S(1)}, f32[4,1,1024]{2,1,0:T(1,128)S(1)}, bf16[2,256,128]{2,1,0:T(8,128)(2,1)S(1)}, bf16[2,256,128]{2,1,0:T(8,1...) custom-call(s32[4]{0:T(128)S(1)} %copy-done.7, s32[2,1024]{1,0:T(2,128)S(1)} %get-tuple-element.405.refs_1_, ...), custom_call_target="tpu_custom_call" | custom-call | flops 44000002048 | bytes 144000000 | tf_op jit(solution)/shard_map/attend/pallas_call | solution.py:173
  117.5 1.2 collective-permute-start.35
  121.1 5.0 %collective-permute-done.35.refs_7_ = bf16[2,2,256,128]{3,2,1,0:T(8,128)(2,1)S(1)} collective-permute-done((bf16[2,2,256,128]{3,2,1,0:T(8,128)(2,1)}, bf16[2,2,256,128]{3,2,1,0:T(8,128)(2,1)S(1)}, u32[]{:S(2)}, u32[]{:S(2)}) %collective-permute-start.35) | collective-permute-done | bytes 262176 | tf_op jit(solution)/shard_map/ppermute | solution.py:855
  126.2 1.4 collective-permute-done.36.refs_8_
  128.4 10.8 %second.3 = (bf16[512,512]{1,0:T(8,128)(2,1)}, f32[512,512]{1,0:T(8,128)}, f32[512,512]{1,0:T(8,128)}, bf16[512,512]{1,0:T(8,128)(2,1)}, f32[512,512]{1,0:T(8,12...) custom-call(s32[4]{0:T(128)S(1)} %copy-done.7, ...), custom_call_target="tpu_custom_call" | custom-call | flops 65999998976 | bytes 216000000 | tf_op jit(solution)/shard_map/second/pallas_call | solution.py:173
  139.1 8.3 %second_back.2 = (bf16[512,512]{1,0:T(8,128)(2,1)S(1)}, bf16[512,2560]{1,0:T(8,128)(2,1)S(1)}, f32[512,512]{1,0:T(8,128)S(1)}, bf16[512,512]{1,0:T(8,128)(2,1)S(...) custom-call(s32[4]{0:T(128)S(1)} %copy-done.7, ...), custom_call_target="tpu_custom_call" | custom-call | flops 54999998464 | bytes 180000000 | tf_op jit(solution)/shard_map/second_back/pallas_call | solution.py:173
  148.9 7.3 %weight_grad.2 = (bf16[16,320,128]{2,1,0:T(8,128)(2,1)S(1)}, bf16[16,320,128]{2,1,0:T(8,128)(2,1)S(1)}, bf16[16,384,128]{2,1,0:T(8,128)(2,1)S(1)}, bf16[16,384,1...) custom-call(s32[4]{0:T(128)S(1)} %copy-done.7, ...), custom_call_target="tpu_custom_call" | custom-call | flops 44000002048 | bytes 144000000 | tf_op jit(solution)/shard_map/weight_grad/pallas_call | solution.py:173
  156.9 5.0 %collective-permute-done.46.refs_8_ = bf16[2,2,256,128]{3,2,1,0:T(8,128)(2,1)S(1)} collective-permute-done((bf16[2,2,256,128]{3,2,1,0:T(8,128)(2,1)S(1)}, bf16[2,2,256,128]{3,2,1,0:T(8,128)(2,1)S(1)}, u32[]{:S(2)}, u32[]{:S(2)}) %collective-permute-start.46) | collective-permute-done | bytes 262176 | tf_op jit(solution)/shard_map/ppermute | solution.py:855
  162.0 5.1 %attend_back.4 = (bf16[2,256,512]{2,1,0:T(8,128)(2,1)S(1)}, bf16[2,256,512]{2,1,0:T(8,128)(2,1)S(1)}, f32[512,384]{1,0:T(8,128)S(1)}, f32[8,128]{1,0:T(8,128)S(1)}) custom-call(s32[4]{0:T(128)S(1)} %copy-done.7, s32[2,1024]{1,0:T(2,128)S(1)} %copy-done.4, f32[2,1,1024]{2,1,0:T(1,128)S(1)} %copy-done.1, bf16[2,1024,384]{2,1,0:T(8,128)(2,1)S(1)} %copy-done.41, ...), custom_call_target="tpu_custom_call" | custom-call | flops 49500000256 | bytes 162000000 | tf_op jit(solution)/shard_map/attend_back/pallas_call | solution.py:173
  169.3 9.6 %attend_back.5 = (bf16[2,256,512]{2,1,0:T(8,128)(2,1)S(1)}, bf16[2,256,512]{2,1,0:T(8,128)(2,1)S(1)}, bf16[8,192,128]{2,1,0:T(8,128)(2,1)S(1)}, f32[8,128]{1,0:T(8,128)S(1)}) custom-call(s32[4]{0:T(128)S(1)} %copy-done.7, s32[2,1024]{1,0:T(2,128)S(1)} %copy-done.4, f32[2,1,1024]{2,1,0:T(1,128)S(1)} %copy-done.1, bf16[2,1024,384]{2,1,0:T(8,128)(2,1)S(1)} %copy-done.41, ...), custom_call_target="tpu_custom_call" | custom-call | flops 49500000256 | bytes 162000000 | tf_op jit(solution)/shard_map/attend_back/pallas_call | solution.py:173
  179.1 1.2 collective-permute-start.52
  180.3 4.8 %collective-permute-done.51.refs_1_ = bf16[8,320,128]{2,1,0:T(8,128)(2,1)S(1)} collective-permute-done((bf16[8,320,128]{2,1,0:T(8,128)(2,1)S(1)}, bf16[8,320,128]{2,1,0:T(8,128)(2,1)S(1)}, u32[]{:S(2)}, u32[]{:S(2)}) %collective-permute-start.51) | collective-permute-done | bytes 655392 | tf_op jit(solution)/shard_map/ppermute | solution.py:855
  186.6 1.6 collective-permute-start.55
  189.9 5.1 %collective-permute-done.53 = bf16[1,256,512]{2,1,0:T(8,128)(2,1)S(1)} collective-permute-done((bf16[1,256,512]{2,1,0:T(8,128)(2,1)S(1)}, bf16[1,256,512]{2,1,0:T(8,128)(2,1)S(1)}, u32[]{:S(2)}, u32[]{:S(2)}) %collective-permute-start.53) | collective-permute-done | bytes 262176 | tf_op jit(solution)/shard_map/ppermute | solution.py:855
  194.9 2.6 first_back.2
  197.5 8.3 %second_back.3 = (bf16[512,512]{1,0:T(8,128)(2,1)S(1)}, bf16[512,2560]{1,0:T(8,128)(2,1)S(1)}, f32[512,512]{1,0:T(8,128)S(1)}, bf16[512,512]{1,0:T(8,128)(2,1)S(...) custom-call(s32[4]{0:T(128)S(1)} %copy-done.7, ...), custom_call_target="tpu_custom_call" | custom-call | flops 54999998464 | bytes 180000000 | tf_op jit(solution)/shard_map/second_back/pallas_call | solution.py:173
  208.4 2.6 collective-permute-start.62
  211.3 1.3 collective-permute-start.66
  212.5 7.2 %weight_grad.3 = (bf16[16,320,128]{2,1,0:T(8,128)(2,1)S(1)}, bf16[16,320,128]{2,1,0:T(8,128)(2,1)S(1)}, bf16[16,384,128]{2,1,0:T(8,128)(2,1)S(1)}, bf16[16,384,1...) custom-call(s32[4]{0:T(128)S(1)} %copy-done.7, ...), custom_call_target="tpu_custom_call" | custom-call | flops 44000002048 | bytes 144000000 | tf_op jit(solution)/shard_map/weight_grad/pallas_call | solution.py:173
  221.5 5.6 %attend_back.6 = (bf16[2,256,512]{2,1,0:T(8,128)(2,1)S(1)}, bf16[2,256,512]{2,1,0:T(8,128)(2,1)S(1)}, f32[512,384]{1,0:T(8,128)S(1)}, f32[8,128]{1,0:T(8,128)S(1)}) custom-call(s32[4]{0:T(128)S(1)} %copy-done.7, s32[2,1024]{1,0:T(2,128)S(1)} %copy-done.5, f32[2,1,1024]{2,1,0:T(1,128)S(1)} %copy-done.2, bf16[2,1024,384]{2,1,0:T(8,128)(2,1)S(1)} %copy-done.39, ...), custom_call_target="tpu_custom_call" | custom-call | flops 49500000256 | bytes 162000000 | tf_op jit(solution)/shard_map/attend_back/pallas_call | solution.py:173
  227.0 1.5 collective-permute-start.63
  231.0 1.4 collective-permute-start.68
  232.5 2.3 collective-permute-done.63.refs_3_
  235.0 9.6 %attend_back.7 = (bf16[2,256,512]{2,1,0:T(8,128)(2,1)S(1)}, bf16[2,256,512]{2,1,0:T(8,128)(2,1)S(1)}, bf16[8,192,128]{2,1,0:T(8,128)(2,1)S(1)}, f32[8,128]{1,0:T(8,128)S(1)}) custom-call(s32[4]{0:T(128)S(1)} %copy-done.7, s32[2,1024]{1,0:T(2,128)S(1)} %copy-done.5, f32[2,1,1024]{2,1,0:T(1,128)S(1)} %copy-done.2, bf16[2,1024,384]{2,1,0:T(8,128)(2,1)S(1)} %copy-done.39, ...), custom_call_target="tpu_custom_call" | custom-call | flops 49500000256 | bytes 162000000 | tf_op jit(solution)/shard_map/attend_back/pallas_call | solution.py:173
  244.7 2.2 collective-permute-start.73
  247.3 2.4 collective-permute-start.75
  252.0 1.6 collective-permute-start.79
  254.3 3.1 %collective-permute-done.74.refs_2_ = bf16[384,128]{1,0:T(8,128)(2,1)S(1)} collective-permute-done((bf16[384,128]{1,0:T(8,128)(2,1)S(1)}, bf16[384,128]{1,0:T(8,128)(2,1)S(1)}, u32[]{:S(2)}, u32[]{:S(2)}) %collective-permute-start.74) | collective-permute-done | bytes 98336 | tf_op jit(solution)/shard_map/ppermute | solution.py:855
  259.5 5.5 %collective-permute-done.72.refs_2_ = bf16[4,320,128]{2,1,0:T(8,128)(2,1)S(1)} collective-permute-done((bf16[4,320,128]{2,1,0:T(8,128)(2,1)S(1)}, bf16[4,320,128]{2,1,0:T(8,128)(2,1)S(1)}, u32[]{:S(2)}, u32[]{:S(2)}) %collective-permute-start.72) | collective-permute-done | bytes 327712 | tf_op jit(solution)/shard_map/ppermute | solution.py:855
  266.7 3.3 %first_back.3 = (f32[512,512]{1,0:T(8,128)}, f32[8,512]{1,0:T(8,128)S(1)}, f32[8,128]{1,0:T(8,128)S(1)}) custom-call(s32[4]{0:T(128)S(1)} %copy-done.7, bf16[512,512]{1,0:T(8,128)(2,1)} %bitcast.25, f32[512,512]{1,0:T(8,128)S(1)} %get-tuple-element.300.refs_2_, f32[512,512]{1,0:T(8,128)S(1)} %get-tuple-element.315.refs_3_, f32[2,8,512]{2,1,0:T(8,128)S(1)} %copy-done.43, ...), custom_call_target="tpu_custom_call" | custom-call | flops 22000001024 | bytes 72000000 | tf_op jit(solution)/shard_map/first_back/pallas_call | solution.py:173
  272.1 3.1 %collective-permute-done.85 = f32[16,512]{1,0:T(8,128)S(1)} collective-permute-done((f32[16,512]{1,0:T(8,128)S(1)}, f32[16,512]{1,0:T(8,128)S(1)}, u32[]{:S(2)}, u32[]{:S(2)}) %collective-permute-start.85) | collective-permute-done | bytes 32800 | tf_op jit(solution)/shard_map/ppermute | solution.py:855
  275.2 1.5 collective-permute-start.86
  276.7 2.2 collective-permute-start.77
  279.2 2.0 collective-permute-start.78
  281.9 2.4 collective-permute-start.82
  284.3 2.0 collective-permute-start.83
  287.0 3.0 %collective-permute-start.87 = (bf16[16,128]{1,0:T(8,128)(2,1)S(1)}, bf16[16,128]{1,0:T(8,128)(2,1)S(1)}, u32[]{:S(2)}, u32[]{:S(2)}) collective-permute-start(bf16[16,128]{1,0:T(8,128)(2,1)S(1)} %get-tuple-element.392), channel_id=1, source_target_pairs={{0,1},{1,0},{2,3},{3,2},{4,5},{5,4},{6,7},{7,6},{8,9},{9,8},{10,11... | collective-permute-start | bytes 12296 | tf_op jit(solution)/shard_map/ppermute | solution.py:855
  290.3 1.4 collective-permute-done.87.refs_9_
  291.7 1.8 collective-permute-start.89
  293.5 5.4 %collective-permute-done.88.refs_10_ = bf16[16,128]{1,0:T(8,128)(2,1)S(1)} collective-permute-done((bf16[16,128]{1,0:T(8,128)(2,1)S(1)}, bf16[16,128]{1,0:T(8,128)(2,1)S(1)}, u32[]{:S(2)}, u32[]{:S(2)}) %collective-permute-start.88) | collective-permute-done | bytes 4128 | tf_op jit(solution)/shard_map/ppermute | solution.py:855
  299.0 1.5 finish.1
  (299 shorter events, 44.3 us)
Async XLA Ops:
  5.6 12.1 %collective-permute-start.4 = (bf16[208,128]{1,0:T(8,128)(2,1)S(1)}, bf16[208,128]{1,0:T(8,128)(2,1)S(1)}, u32[]{:S(2)}, u32[]{:S(2)}) collective-permute-start(bf16[208,128]{1,0:T(8,128)(2,1)S(1)} %get-tuple-element.207.refs_0_), channel_id=1, source_target_pairs={{0,3},{1,2},{2,1},{3,0},{4,7},{5,6},{6,5},{7,4},{8,11},{9,10},{10,... | collective-permute-start | bytes 159752 | tf_op jit(solution)/shard_map/ppermute | solution.py:855
  10.7 12.2 %collective-permute-start.3 = (bf16[208,128]{1,0:T(8,128)(2,1)S(1)}, bf16[208,128]{1,0:T(8,128)(2,1)S(1)}, u32[]{:S(2)}, u32[]{:S(2)}) collective-permute-start(bf16[208,128]{1,0:T(8,128)(2,1)S(1)} %get-tuple-element.207.refs_0_), channel_id=1, source_target_pairs={{0,2},{1,3},{2,0},{3,1},{4,6},{5,7},{6,4},{7,5},{8,10},{9,11},{10,... | collective-permute-start | bytes 159752 | tf_op jit(solution)/shard_map/ppermute | solution.py:855
  10.7 12.2 %collective-permute-start.2 = (bf16[208,128]{1,0:T(8,128)(2,1)S(1)}, bf16[208,128]{1,0:T(8,128)(2,1)S(1)}, u32[]{:S(2)}, u32[]{:S(2)}) collective-permute-start(bf16[208,128]{1,0:T(8,128)(2,1)S(1)} %get-tuple-element.207.refs_0_), channel_id=1, source_target_pairs={{0,1},{1,0},{2,3},{3,2},{4,5},{5,4},{6,7},{7,6},{8,9},{9,8},{10,11... | collective-permute-start | bytes 159752 | tf_op jit(solution)/shard_map/ppermute | solution.py:855
  11.4 17.9 %collective-permute-start.9 = (bf16[704,128]{1,0:T(8,128)(2,1)S(1)}, bf16[704,128]{1,0:T(8,128)(2,1)S(1)}, u32[]{:S(2)}, u32[]{:S(2)}) collective-permute-start(bf16[704,128]{1,0:T(8,128)(2,1)S(1)} %get-tuple-element.213.refs_0_), channel_id=1, source_target_pairs={{0,3},{1,2},{2,1},{3,0},{4,7},{5,6},{6,5},{7,4},{8,11},{9,10},{10,... | collective-permute-start | bytes 540680 | tf_op jit(solution)/shard_map/ppermute | solution.py:855
  15.2 12.5 %collective-permute-start.1 = (bf16[2,256,512]{2,1,0:T(8,128)(2,1)S(1)}, bf16[2,256,512]{2,1,0:T(8,128)(2,1)S(1)}, u32[]{:S(2)}, u32[]{:S(2)}) collective-permute-start(bf16[2,256,512]{2,1,0:T(8,128)(2,1)S(1)} %copy-done.14), channel_id=1, source_target_pairs={{0,8},{4,12},{8,0},{12,4},{1,9},{5,13},{9,1},{13,5},{2,10},{6,14},... | collective-permute-start | bytes 1572872 | tf_op jit(solution)/shard_map/ppermute | solution.py:855
  17.6 13.4 %collective-permute-start.8 = (bf16[704,128]{1,0:T(8,128)(2,1)S(1)}, bf16[704,128]{1,0:T(8,128)(2,1)S(1)}, u32[]{:S(2)}, u32[]{:S(2)}) collective-permute-start(bf16[704,128]{1,0:T(8,128)(2,1)S(1)} %get-tuple-element.213.refs_0_), channel_id=1, source_target_pairs={{0,2},{1,3},{2,0},{3,1},{4,6},{5,7},{6,4},{7,5},{8,10},{9,11},{10,... | collective-permute-start | bytes 540680 | tf_op jit(solution)/shard_map/ppermute | solution.py:855
  22.9 9.2 %collective-permute-start.7 = (bf16[704,128]{1,0:T(8,128)(2,1)S(1)}, bf16[704,128]{1,0:T(8,128)(2,1)S(1)}, u32[]{:S(2)}, u32[]{:S(2)}) collective-permute-start(bf16[704,128]{1,0:T(8,128)(2,1)S(1)} %get-tuple-element.213.refs_0_), channel_id=1, source_target_pairs={{0,1},{1,0},{2,3},{3,2},{4,5},{5,4},{6,7},{7,6},{8,9},{9,8},{10,11... | collective-permute-start | bytes 540680 | tf_op jit(solution)/shard_map/ppermute | solution.py:855
  22.9 13.7 %collective-permute-start = (bf16[2,256,512]{2,1,0:T(8,128)(2,1)S(1)}, bf16[2,256,512]{2,1,0:T(8,128)(2,1)S(1)}, u32[]{:S(2)}, u32[]{:S(2)}) collective-permute-start(bf16[2,256,512]{2,1,0:T(8,128)(2,1)S(1)} %copy-done.14), channel_id=1, source_target_pairs={{0,4},{4,0},{8,12},{12,8},{1,5},{5,1},{9,13},{13,9},{2,6},{6,2},{1... | collective-permute-start | bytes 1572872 | tf_op jit(solution)/shard_map/ppermute | solution.py:855
  29.3 8.8 %collective-permute-start.5 = (bf16[2,256,512]{2,1,0:T(8,128)(2,1)S(1)}, bf16[2,256,512]{2,1,0:T(8,128)(2,1)S(1)}, u32[]{:S(2)}, u32[]{:S(2)}) collective-permute-start(bf16[2,256,512]{2,1,0:T(8,128)(2,1)S(1)} %get-tuple-element.211), channel_id=1, source_target_pairs={{0,4},{4,0},{8,12},{12,8},{1,5},{5,1},{9,13},{13,9},{2,6},{6,2},{1... | collective-permute-start | bytes 1572872 | tf_op jit(solution)/shard_map/ppermute | solution.py:855
  32.2 21.6 %collective-permute-start.20 = (bf16[896,128]{1,0:T(8,128)(2,1)S(1)}, bf16[896,128]{1,0:T(8,128)(2,1)S(1)}, u32[]{:S(2)}, u32[]{:S(2)}) collective-permute-start(bf16[896,128]{1,0:T(8,128)(2,1)S(1)} %get-tuple-element.224.refs_0_), channel_id=1, source_target_pairs={{0,3},{1,2},{2,1},{3,0},{4,7},{5,6},{6,5},{7,4},{8,11},{9,10},{10,... | collective-permute-start | bytes 688136 | tf_op jit(solution)/shard_map/ppermute | solution.py:855
  33.7 20.0 %collective-permute-start.19 = (bf16[896,128]{1,0:T(8,128)(2,1)S(1)}, bf16[896,128]{1,0:T(8,128)(2,1)S(1)}, u32[]{:S(2)}, u32[]{:S(2)}) collective-permute-start(bf16[896,128]{1,0:T(8,128)(2,1)S(1)} %get-tuple-element.224.refs_0_), channel_id=1, source_target_pairs={{0,2},{1,3},{2,0},{3,1},{4,6},{5,7},{6,4},{7,5},{8,10},{9,11},{10,... | collective-permute-start | bytes 688136 | tf_op jit(solution)/shard_map/ppermute | solution.py:855
  33.7 20.0 %collective-permute-start.18 = (bf16[896,128]{1,0:T(8,128)(2,1)S(1)}, bf16[896,128]{1,0:T(8,128)(2,1)S(1)}, u32[]{:S(2)}, u32[]{:S(2)}) collective-permute-start(bf16[896,128]{1,0:T(8,128)(2,1)S(1)} %get-tuple-element.224.refs_0_), channel_id=1, source_target_pairs={{0,1},{1,0},{2,3},{3,2},{4,5},{5,4},{6,7},{7,6},{8,9},{9,8},{10,11... | collective-permute-start | bytes 688136 | tf_op jit(solution)/shard_map/ppermute | solution.py:855
  36.7 17.1 %collective-permute-start.14 = (bf16[4,704,128]{2,1,0:T(8,128)(2,1)S(1)}, bf16[4,704,128]{2,1,0:T(8,128)(2,1)S(1)}, u32[]{:S(2)}, u32[]{:S(2)}) collective-permute-start(bf16[4,704,128]{2,1,0:T(8,128)(2,1)S(1)} %get-tuple-element.223.refs_9_.refs_7_.refs_10_), channel_id=1, source_target_pairs={{0,8},{4,12},{8,0},{12,4},{1,9},{5,13},{9,1},{13,5},{2,10},{6,14},... | collective-permute-start | bytes 2162696 | tf_op jit(solution)/shard_map/ppermute | solution.py:855
  38.1 15.7 %collective-permute-start.13 = (bf16[4,704,128]{2,1,0:T(8,128)(2,1)S(1)}, bf16[4,704,128]{2,1,0:T(8,128)(2,1)S(1)}, u32[]{:S(2)}, u32[]{:S(2)}) collective-permute-start(bf16[4,704,128]{2,1,0:T(8,128)(2,1)S(1)} %get-tuple-element.223.refs_9_.refs_7_.refs_10_), channel_id=1, source_target_pairs={{0,16},{16,0},{1,17},{17,1},{2,18},{18,2},{3,19},{19,3},{4,20},{20... | collective-permute-start | bytes 2162696 | tf_op jit(solution)/shard_map/ppermute | solution.py:855
  53.9 12.1 %collective-permute-start.22 = (bf16[4,320,128]{2,1,0:T(8,128)(2,1)S(1)}, bf16[4,320,128]{2,1,0:T(8,128)(2,1)S(1)}, u32[]{:S(2)}, u32[]{:S(2)}) collective-permute-start(bf16[4,320,128]{2,1,0:T(8,128)(2,1)S(1)} %get-tuple-element.227), channel_id=1, source_target_pairs={{0,8},{4,12},{8,0},{12,4},{1,9},{5,13},{9,1},{13,5},{2,10},{6,14},... | collective-permute-start | bytes 983048 | tf_op jit(solution)/shard_map/ppermute | solution.py:855
  54.6 11.4 %collective-permute-start.11 = (bf16[2,2,256,128]{3,2,1,0:T(8,128)(2,1)S(1)}, bf16[2,2,256,128]{3,2,1,0:T(8,128)(2,1)S(1)}, u32[]{:S(2)}, u32[]{:S(2)}) collective-permute-start(bf16[2,2,256,128]{3,2,1,0:T(8,128)(2,1)S(1)} %get-tuple-element.222), channel_id=1, source_target_pairs={{0,8},{4,12},{8,0},{12,4},{1,9},{5,13},{9,1},{13,5},{2,10},{6,14},... | collective-permute-start | bytes 786440 | tf_op jit(solution)/shard_map/ppermute | solution.py:855
  56.0 12.2 %collective-permute-start.15 = (bf16[4,704,128]{2,1,0:T(8,128)(2,1)S(1)}, bf16[4,704,128]{2,1,0:T(8,128)(2,1)S(1)}, u32[]{:S(2)}, u32[]{:S(2)}) collective-permute-start(bf16[4,704,128]{2,1,0:T(8,128)(2,1)S(1)} %get-tuple-element.223.refs_9_.refs_7_.refs_10_), channel_id=1, source_target_pairs={{0,4},{4,0},{8,12},{12,8},{1,5},{5,1},{9,13},{13,9},{2,6},{6,2},{1... | collective-permute-start | bytes 2162696 | tf_op jit(solution)/shard_map/ppermute | solution.py:855
  56.0 11.7 %collective-permute-start.10 = (bf16[2,256,128]{2,1,0:T(8,128)(2,1)S(1)}, bf16[2,256,128]{2,1,0:T(8,128)(2,1)S(1)}, u32[]{:S(2)}, u32[]{:S(2)}) collective-permute-start(bf16[2,256,128]{2,1,0:T(8,128)(2,1)S(1)} %get-tuple-element.221), channel_id=1, source_target_pairs={{0,4},{4,0},{8,12},{12,8},{1,5},{5,1},{9,13},{13,9},{2,6},{6,2},{1... | collective-permute-start | bytes 393224 | tf_op jit(solution)/shard_map/ppermute | solution.py:855
  56.5 11.0 %collective-permute-start.21 = (bf16[4,384,128]{2,1,0:T(8,128)(2,1)S(1)}, bf16[4,384,128]{2,1,0:T(8,128)(2,1)S(1)}, u32[]{:S(2)}, u32[]{:S(2)}) collective-permute-start(bf16[4,384,128]{2,1,0:T(8,128)(2,1)S(1)} %get-tuple-element.226), channel_id=1, source_target_pairs={{0,16},{16,0},{1,17},{17,1},{2,18},{18,2},{3,19},{19,3},{4,20},{20... | collective-permute-start | bytes 1179656 | tf_op jit(solution)/shard_map/ppermute | solution.py:855
  70.6 29.8 %collective-permute-start.33 = (bf16[4,704,128]{2,1,0:T(8,128)(2,1)S(1)}, bf16[4,704,128]{2,1,0:T(8,128)(2,1)S(1)}, u32[]{:S(2)}, u32[]{:S(2)}) collective-permute-start(bf16[4,704,128]{2,1,0:T(8,128)(2,1)S(1)} %get-tuple-element.237.refs_9_.refs_7_.refs_10_), channel_id=1, source_target_pairs={{0,16},{16,0},{1,17},{17,1},{2,18},{18,2},{3,19},{19,3},{4,20},{20... | collective-permute-start | bytes 2162696 | tf_op jit(solution)/shard_map/ppermute | solution.py:855
  71.3 29.7 %collective-permute-start.32 = (bf16[4,704,128]{2,1,0:T(8,128)(2,1)S(1)}, bf16[4,704,128]{2,1,0:T(8,128)(2,1)S(1)}, u32[]{:S(2)}, u32[]{:S(2)}) collective-permute-start(bf16[4,704,128]{2,1,0:T(8,128)(2,1)S(1)} %get-tuple-element.237.refs_9_.refs_7_.refs_10_), channel_id=1, source_target_pairs={{0,8},{4,12},{8,0},{12,4},{1,9},{5,13},{9,1},{13,5},{2,10},{6,14},... | collective-permute-start | bytes 2162696 | tf_op jit(solution)/shard_map/ppermute | solution.py:855
  84.8 11.2 %collective-permute-start.27 = (bf16[256,512]{1,0:T(8,128)(2,1)S(1)}, bf16[256,512]{1,0:T(8,128)(2,1)S(1)}, u32[]{:S(2)}, u32[]{:S(2)}) collective-permute-start(bf16[256,512]{1,0:T(8,128)(2,1)S(1)} %get-tuple-element.234.refs_3_.refs_8_.refs_9_), channel_id=1, source_target_pairs={{0,8},{4,12},{8,0},{12,4},{1,9},{5,13},{9,1},{13,5},{2,10},{6,14},... | collective-permute-start | bytes 786440 | tf_op jit(solution)/shard_map/ppermute | solution.py:855
  85.2 15.2 %collective-permute-start.28 = (bf16[256,512]{1,0:T(8,128)(2,1)S(1)}, bf16[256,512]{1,0:T(8,128)(2,1)S(1)}, u32[]{:S(2)}, u32[]{:S(2)}) collective-permute-start(bf16[256,512]{1,0:T(8,128)(2,1)S(1)} %get-tuple-element.235.refs_4_.refs_9_), channel_id=1, source_target_pairs={{0,8},{4,12},{8,0},{12,4},{1,9},{5,13},{9,1},{13,5},{2,10},{6,14},... | collective-permute-start | bytes 786440 | tf_op jit(solution)/shard_map/ppermute | solution.py:855
  93.0 25.9 %collective-permute-start.37 = (bf16[4,704,128]{2,1,0:T(8,128)(2,1)S(1)}, bf16[4,704,128]{2,1,0:T(8,128)(2,1)S(1)}, u32[]{:S(2)}, u32[]{:S(2)}) collective-permute-start(bf16[4,704,128]{2,1,0:T(8,128)(2,1)S(1)} %get-tuple-element.237.refs_9_.refs_7_.refs_10_), channel_id=1, source_target_pairs={{0,4},{4,0},{8,12},{12,8},{1,5},{5,1},{9,13},{13,9},{2,6},{6,2},{1... | collective-permute-start | bytes 2162696 | tf_op jit(solution)/shard_map/ppermute | solution.py:855
  101.1 16.4 %collective-permute-start.41 = (bf16[4,320,128]{2,1,0:T(8,128)(2,1)S(1)}, bf16[4,320,128]{2,1,0:T(8,128)(2,1)S(1)}, u32[]{:S(2)}, u32[]{:S(2)}) collective-permute-start(bf16[4,320,128]{2,1,0:T(8,128)(2,1)S(1)} %get-tuple-element.244), channel_id=1, source_target_pairs={{0,8},{4,12},{8,0},{12,4},{1,9},{5,13},{9,1},{13,5},{2,10},{6,14},... | collective-permute-start | bytes 983048 | tf_op jit(solution)/shard_map/ppermute | solution.py:855
  102.9 15.9 %collective-permute-start.40 = (bf16[4,384,128]{2,1,0:T(8,128)(2,1)S(1)}, bf16[4,384,128]{2,1,0:T(8,128)(2,1)S(1)}, u32[]{:S(2)}, u32[]{:S(2)}) collective-permute-start(bf16[4,384,128]{2,1,0:T(8,128)(2,1)S(1)} %get-tuple-element.243), channel_id=1, source_target_pairs={{0,16},{16,0},{1,17},{17,1},{2,18},{18,2},{3,19},{19,3},{4,20},{20... | collective-permute-start | bytes 1179656 | tf_op jit(solution)/shard_map/ppermute | solution.py:855
  103.4 24.2 %collective-permute-start.38 = (bf16[4,704,128]{2,1,0:T(8,128)(2,1)S(1)}, bf16[4,704,128]{2,1,0:T(8,128)(2,1)}, u32[]{:S(2)}, u32[]{:S(2)}) collective-permute-start(bf16[4,704,128]{2,1,0:T(8,128)(2,1)S(1)} %collective-permute-done.33.refs_0_.refs_1_.refs_10_.refs_8_.refs_11_), channel_id=1, source_target_pairs={{0,4},{4,0},{8,12},{12,8},{1,5},{5,1},{9,13},{13,9},{2,6},{6,2},{1... | collective-permute-start | bytes 2162696 | tf_op jit(solution)/shard_map/ppermute | solution.py:855
  103.5 24.1 %collective-permute-start.39 = (bf16[4,704,128]{2,1,0:T(8,128)(2,1)S(1)}, bf16[4,704,128]{2,1,0:T(8,128)(2,1)}, u32[]{:S(2)}, u32[]{:S(2)}) collective-permute-start(bf16[4,704,128]{2,1,0:T(8,128)(2,1)S(1)} %collective-permute-done.32.refs_1_.refs_0_.refs_11_.refs_9_.refs_12_), channel_id=1, source_target_pairs={{0,4},{4,0},{8,12},{12,8},{1,5},{5,1},{9,13},{13,9},{2,6},{6,2},{1... | collective-permute-start | bytes 2162696 | tf_op jit(solution)/shard_map/ppermute | solution.py:855
  117.5 8.5 %collective-permute-start.35 = (bf16[2,2,256,128]{3,2,1,0:T(8,128)(2,1)}, bf16[2,2,256,128]{3,2,1,0:T(8,128)(2,1)S(1)}, u32[]{:S(2)}, u32[]{:S(2)}) collective-permute-start(bf16[2,2,256,128]{3,2,1,0:T(8,128)(2,1)} %get-tuple-element.242), channel_id=1, source_target_pairs={{0,8},{4,12},{8,0},{12,4},{1,9},{5,13},{9,1},{13,5},{2,10},{6,14},... | collective-permute-start | bytes 786440 | tf_op jit(solution)/shard_map/ppermute | solution.py:855
  119.8 7.8 %collective-permute-start.42 = (bf16[4,384,128]{2,1,0:T(8,128)(2,1)S(1)}, bf16[4,384,128]{2,1,0:T(8,128)(2,1)}, u32[]{:S(2)}, u32[]{:S(2)}) collective-permute-start(bf16[4,384,128]{2,1,0:T(8,128)(2,1)S(1)} %get-tuple-element.246.refs_15_.refs_13_.refs_16_), channel_id=1, source_target_pairs={{0,4},{4,0},{8,12},{12,8},{1,5},{5,1},{9,13},{13,9},{2,6},{6,2},{1... | collective-permute-start | bytes 1179656 | tf_op jit(solution)/shard_map/ppermute | solution.py:855
  147.5 9.4 %collective-permute-start.44 = (bf16[2,256,128]{2,1,0:T(8,128)(2,1)S(1)}, bf16[2,256,128]{2,1,0:T(8,128)(2,1)S(1)}, u32[]{:S(2)}, u32[]{:S(2)}) collective-permute-start(bf16[2,256,128]{2,1,0:T(8,128)(2,1)S(1)} %get-tuple-element.269), channel_id=1, source_target_pairs={{0,4},{4,0},{8,12},{12,8},{1,5},{5,1},{9,13},{13,9},{2,6},{6,2},{1... | collective-permute-start | bytes 393224 | tf_op jit(solution)/shard_map/ppermute | solution.py:855
  147.7 9.1 %collective-permute-start.45 = (bf16[2,2,256,128]{3,2,1,0:T(8,128)(2,1)S(1)}, bf16[2,2,256,128]{3,2,1,0:T(8,128)(2,1)S(1)}, u32[]{:S(2)}, u32[]{:S(2)}) collective-permute-start(bf16[2,2,256,128]{3,2,1,0:T(8,128)(2,1)S(1)} %get-tuple-element.270), channel_id=1, source_target_pairs={{0,8},{4,12},{8,0},{12,4},{1,9},{5,13},{9,1},{13,5},{2,10},{6,14},... | collective-permute-start | bytes 786440 | tf_op jit(solution)/shard_map/ppermute | solution.py:855
  156.2 11.4 %collective-permute-start.48 = (bf16[16,320,128]{2,1,0:T(8,128)(2,1)S(1)}, bf16[16,320,128]{2,1,0:T(8,128)(2,1)S(1)}, u32[]{:S(2)}, u32[]{:S(2)}) collective-permute-start(bf16[16,320,128]{2,1,0:T(8,128)(2,1)S(1)} %get-tuple-element.275), channel_id=1, source_target_pairs={{0,4},{4,0},{8,12},{12,8},{1,5},{5,1},{9,13},{13,9},{2,6},{6,2},{1... | collective-permute-start | bytes 3932168 | tf_op jit(solution)/shard_map/ppermute | solution.py:855
  156.4 10.9 %collective-permute-start.49 = (bf16[16,384,128]{2,1,0:T(8,128)(2,1)S(1)}, bf16[16,384,128]{2,1,0:T(8,128)(2,1)S(1)}, u32[]{:S(2)}, u32[]{:S(2)}) collective-permute-start(bf16[16,384,128]{2,1,0:T(8,128)(2,1)S(1)} %get-tuple-element.277), channel_id=1, source_target_pairs={{0,4},{4,0},{8,12},{12,8},{1,5},{5,1},{9,13},{13,9},{2,6},{6,2},{1... | collective-permute-start | bytes 4718600 | tf_op jit(solution)/shard_map/ppermute | solution.py:855
  168.0 17.1 %collective-permute-start.51 = (bf16[8,320,128]{2,1,0:T(8,128)(2,1)S(1)}, bf16[8,320,128]{2,1,0:T(8,128)(2,1)S(1)}, u32[]{:S(2)}, u32[]{:S(2)}) collective-permute-start(bf16[8,320,128]{2,1,0:T(8,128)(2,1)S(1)} %get-tuple-element.287), channel_id=1, source_target_pairs={{0,16},{16,0},{1,17},{17,1},{2,18},{18,2},{3,19},{19,3},{4,20},{20... | collective-permute-start | bytes 1966088 | tf_op jit(solution)/shard_map/ppermute | solution.py:855
  179.1 10.8 %collective-permute-start.52 = (bf16[1,256,512]{2,1,0:T(8,128)(2,1)S(1)}, bf16[1,256,512]{2,1,0:T(8,128)(2,1)S(1)}, u32[]{:S(2)}, u32[]{:S(2)}) collective-permute-start(bf16[1,256,512]{2,1,0:T(8,128)(2,1)S(1)} %get-tuple-element.291), channel_id=1, source_target_pairs={{0,8},{4,12},{8,0},{12,4},{1,9},{5,13},{9,1},{13,5},{2,10},{6,14},... | collective-permute-start | bytes 786440 | tf_op jit(solution)/shard_map/ppermute | solution.py:855
  185.7 9.3 %collective-permute-start.53 = (bf16[1,256,512]{2,1,0:T(8,128)(2,1)S(1)}, bf16[1,256,512]{2,1,0:T(8,128)(2,1)S(1)}, u32[]{:S(2)}, u32[]{:S(2)}) collective-permute-start(bf16[1,256,512]{2,1,0:T(8,128)(2,1)S(1)} %get-tuple-element.292), channel_id=1, source_target_pairs={{0,8},{4,12},{8,0},{12,4},{1,9},{5,13},{9,1},{13,5},{2,10},{6,14},... | collective-permute-start | bytes 786440 | tf_op jit(solution)/shard_map/ppermute | solution.py:855
  186.6 20.3 %collective-permute-start.55 = (bf16[4,192,128]{2,1,0:T(8,128)(2,1)S(1)}, bf16[4,192,128]{2,1,0:T(8,128)(2,1)S(1)}, u32[]{:S(2)}, u32[]{:S(2)}) collective-permute-start(bf16[4,192,128]{2,1,0:T(8,128)(2,1)S(1)} %get-tuple-element.408), channel_id=1, source_target_pairs={{0,16},{16,0},{1,17},{17,1},{2,18},{18,2},{3,19},{19,3},{4,20},{20... | collective-permute-start | bytes 589832 | tf_op jit(solution)/shard_map/ppermute | solution.py:855
  188.1 22.9 %collective-permute-start.54 = (bf16[8,384,128]{2,1,0:T(8,128)(2,1)S(1)}, bf16[8,384,128]{2,1,0:T(8,128)(2,1)S(1)}, u32[]{:S(2)}, u32[]{:S(2)}) collective-permute-start(bf16[8,384,128]{2,1,0:T(8,128)(2,1)S(1)} %get-tuple-element.308), channel_id=1, source_target_pairs={{0,16},{16,0},{1,17},{17,1},{2,18},{18,2},{3,19},{19,3},{4,20},{20... | collective-permute-start | bytes 2359304 | tf_op jit(solution)/shard_map/ppermute | solution.py:855
  188.7 18.2 %collective-permute-start.56 = (bf16[4,320,128]{2,1,0:T(8,128)(2,1)S(1)}, bf16[4,320,128]{2,1,0:T(8,128)(2,1)S(1)}, u32[]{:S(2)}, u32[]{:S(2)}) collective-permute-start(bf16[4,320,128]{2,1,0:T(8,128)(2,1)S(1)} %get-tuple-element.311), channel_id=1, source_target_pairs={{0,8},{4,12},{8,0},{12,4},{1,9},{5,13},{9,1},{13,5},{2,10},{6,14},... | collective-permute-start | bytes 983048 | tf_op jit(solution)/shard_map/ppermute | solution.py:855
  205.9 14.0 %collective-permute-start.57 = (bf16[2,256,128]{2,1,0:T(8,128)(2,1)S(1)}, bf16[2,256,128]{2,1,0:T(8,128)(2,1)S(1)}, u32[]{:S(2)}, u32[]{:S(2)}) collective-permute-start(bf16[2,256,128]{2,1,0:T(8,128)(2,1)S(1)} %get-tuple-element.321), channel_id=1, source_target_pairs={{0,4},{4,0},{8,12},{12,8},{1,5},{5,1},{9,13},{13,9},{2,6},{6,2},{1... | collective-permute-start | bytes 393224 | tf_op jit(solution)/shard_map/ppermute | solution.py:855
  205.9 13.8 %collective-permute-start.58 = (bf16[2,2,256,128]{3,2,1,0:T(8,128)(2,1)S(1)}, bf16[2,2,256,128]{3,2,1,0:T(8,128)(2,1)S(1)}, u32[]{:S(2)}, u32[]{:S(2)}) collective-permute-start(bf16[2,2,256,128]{3,2,1,0:T(8,128)(2,1)S(1)} %get-tuple-element.322), channel_id=1, source_target_pairs={{0,8},{4,12},{8,0},{12,4},{1,9},{5,13},{9,1},{13,5},{2,10},{6,14},... | collective-permute-start | bytes 786440 | tf_op jit(solution)/shard_map/ppermute | solution.py:855
  207.5 23.5 %collective-permute-start.61 = (bf16[512,128]{1,0:T(8,128)(2,1)S(1)}, bf16[512,128]{1,0:T(8,128)(2,1)S(1)}, u32[]{:S(2)}, u32[]{:S(2)}) collective-permute-start(bf16[512,128]{1,0:T(8,128)(2,1)S(1)} %get-tuple-element.330), channel_id=1, source_target_pairs={{0,1},{1,0},{2,3},{3,2},{4,5},{5,4},{6,7},{7,6},{8,9},{9,8},{10,11... | collective-permute-start | bytes 393224 | tf_op jit(solution)/shard_map/ppermute | solution.py:855
  208.4 24.0 %collective-permute-start.62 = (bf16[512,128]{1,0:T(8,128)(2,1)S(1)}, bf16[512,128]{1,0:T(8,128)(2,1)S(1)}, u32[]{:S(2)}, u32[]{:S(2)}) collective-permute-start(bf16[512,128]{1,0:T(8,128)(2,1)S(1)} %get-tuple-element.331), channel_id=1, source_target_pairs={{0,2},{1,3},{2,0},{3,1},{4,6},{5,7},{6,4},{7,5},{8,10},{9,11},{10,... | collective-permute-start | bytes 393224 | tf_op jit(solution)/shard_map/ppermute | solution.py:855
  211.3 15.8 %collective-permute-start.66 = (bf16[4,384,128]{2,1,0:T(8,128)(2,1)S(1)}, bf16[4,384,128]{2,1,0:T(8,128)(2,1)S(1)}, u32[]{:S(2)}, u32[]{:S(2)}) collective-permute-start(bf16[4,384,128]{2,1,0:T(8,128)(2,1)S(1)} %get-tuple-element.338), channel_id=1, source_target_pairs={{0,8},{4,12},{8,0},{12,4},{1,9},{5,13},{9,1},{13,5},{2,10},{6,14},... | collective-permute-start | bytes 1179656 | tf_op jit(solution)/shard_map/ppermute | solution.py:855
  219.9 9.9 %collective-permute-start.64 = (bf16[16,320,128]{2,1,0:T(8,128)(2,1)S(1)}, bf16[16,320,128]{2,1,0:T(8,128)(2,1)S(1)}, u32[]{:S(2)}, u32[]{:S(2)}) collective-permute-start(bf16[16,320,128]{2,1,0:T(8,128)(2,1)S(1)} %get-tuple-element.334), channel_id=1, source_target_pairs={{0,4},{4,0},{8,12},{12,8},{1,5},{5,1},{9,13},{13,9},{2,6},{6,2},{1... | collective-permute-start | bytes 3932168 | tf_op jit(solution)/shard_map/ppermute | solution.py:855
  221.3 7.9 %collective-permute-start.65 = (bf16[16,384,128]{2,1,0:T(8,128)(2,1)S(1)}, bf16[16,384,128]{2,1,0:T(8,128)(2,1)S(1)}, u32[]{:S(2)}, u32[]{:S(2)}) collective-permute-start(bf16[16,384,128]{2,1,0:T(8,128)(2,1)S(1)} %get-tuple-element.336), channel_id=1, source_target_pairs={{0,4},{4,0},{8,12},{12,8},{1,5},{5,1},{9,13},{13,9},{2,6},{6,2},{1... | collective-permute-start | bytes 4718600 | tf_op jit(solution)/shard_map/ppermute | solution.py:855
  227.0 7.7 %collective-permute-start.63 = (bf16[512,128]{1,0:T(8,128)(2,1)S(1)}, bf16[512,128]{1,0:T(8,128)(2,1)S(1)}, u32[]{:S(2)}, u32[]{:S(2)}) collective-permute-start(bf16[512,128]{1,0:T(8,128)(2,1)S(1)} %get-tuple-element.332), channel_id=1, source_target_pairs={{0,3},{1,2},{2,1},{3,0},{4,7},{5,6},{6,5},{7,4},{8,11},{9,10},{10,... | collective-permute-start | bytes 393224 | tf_op jit(solution)/shard_map/ppermute | solution.py:855
  230.1 17.1 %collective-permute-start.69 = (bf16[8,320,128]{2,1,0:T(8,128)(2,1)S(1)}, bf16[8,320,128]{2,1,0:T(8,128)(2,1)S(1)}, u32[]{:S(2)}, u32[]{:S(2)}) collective-permute-start(bf16[8,320,128]{2,1,0:T(8,128)(2,1)S(1)} %get-tuple-element.355), channel_id=1, source_target_pairs={{0,8},{4,12},{8,0},{12,4},{1,9},{5,13},{9,1},{13,5},{2,10},{6,14},... | collective-permute-start | bytes 1966088 | tf_op jit(solution)/shard_map/ppermute | solution.py:855
  231.0 19.6 %collective-permute-start.68 = (bf16[8,384,128]{2,1,0:T(8,128)(2,1)S(1)}, bf16[8,384,128]{2,1,0:T(8,128)(2,1)S(1)}, u32[]{:S(2)}, u32[]{:S(2)}) collective-permute-start(bf16[8,384,128]{2,1,0:T(8,128)(2,1)S(1)} %get-tuple-element.353), channel_id=1, source_target_pairs={{0,16},{16,0},{1,17},{17,1},{2,18},{18,2},{3,19},{19,3},{4,20},{20... | collective-permute-start | bytes 2359304 | tf_op jit(solution)/shard_map/ppermute | solution.py:855
  244.7 9.0 %collective-permute-start.73 = (bf16[384,128]{1,0:T(8,128)(2,1)S(1)}, bf16[384,128]{1,0:T(8,128)(2,1)S(1)}, u32[]{:S(2)}, u32[]{:S(2)}) collective-permute-start(bf16[384,128]{1,0:T(8,128)(2,1)S(1)} %get-tuple-element.365), channel_id=1, source_target_pairs={{0,1},{1,0},{2,3},{3,2},{4,5},{5,4},{6,7},{7,6},{8,9},{9,8},{10,11... | collective-permute-start | bytes 294920 | tf_op jit(solution)/shard_map/ppermute | solution.py:855
  246.8 10.6 %collective-permute-start.74 = (bf16[384,128]{1,0:T(8,128)(2,1)S(1)}, bf16[384,128]{1,0:T(8,128)(2,1)S(1)}, u32[]{:S(2)}, u32[]{:S(2)}) collective-permute-start(bf16[384,128]{1,0:T(8,128)(2,1)S(1)} %get-tuple-element.366), channel_id=1, source_target_pairs={{0,2},{1,3},{2,0},{3,1},{4,6},{5,7},{6,4},{7,5},{8,10},{9,11},{10,... | collective-permute-start | bytes 294920 | tf_op jit(solution)/shard_map/ppermute | solution.py:855
  247.3 11.0 %collective-permute-start.75 = (bf16[384,128]{1,0:T(8,128)(2,1)S(1)}, bf16[384,128]{1,0:T(8,128)(2,1)S(1)}, u32[]{:S(2)}, u32[]{:S(2)}) collective-permute-start(bf16[384,128]{1,0:T(8,128)(2,1)S(1)} %get-tuple-element.367), channel_id=1, source_target_pairs={{0,3},{1,2},{2,1},{3,0},{4,7},{5,6},{6,5},{7,4},{8,11},{9,10},{10,... | collective-permute-start | bytes 294920 | tf_op jit(solution)/shard_map/ppermute | solution.py:855
  250.6 15.0 %collective-permute-start.70 = (bf16[1,256,512]{2,1,0:T(8,128)(2,1)S(1)}, bf16[1,256,512]{2,1,0:T(8,128)(2,1)S(1)}, u32[]{:S(2)}, u32[]{:S(2)}) collective-permute-start(bf16[1,256,512]{2,1,0:T(8,128)(2,1)S(1)} %get-tuple-element.360), channel_id=1, source_target_pairs={{0,8},{4,12},{8,0},{12,4},{1,9},{5,13},{9,1},{13,5},{2,10},{6,14},... | collective-permute-start | bytes 786440 | tf_op jit(solution)/shard_map/ppermute | solution.py:855
  252.0 29.1 %collective-permute-start.79 = (bf16[4,192,128]{2,1,0:T(8,128)(2,1)S(1)}, bf16[4,192,128]{2,1,0:T(8,128)(2,1)S(1)}, u32[]{:S(2)}, u32[]{:S(2)}) collective-permute-start(bf16[4,192,128]{2,1,0:T(8,128)(2,1)S(1)} %get-tuple-element.406), channel_id=1, source_target_pairs={{0,16},{16,0},{1,17},{17,1},{2,18},{18,2},{3,19},{19,3},{4,20},{20... | collective-permute-start | bytes 589832 | tf_op jit(solution)/shard_map/ppermute | solution.py:855
  253.7 11.2 %collective-permute-start.72 = (bf16[4,320,128]{2,1,0:T(8,128)(2,1)S(1)}, bf16[4,320,128]{2,1,0:T(8,128)(2,1)S(1)}, u32[]{:S(2)}, u32[]{:S(2)}) collective-permute-start(bf16[4,320,128]{2,1,0:T(8,128)(2,1)S(1)} %get-tuple-element.363), channel_id=1, source_target_pairs={{0,16},{16,0},{1,17},{17,1},{2,18},{18,2},{3,19},{19,3},{4,20},{20... | collective-permute-start | bytes 983048 | tf_op jit(solution)/shard_map/ppermute | solution.py:855
  257.4 9.2 %collective-permute-start.71 = (bf16[1,256,512]{2,1,0:T(8,128)(2,1)S(1)}, bf16[1,256,512]{2,1,0:T(8,128)(2,1)S(1)}, u32[]{:S(2)}, u32[]{:S(2)}) collective-permute-start(bf16[1,256,512]{2,1,0:T(8,128)(2,1)S(1)} %get-tuple-element.361), channel_id=1, source_target_pairs={{0,8},{4,12},{8,0},{12,4},{1,9},{5,13},{9,1},{13,5},{2,10},{6,14},... | collective-permute-start | bytes 786440 | tf_op jit(solution)/shard_map/ppermute | solution.py:855
  258.2 22.9 %collective-permute-start.80 = (bf16[4,384,128]{2,1,0:T(8,128)(2,1)S(1)}, bf16[4,384,128]{2,1,0:T(8,128)(2,1)S(1)}, u32[]{:S(2)}, u32[]{:S(2)}) collective-permute-start(bf16[4,384,128]{2,1,0:T(8,128)(2,1)S(1)} %get-tuple-element.380), channel_id=1, source_target_pairs={{0,8},{4,12},{8,0},{12,4},{1,9},{5,13},{9,1},{13,5},{2,10},{6,14},... | collective-permute-start | bytes 1179656 | tf_op jit(solution)/shard_map/ppermute | solution.py:855
  276.7 7.6 %collective-permute-start.76 = (bf16[320,128]{1,0:T(8,128)(2,1)S(1)}, bf16[320,128]{1,0:T(8,128)(2,1)S(1)}, u32[]{:S(2)}, u32[]{:S(2)}) collective-permute-start(bf16[320,128]{1,0:T(8,128)(2,1)S(1)} %get-tuple-element.375), channel_id=1, source_target_pairs={{0,1},{1,0},{2,3},{3,2},{4,5},{5,4},{6,7},{7,6},{8,9},{9,8},{10,11... | collective-permute-start | bytes 245768 | tf_op jit(solution)/shard_map/ppermute | solution.py:855
  276.7 9.6 %collective-permute-start.77 = (bf16[320,128]{1,0:T(8,128)(2,1)S(1)}, bf16[320,128]{1,0:T(8,128)(2,1)S(1)}, u32[]{:S(2)}, u32[]{:S(2)}) collective-permute-start(bf16[320,128]{1,0:T(8,128)(2,1)S(1)} %get-tuple-element.376), channel_id=1, source_target_pairs={{0,2},{1,3},{2,0},{3,1},{4,6},{5,7},{6,4},{7,5},{8,10},{9,11},{10,... | collective-permute-start | bytes 245768 | tf_op jit(solution)/shard_map/ppermute | solution.py:855
  281.8 17.1 %collective-permute-start.81 = (bf16[576,128]{1,0:T(8,128)(2,1)S(1)}, bf16[576,128]{1,0:T(8,128)(2,1)S(1)}, u32[]{:S(2)}, u32[]{:S(2)}) collective-permute-start(bf16[576,128]{1,0:T(8,128)(2,1)S(1)} %get-tuple-element.385), channel_id=1, source_target_pairs={{0,1},{1,0},{2,3},{3,2},{4,5},{5,4},{6,7},{7,6},{8,9},{9,8},{10,11... | collective-permute-start | bytes 442376 | tf_op jit(solution)/shard_map/ppermute | solution.py:855
  281.9 17.0 %collective-permute-start.82 = (bf16[576,128]{1,0:T(8,128)(2,1)S(1)}, bf16[576,128]{1,0:T(8,128)(2,1)S(1)}, u32[]{:S(2)}, u32[]{:S(2)}) collective-permute-start(bf16[576,128]{1,0:T(8,128)(2,1)S(1)} %get-tuple-element.386), channel_id=1, source_target_pairs={{0,2},{1,3},{2,0},{3,1},{4,6},{5,7},{6,4},{7,5},{8,10},{9,11},{10,... | collective-permute-start | bytes 442376 | tf_op jit(solution)/shard_map/ppermute | solution.py:855
  284.3 14.6 %collective-permute-start.83 = (bf16[576,128]{1,0:T(8,128)(2,1)S(1)}, bf16[576,128]{1,0:T(8,128)(2,1)S(1)}, u32[]{:S(2)}, u32[]{:S(2)}) collective-permute-start(bf16[576,128]{1,0:T(8,128)(2,1)S(1)} %get-tuple-element.387), channel_id=1, source_target_pairs={{0,3},{1,2},{2,1},{3,0},{4,7},{5,6},{6,5},{7,4},{8,11},{9,10},{10,... | collective-permute-start | bytes 442376 | tf_op jit(solution)/shard_map/ppermute | solution.py:855
  290.0 8.9 %collective-permute-start.88 = (bf16[16,128]{1,0:T(8,128)(2,1)S(1)}, bf16[16,128]{1,0:T(8,128)(2,1)S(1)}, u32[]{:S(2)}, u32[]{:S(2)}) collective-permute-start(bf16[16,128]{1,0:T(8,128)(2,1)S(1)} %get-tuple-element.393), channel_id=1, source_target_pairs={{0,2},{1,3},{2,0},{3,1},{4,6},{5,7},{6,4},{7,5},{8,10},{9,11},{10,... | collective-permute-start | bytes 12296 | tf_op jit(solution)/shard_map/ppermute | solution.py:855
  (84 other events, 667.2 us)

commit v2 on v1

--- a/solution.py
+++ b/solution.py
@@ -532,7 +532,7 @@
 
 def second_back_body(
     wd, wu, layer, mp_size, chunks, batch, me_ref, g_ref, mid_ref, n2_ref, s2_ref, slope_ref,
-    par_ref, *refs
+    par_ref, *refs, before=None
 ):
     d_refs, refs = refs[: len(wd.arrays)], refs[len(wd.arrays) :]
     u_refs, refs = shared(wd, wu, d_refs, refs)
@@ -541,6 +541,8 @@
     o_refs, refs = [refs[0], refs[1], refs[2].at[0], refs[2].at[1]], refs[3:]
     o_scr, d_scr, u_scr, d_sem, u_sem = refs
     w_d = wd.open(d_refs, me_ref, d_scr, d_sem, chunks)
+    if before is not None:
+        before()
     ff = slope_ref.shape[1]
     model = g_ref.shape[1]
     ff_m = ff // mp_size
@@ -771,6 +773,61 @@
     )
 
 
+def turn_body(wd, wu, layer, mp_size, chunks, batch, me_ref, *refs):
+    count = 6 + 2 * batch
+    upper, refs = refs[:count], refs[count:]
+    lower, refs = refs[:4], refs[4:]
+    arrays = len(wd.arrays) + len(others(wd, wu))
+    parts, refs = refs[:arrays], refs[arrays:]
+    sums_ref, refs = refs[0], refs[1:]
+    g_scr, rest = refs[-6], refs[:-6] + refs[-5:]
+
+    def before():
+        first_back_body(layer + 1, batch, me_ref, *upper, g_scr, sums_ref)
+
+    second_back_body(
+        wd, wu, layer, mp_size, chunks, batch, me_ref, g_scr, *lower, upper[3], *parts, *rest,
+        before=before,
+    )
+
+
+def turn(me, upper, kept, got, lower, wd, wu, layer, mp_size, chunks):
+    x, gmid, local, par, sums2, sums1 = upper
+    mid, n2, s2, slope = lower
+    batch = len(kept)
+    rows, model = x.shape
+    ff = slope.shape[1]
+    out = [
+        sds((8, model), F32),
+        sds((rows, model), BF16),
+        sds((rows, ff + LANE * mp_size), BF16),
+        sds((rows, model), F32),
+        sds((rows, model), BF16),
+        sds((8, model), F32),
+    ]
+    out += [sds((batch, rows // batch, LANE), BF16)] * 2
+    out += [sds((2, batch, rows // batch, LANE), BF16)]
+    return call(
+        functools.partial(turn_body, wd, wu, layer, mp_size, chunks, batch),
+        "second_back",
+        out,
+        [me, Late(x), gmid, local, par, sums2, sums1]
+        + kept
+        + got
+        + [Late(mid), Late(n2), Late(s2), Late(slope)],
+        smem=1,
+        parts=wd.arrays + others(wd, wu),
+        scratch=[
+            pltpu.VMEM((rows, model), F32),
+            pltpu.VMEM((rows, LANE), BF16),
+            pltpu.VMEM((chunks * mp_size, wd.rows, LANE), BF16),
+            pltpu.VMEM((chunks * mp_size, wu.rows, LANE), BF16),
+            pltpu.SemaphoreType.DMA,
+            pltpu.SemaphoreType.DMA,
+        ],
+    )
+
+
 def put_blocks(outs, mx, me_d, chunks, at_block, res, mp_first=False):
     half = chunks // 2
     for d in range(chunks):
@@ -1288,9 +1345,14 @@
             x, n_parts, kept, att, s1, mid, n2, s2, act, slope = saved[l]
             n_rows = [n_parts[r][0] for r in range(batch)]
             final, first_of_two = l == 0, l + 1 < layers
-            b2, dcomb, gmid, b1, sums2, *o_parts = second_back(
-                me, g, mid, n2, s2, slope, par, wd, wu, l, mp_size, chunks, batch
-            )
+            if first_of_two:
+                all_sums[l + 1], b2, dcomb, gmid, b1, sums2, *o_parts = turn(
+                    me, upper, keeps, gots, (mid, n2, s2, slope), wd, wu, l, mp_size, chunks
+                )
+            else:
+                b2, dcomb, gmid, b1, sums2, *o_parts = second_back(
+                    me, g, mid, n2, s2, slope, par, wd, wu, l, mp_size, chunks, batch
+                )
             d_parts = exchange(*o_parts)
             if first_of_two:
                 reduce_4([("q", l + 1), ("u", l + 1)])
@@ -1329,7 +1391,9 @@
                 moving["q", l] = (q_grad[:half], dp_swap(q_grad[half:]))
                 if final:
                     reduce_4([("u", l)])
-            g, all_sums[l] = first_back(me, x, gmid, local, par, sums2, sums1, keeps, gots, l)
+            upper = (x, gmid, local, par, sums2, sums1)
+            if final:
+                g, all_sums[l] = first_back(me, *upper, keeps, gots, l)
             if direct and final:
                 reduce_4([("q", l), ("d", l)])
                 moving["u", l] = [reduce_5(("u", l))]

time: 306 us -> 306 us (level)
    pallas_call x53 -> x52, Pallas kernels: 125 us -> 123 us  [call(): pl.pallas_call(inner, name=name, out_shape=[pltpu.HBM(o.shape, o.dtype) i...]
where the time goes in v2:
time: 306 us; the launch traced here: 300 us
  Pallas kernels  123 us (40%)
  waiting for transfers between devices  83.3 us (27%)
  starting transfers between devices  83 us (27%)
  local copies, waits for them, and re-layouts  7.28 us (2%)
    pallas_call x52, Pallas kernels, call(): pl.pallas_call(inner, name=name, out_shape=[pltpu.HBM(o.shape, o.dtype) i...  123 us
    ppermute x90, waiting for transfers between devices, swap(): return lax.ppermute(value, axis, [(i, i ^ bits) for i in range(size)])  83.3 us
    ppermute x90, starting transfers between devices, swap(): return lax.ppermute(value, axis, [(i, i ^ bits) for i in range(size)])  83 us
  transfers between devices with their start and end apart: 90, of which 27 were waited for; matrix products, arithmetic and copies ran while one was open for 0% of the time, Pallas kernels for 34%

profile of v2, /device:TPU:0, one launch (start us, length us, event | category | flops | bytes accessed | tf_op | source)
XLA Modules:
  0.0 299.9 jit_solution(1211956823518949714)
XLA Ops:
  0.6 1.3 slice.15
  5.6 5.1 %collective-permute-start.4 = (bf16[208,128]{1,0:T(8,128)(2,1)S(1)}, bf16[208,128]{1,0:T(8,128)(2,1)S(1)}, u32[]{:S(2)}, u32[]{:S(2)}) collective-permute-start(bf16[208,128]{1,0:T(8,128)(2,1)S(1)} %get-tuple-element.205.refs_0_), channel_id=1, source_target_pairs={{0,3},{1,2},{2,1},{3,0},{4,7},{5,6},{6,5},{7,4},{8,11},{9,10},{10,... | collective-permute-start | bytes 159752 | tf_op jit(solution)/shard_map/ppermute | solution.py:912
  11.4 3.8 %collective-permute-start.9 = (bf16[704,128]{1,0:T(8,128)(2,1)S(1)}, bf16[704,128]{1,0:T(8,128)(2,1)S(1)}, u32[]{:S(2)}, u32[]{:S(2)}) collective-permute-start(bf16[704,128]{1,0:T(8,128)(2,1)S(1)} %get-tuple-element.211.refs_0_), channel_id=1, source_target_pairs={{0,3},{1,2},{2,1},{3,0},{4,7},{5,6},{6,5},{7,4},{8,11},{9,10},{10,... | collective-permute-start | bytes 540680 | tf_op jit(solution)/shard_map/ppermute | solution.py:912
  15.2 1.5 collective-permute-start.1
  17.7 5.1 %collective-permute-done.3.refs_2_ = bf16[208,128]{1,0:T(8,128)(2,1)S(1)} collective-permute-done((bf16[208,128]{1,0:T(8,128)(2,1)S(1)}, bf16[208,128]{1,0:T(8,128)(2,1)S(1)}, u32[]{:S(2)}, u32[]{:S(2)}) %collective-permute-start.3) | collective-permute-done | bytes 53280 | tf_op jit(solution)/shard_map/ppermute | solution.py:912
  23.0 4.7 %collective-permute-done.1.refs_0_.refs_5_ = bf16[2,256,512]{2,1,0:T(8,128)(2,1)S(1)} collective-permute-done((bf16[2,256,512]{2,1,0:T(8,128)(2,1)S(1)}, bf16[2,256,512]{2,1,0:T(8,128)(2,1)S(1)}, u32[]{:S(2)}, u32[]{:S(2)}) %collective-permute-start.1) | collective-permute-done | bytes 524320 | tf_op jit(solution)/shard_map/ppermute | solution.py:912
  27.8 1.5 collective-permute-start.6
  29.4 1.6 collective-permute-done.8.refs_2_
  32.2 1.5 collective-permute-start.20
  33.7 2.9 collective-permute-start.18
  36.7 1.4 collective-permute-start.14
  38.1 1.5 collective-permute-start.13
  39.6 14.2 %attend.2 = (bf16[2,1024,384]{2,1,0:T(8,128)(2,1)}, f32[4,1,1024]{2,1,0:T(1,128)}, bf16[2,256,128]{2,1,0:T(8,128)(2,1)S(1)}, bf16[2,256,128]{2,1,0:T(8,128)(2,1)...) custom-call(s32[4]{0:T(128)S(1)} %copy-done.5, ...), custom_call_target="tpu_custom_call" | custom-call | flops 44000002048 | bytes 144000000 | tf_op jit(solution)/shard_map/attend/pallas_call | solution.py:173
  54.7 1.4 collective-permute-start.11
  57.4 8.7 %collective-permute-done.11.refs_0_.refs_7_ = bf16[2,2,256,128]{3,2,1,0:T(8,128)(2,1)S(1)} collective-permute-done((bf16[2,2,256,128]{3,2,1,0:T(8,128)(2,1)S(1)}, bf16[2,2,256,128]{3,2,1,0:T(8,128)(2,1)S(1)}, u32[]{:S(2)}, u32[]{:S(2)}) %collective-permute-start.11) | collective-permute-done | bytes 262176 | tf_op jit(solution)/shard_map/ppermute | solution.py:912
  68.4 2.3 collective-permute-done.12.refs_8_
  71.3 1.7 collective-permute-start.32
  74.1 10.7 %second.2 = (bf16[512,512]{1,0:T(8,128)(2,1)}, f32[512,512]{1,0:T(8,128)}, f32[512,512]{1,0:T(8,128)}, bf16[512,512]{1,0:T(8,128)(2,1)}, f32[512,512]{1,0:T(8,12...) custom-call(s32[4]{0:T(128)S(1)} %copy-done.5, ...), custom_call_target="tpu_custom_call" | custom-call | flops 65999998976 | bytes 216000000 | tf_op jit(solution)/shard_map/second/pallas_call | solution.py:173
  85.2 1.7 collective-permute-start.28
  87.4 5.7 %collective-permute-done.31.refs_2_.refs_12_.refs_14_.refs_15_ = bf16[4,192,128]{2,1,0:T(8,128)(2,1)S(1)} collective-permute-done((bf16[4,192,128]{2,1,0:T(8,128)(2,1)S(1)}, bf16[4,192,128]{2,1,0:T(8,128)(2,1)S(1)}, u32[]{:S(2)}, u32[]{:S(2)}) %collective-permute-start.31) | collective-permute-done | bytes 196640 | tf_op jit(solution)/shard_map/ppermute | solution.py:912
  93.1 2.8 collective-permute-done.27.refs_3_.refs_7_.refs_11_
  96.0 4.5 %collective-permute-done.28.refs_4_.refs_8_.refs_11_ = bf16[256,512]{1,0:T(8,128)(2,1)S(1)} collective-permute-done((bf16[256,512]{1,0:T(8,128)(2,1)S(1)}, bf16[256,512]{1,0:T(8,128)(2,1)S(1)}, u32[]{:S(2)}, u32[]{:S(2)}) %collective-permute-start.28) | collective-permute-done | bytes 262176 | tf_op jit(solution)/shard_map/ppermute | solution.py:912
  101.1 1.7 collective-permute-start.41
  104.1 13.4 %attend.3 = (bf16[2,1024,384]{2,1,0:T(8,128)(2,1)S(1)}, f32[4,1,1024]{2,1,0:T(1,128)S(1)}, bf16[2,256,128]{2,1,0:T(8,128)(2,1)S(1)}, bf16[2,256,128]{2,1,0:T(8,1...) custom-call(s32[4]{0:T(128)S(1)} %copy-done.5, s32[2,1024]{1,0:T(2,128)S(1)} %get-tuple-element.401.refs_1_, ...), custom_call_target="tpu_custom_call" | custom-call | flops 44000002048 | bytes 144000000 | tf_op jit(solution)/shard_map/attend/pallas_call | solution.py:173
  117.6 1.3 collective-permute-start.35
  121.2 4.9 %collective-permute-done.35.refs_7_ = bf16[2,2,256,128]{3,2,1,0:T(8,128)(2,1)S(1)} collective-permute-done((bf16[2,2,256,128]{3,2,1,0:T(8,128)(2,1)}, bf16[2,2,256,128]{3,2,1,0:T(8,128)(2,1)S(1)}, u32[]{:S(2)}, u32[]{:S(2)}) %collective-permute-start.35) | collective-permute-done | bytes 262176 | tf_op jit(solution)/shard_map/ppermute | solution.py:912
  126.3 1.4 collective-permute-done.36.refs_8_
  128.4 10.8 %second.3 = (bf16[512,512]{1,0:T(8,128)(2,1)}, f32[512,512]{1,0:T(8,128)}, f32[512,512]{1,0:T(8,128)}, bf16[512,512]{1,0:T(8,128)(2,1)}, f32[512,512]{1,0:T(8,12...) custom-call(s32[4]{0:T(128)S(1)} %copy-done.5, ...), custom_call_target="tpu_custom_call" | custom-call | flops 65999998976 | bytes 216000000 | tf_op jit(solution)/shard_map/second/pallas_call | solution.py:173
  139.2 8.3 %second_back.2 = (bf16[512,512]{1,0:T(8,128)(2,1)S(1)}, bf16[512,2560]{1,0:T(8,128)(2,1)S(1)}, f32[512,512]{1,0:T(8,128)S(1)}, bf16[512,512]{1,0:T(8,128)(2,1)S(...) custom-call(s32[4]{0:T(128)S(1)} %copy-done.5, ...), custom_call_target="tpu_custom_call" | custom-call | flops 54999998464 | bytes 180000000 | tf_op jit(solution)/shard_map/second_back/pallas_call | solution.py:173
  147.7 1.3 collective-permute-start.45
  149.0 7.3 %weight_grad.2 = (bf16[16,320,128]{2,1,0:T(8,128)(2,1)S(1)}, bf16[16,320,128]{2,1,0:T(8,128)(2,1)S(1)}, bf16[16,384,128]{2,1,0:T(8,128)(2,1)S(1)}, bf16[16,384,1...) custom-call(s32[4]{0:T(128)S(1)} %copy-done.5, ...), custom_call_target="tpu_custom_call" | custom-call | flops 44000002048 | bytes 144000000 | tf_op jit(solution)/shard_map/weight_grad/pallas_call | solution.py:173
  157.0 5.0 %collective-permute-done.46.refs_8_ = bf16[2,2,256,128]{3,2,1,0:T(8,128)(2,1)S(1)} collective-permute-done((bf16[2,2,256,128]{3,2,1,0:T(8,128)(2,1)S(1)}, bf16[2,2,256,128]{3,2,1,0:T(8,128)(2,1)S(1)}, u32[]{:S(2)}, u32[]{:S(2)}) %collective-permute-start.46) | collective-permute-done | bytes 262176 | tf_op jit(solution)/shard_map/ppermute | solution.py:912
  162.1 5.1 %attend_back.4 = (bf16[2,256,512]{2,1,0:T(8,128)(2,1)S(1)}, bf16[2,256,512]{2,1,0:T(8,128)(2,1)S(1)}, f32[512,384]{1,0:T(8,128)S(1)}, f32[8,128]{1,0:T(8,128)S(1)}) custom-call(s32[4]{0:T(128)S(1)} %copy-done.5, s32[2,1024]{1,0:T(2,128)S(1)} %copy-done.3, f32[2,1,1024]{2,1,0:T(1,128)S(1)} %copy-done.1, bf16[2,1024,384]{2,1,0:T(8,128)(2,1)S(1)} %copy-done.39, ...), custom_call_target="tpu_custom_call" | custom-call | flops 49500000256 | bytes 162000000 | tf_op jit(solution)/shard_map/attend_back/pallas_call | solution.py:173
  169.3 9.6 %attend_back.5 = (bf16[2,256,512]{2,1,0:T(8,128)(2,1)S(1)}, bf16[2,256,512]{2,1,0:T(8,128)(2,1)S(1)}, bf16[8,192,128]{2,1,0:T(8,128)(2,1)S(1)}, f32[8,128]{1,0:T(8,128)S(1)}) custom-call(s32[4]{0:T(128)S(1)} %copy-done.5, s32[2,1024]{1,0:T(2,128)S(1)} %copy-done.3, f32[2,1,1024]{2,1,0:T(1,128)S(1)} %copy-done.1, bf16[2,1024,384]{2,1,0:T(8,128)(2,1)S(1)} %copy-done.39, ...), custom_call_target="tpu_custom_call" | custom-call | flops 49500000256 | bytes 162000000 | tf_op jit(solution)/shard_map/attend_back/pallas_call | solution.py:173
  179.1 1.2 collective-permute-start.52
  180.3 4.9 %collective-permute-done.51.refs_1_ = bf16[8,320,128]{2,1,0:T(8,128)(2,1)S(1)} collective-permute-done((bf16[8,320,128]{2,1,0:T(8,128)(2,1)S(1)}, bf16[8,320,128]{2,1,0:T(8,128)(2,1)S(1)}, u32[]{:S(2)}, u32[]{:S(2)}) %collective-permute-start.51) | collective-permute-done | bytes 655392 | tf_op jit(solution)/shard_map/ppermute | solution.py:912
  186.7 1.5 collective-permute-start.55
  190.0 5.1 %collective-permute-done.53 = bf16[1,256,512]{2,1,0:T(8,128)(2,1)S(1)} collective-permute-done((bf16[1,256,512]{2,1,0:T(8,128)(2,1)S(1)}, bf16[1,256,512]{2,1,0:T(8,128)(2,1)S(1)}, u32[]{:S(2)}, u32[]{:S(2)}) %collective-permute-start.53) | collective-permute-done | bytes 262176 | tf_op jit(solution)/shard_map/ppermute | solution.py:912
  195.1 8.8 %second_back.3 = (f32[8,512]{1,0:T(8,128)S(1)}, bf16[512,512]{1,0:T(8,128)(2,1)S(1)}, bf16[512,2560]{1,0:T(8,128)(2,1)S(1)}, f32[512,512]{1,0:T(8,128)S(1)}, bf1...) custom-call(s32[4]{0:T(128)S(1)} %copy-done.5, ...), custom_call_target="tpu_custom_call" | custom-call | flops 54999998464 | bytes 180000000 | tf_op jit(solution)/shard_map/second_back/pallas_call | solution.py:173
  206.4 2.5 collective-permute-start.62
  209.9 1.3 collective-permute-start.66
  211.2 7.1 %weight_grad.3 = (bf16[16,320,128]{2,1,0:T(8,128)(2,1)S(1)}, bf16[16,320,128]{2,1,0:T(8,128)(2,1)S(1)}, bf16[16,384,128]{2,1,0:T(8,128)(2,1)S(1)}, bf16[16,384,1...) custom-call(s32[4]{0:T(128)S(1)} %copy-done.5, ...), custom_call_target="tpu_custom_call" | custom-call | flops 44000002048 | bytes 144000000 | tf_op jit(solution)/shard_map/weight_grad/pallas_call | solution.py:173
  220.1 5.5 %attend_back.6 = (bf16[2,256,512]{2,1,0:T(8,128)(2,1)S(1)}, bf16[2,256,512]{2,1,0:T(8,128)(2,1)S(1)}, f32[512,384]{1,0:T(8,128)S(1)}, f32[8,128]{1,0:T(8,128)S(1)}) custom-call(s32[4]{0:T(128)S(1)} %copy-done.5, s32[2,1024]{1,0:T(2,128)S(1)} %copy-done.3, f32[2,1,1024]{2,1,0:T(1,128)S(1)} %copy-done.1, bf16[2,1024,384]{2,1,0:T(8,128)(2,1)S(1)} %copy-done.37, ...), custom_call_target="tpu_custom_call" | custom-call | flops 49500000256 | bytes 162000000 | tf_op jit(solution)/shard_map/attend_back/pallas_call | solution.py:173
  225.6 2.9 collective-permute-start.63
  231.0 1.5 collective-permute-start.68
  233.6 9.6 %attend_back.7 = (bf16[2,256,512]{2,1,0:T(8,128)(2,1)S(1)}, bf16[2,256,512]{2,1,0:T(8,128)(2,1)S(1)}, bf16[8,192,128]{2,1,0:T(8,128)(2,1)S(1)}, f32[8,128]{1,0:T(8,128)S(1)}) custom-call(s32[4]{0:T(128)S(1)} %copy-done.5, s32[2,1024]{1,0:T(2,128)S(1)} %copy-done.3, f32[2,1,1024]{2,1,0:T(1,128)S(1)} %copy-done.1, bf16[2,1024,384]{2,1,0:T(8,128)(2,1)S(1)} %copy-done.37, ...), custom_call_target="tpu_custom_call" | custom-call | flops 49500000256 | bytes 162000000 | tf_op jit(solution)/shard_map/attend_back/pallas_call | solution.py:173
  243.3 2.4 collective-permute-start.73
  245.7 1.2 collective-permute-start.74
  248.6 2.1 collective-permute-done.68.refs_1_
  252.0 1.6 collective-permute-start.79
  254.3 1.9 collective-permute-done.74.refs_2_
  258.3 6.6 %collective-permute-done.72.refs_2_ = bf16[4,320,128]{2,1,0:T(8,128)(2,1)S(1)} collective-permute-done((bf16[4,320,128]{2,1,0:T(8,128)(2,1)S(1)}, bf16[4,320,128]{2,1,0:T(8,128)(2,1)S(1)}, u32[]{:S(2)}, u32[]{:S(2)}) %collective-permute-start.72) | collective-permute-done | bytes 327712 | tf_op jit(solution)/shard_map/ppermute | solution.py:912
  265.6 3.3 %first_back.1 = (f32[512,512]{1,0:T(8,128)}, f32[8,512]{1,0:T(8,128)S(1)}, f32[8,128]{1,0:T(8,128)S(1)}) custom-call(s32[4]{0:T(128)S(1)} %copy-done.5, bf16[512,512]{1,0:T(8,128)(2,1)} %bitcast.25, f32[512,512]{1,0:T(8,128)S(1)} %get-tuple-element.296.refs_2_, f32[512,512]{1,0:T(8,128)S(1)} %get-tuple-element.311.refs_3_, f32[2,8,512]{2,1,0:T(8,128)S(1)} %copy-done.41, ...), custom_call_target="tpu_custom_call" | custom-call | flops 22000001024 | bytes 72000000 | tf_op jit(solution)/shard_map/first_back/pallas_call | solution.py:173
  271.3 2.9 collective-permute-done.85
  274.2 1.5 collective-permute-start.86
  276.0 2.7 collective-permute-start.77
  278.6 1.9 collective-permute-start.78
  281.3 2.5 collective-permute-start.82
  283.8 1.9 collective-permute-start.83
  286.5 2.6 collective-permute-start.87
  289.7 1.4 collective-permute-done.87.refs_9_
  291.1 1.9 collective-permute-start.89
  293.0 5.2 %collective-permute-done.88.refs_10_ = bf16[16,128]{1,0:T(8,128)(2,1)S(1)} collective-permute-done((bf16[16,128]{1,0:T(8,128)(2,1)S(1)}, bf16[16,128]{1,0:T(8,128)(2,1)S(1)}, u32[]{:S(2)}, u32[]{:S(2)}) %collective-permute-start.88) | collective-permute-done | bytes 4128 | tf_op jit(solution)/shard_map/ppermute | solution.py:912
  298.2 1.5 finish.1
  (294 shorter events, 44.4 us)
Async XLA Ops:
  5.6 12.1 %collective-permute-start.4 = (bf16[208,128]{1,0:T(8,128)(2,1)S(1)}, bf16[208,128]{1,0:T(8,128)(2,1)S(1)}, u32[]{:S(2)}, u32[]{:S(2)}) collective-permute-start(bf16[208,128]{1,0:T(8,128)(2,1)S(1)} %get-tuple-element.205.refs_0_), channel_id=1, source_target_pairs={{0,3},{1,2},{2,1},{3,0},{4,7},{5,6},{6,5},{7,4},{8,11},{9,10},{10,... | collective-permute-start | bytes 159752 | tf_op jit(solution)/shard_map/ppermute | solution.py:912
  10.7 12.2 %collective-permute-start.3 = (bf16[208,128]{1,0:T(8,128)(2,1)S(1)}, bf16[208,128]{1,0:T(8,128)(2,1)S(1)}, u32[]{:S(2)}, u32[]{:S(2)}) collective-permute-start(bf16[208,128]{1,0:T(8,128)(2,1)S(1)} %get-tuple-element.205.refs_0_), channel_id=1, source_target_pairs={{0,2},{1,3},{2,0},{3,1},{4,6},{5,7},{6,4},{7,5},{8,10},{9,11},{10,... | collective-permute-start | bytes 159752 | tf_op jit(solution)/shard_map/ppermute | solution.py:912
  10.7 12.2 %collective-permute-start.2 = (bf16[208,128]{1,0:T(8,128)(2,1)S(1)}, bf16[208,128]{1,0:T(8,128)(2,1)S(1)}, u32[]{:S(2)}, u32[]{:S(2)}) collective-permute-start(bf16[208,128]{1,0:T(8,128)(2,1)S(1)} %get-tuple-element.205.refs_0_), channel_id=1, source_target_pairs={{0,1},{1,0},{2,3},{3,2},{4,5},{5,4},{6,7},{7,6},{8,9},{9,8},{10,11... | collective-permute-start | bytes 159752 | tf_op jit(solution)/shard_map/ppermute | solution.py:912
  11.4 17.9 %collective-permute-start.9 = (bf16[704,128]{1,0:T(8,128)(2,1)S(1)}, bf16[704,128]{1,0:T(8,128)(2,1)S(1)}, u32[]{:S(2)}, u32[]{:S(2)}) collective-permute-start(bf16[704,128]{1,0:T(8,128)(2,1)S(1)} %get-tuple-element.211.refs_0_), channel_id=1, source_target_pairs={{0,3},{1,2},{2,1},{3,0},{4,7},{5,6},{6,5},{7,4},{8,11},{9,10},{10,... | collective-permute-start | bytes 540680 | tf_op jit(solution)/shard_map/ppermute | solution.py:912
  15.2 12.5 %collective-permute-start.1 = (bf16[2,256,512]{2,1,0:T(8,128)(2,1)S(1)}, bf16[2,256,512]{2,1,0:T(8,128)(2,1)S(1)}, u32[]{:S(2)}, u32[]{:S(2)}) collective-permute-start(bf16[2,256,512]{2,1,0:T(8,128)(2,1)S(1)} %copy-done.12), channel_id=1, source_target_pairs={{0,8},{4,12},{8,0},{12,4},{1,9},{5,13},{9,1},{13,5},{2,10},{6,14},... | collective-permute-start | bytes 1572872 | tf_op jit(solution)/shard_map/ppermute | solution.py:912
  17.6 13.4 %collective-permute-start.8 = (bf16[704,128]{1,0:T(8,128)(2,1)S(1)}, bf16[704,128]{1,0:T(8,128)(2,1)S(1)}, u32[]{:S(2)}, u32[]{:S(2)}) collective-permute-start(bf16[704,128]{1,0:T(8,128)(2,1)S(1)} %get-tuple-element.211.refs_0_), channel_id=1, source_target_pairs={{0,2},{1,3},{2,0},{3,1},{4,6},{5,7},{6,4},{7,5},{8,10},{9,11},{10,... | collective-permute-start | bytes 540680 | tf_op jit(solution)/shard_map/ppermute | solution.py:912
  22.9 9.2 %collective-permute-start.7 = (bf16[704,128]{1,0:T(8,128)(2,1)S(1)}, bf16[704,128]{1,0:T(8,128)(2,1)S(1)}, u32[]{:S(2)}, u32[]{:S(2)}) collective-permute-start(bf16[704,128]{1,0:T(8,128)(2,1)S(1)} %get-tuple-element.211.refs_0_), channel_id=1, source_target_pairs={{0,1},{1,0},{2,3},{3,2},{4,5},{5,4},{6,7},{7,6},{8,9},{9,8},{10,11... | collective-permute-start | bytes 540680 | tf_op jit(solution)/shard_map/ppermute | solution.py:912
  22.9 13.7 %collective-permute-start = (bf16[2,256,512]{2,1,0:T(8,128)(2,1)S(1)}, bf16[2,256,512]{2,1,0:T(8,128)(2,1)S(1)}, u32[]{:S(2)}, u32[]{:S(2)}) collective-permute-start(bf16[2,256,512]{2,1,0:T(8,128)(2,1)S(1)} %copy-done.12), channel_id=1, source_target_pairs={{0,4},{4,0},{8,12},{12,8},{1,5},{5,1},{9,13},{13,9},{2,6},{6,2},{1... | collective-permute-start | bytes 1572872 | tf_op jit(solution)/shard_map/ppermute | solution.py:912
  29.3 8.8 %collective-permute-start.5 = (bf16[2,256,512]{2,1,0:T(8,128)(2,1)S(1)}, bf16[2,256,512]{2,1,0:T(8,128)(2,1)S(1)}, u32[]{:S(2)}, u32[]{:S(2)}) collective-permute-start(bf16[2,256,512]{2,1,0:T(8,128)(2,1)S(1)} %get-tuple-element.209), channel_id=1, source_target_pairs={{0,4},{4,0},{8,12},{12,8},{1,5},{5,1},{9,13},{13,9},{2,6},{6,2},{1... | collective-permute-start | bytes 1572872 | tf_op jit(solution)/shard_map/ppermute | solution.py:912
  32.2 21.6 %collective-permute-start.20 = (bf16[896,128]{1,0:T(8,128)(2,1)S(1)}, bf16[896,128]{1,0:T(8,128)(2,1)S(1)}, u32[]{:S(2)}, u32[]{:S(2)}) collective-permute-start(bf16[896,128]{1,0:T(8,128)(2,1)S(1)} %get-tuple-element.222.refs_0_), channel_id=1, source_target_pairs={{0,3},{1,2},{2,1},{3,0},{4,7},{5,6},{6,5},{7,4},{8,11},{9,10},{10,... | collective-permute-start | bytes 688136 | tf_op jit(solution)/shard_map/ppermute | solution.py:912
  33.7 20.1 %collective-permute-start.19 = (bf16[896,128]{1,0:T(8,128)(2,1)S(1)}, bf16[896,128]{1,0:T(8,128)(2,1)S(1)}, u32[]{:S(2)}, u32[]{:S(2)}) collective-permute-start(bf16[896,128]{1,0:T(8,128)(2,1)S(1)} %get-tuple-element.222.refs_0_), channel_id=1, source_target_pairs={{0,2},{1,3},{2,0},{3,1},{4,6},{5,7},{6,4},{7,5},{8,10},{9,11},{10,... | collective-permute-start | bytes 688136 | tf_op jit(solution)/shard_map/ppermute | solution.py:912
  33.7 20.1 %collective-permute-start.18 = (bf16[896,128]{1,0:T(8,128)(2,1)S(1)}, bf16[896,128]{1,0:T(8,128)(2,1)S(1)}, u32[]{:S(2)}, u32[]{:S(2)}) collective-permute-start(bf16[896,128]{1,0:T(8,128)(2,1)S(1)} %get-tuple-element.222.refs_0_), channel_id=1, source_target_pairs={{0,1},{1,0},{2,3},{3,2},{4,5},{5,4},{6,7},{7,6},{8,9},{9,8},{10,11... | collective-permute-start | bytes 688136 | tf_op jit(solution)/shard_map/ppermute | solution.py:912
  36.7 17.2 %collective-permute-start.14 = (bf16[4,704,128]{2,1,0:T(8,128)(2,1)S(1)}, bf16[4,704,128]{2,1,0:T(8,128)(2,1)S(1)}, u32[]{:S(2)}, u32[]{:S(2)}) collective-permute-start(bf16[4,704,128]{2,1,0:T(8,128)(2,1)S(1)} %get-tuple-element.221.refs_9_.refs_15_.refs_10_), channel_id=1, source_target_pairs={{0,8},{4,12},{8,0},{12,4},{1,9},{5,13},{9,1},{13,5},{2,10},{6,14},... | collective-permute-start | bytes 2162696 | tf_op jit(solution)/shard_map/ppermute | solution.py:912
  38.1 15.8 %collective-permute-start.13 = (bf16[4,704,128]{2,1,0:T(8,128)(2,1)S(1)}, bf16[4,704,128]{2,1,0:T(8,128)(2,1)S(1)}, u32[]{:S(2)}, u32[]{:S(2)}) collective-permute-start(bf16[4,704,128]{2,1,0:T(8,128)(2,1)S(1)} %get-tuple-element.221.refs_9_.refs_15_.refs_10_), channel_id=1, source_target_pairs={{0,16},{16,0},{1,17},{17,1},{2,18},{18,2},{3,19},{19,3},{4,20},{20... | collective-permute-start | bytes 2162696 | tf_op jit(solution)/shard_map/ppermute | solution.py:912
  54.0 12.1 %collective-permute-start.22 = (bf16[4,320,128]{2,1,0:T(8,128)(2,1)S(1)}, bf16[4,320,128]{2,1,0:T(8,128)(2,1)S(1)}, u32[]{:S(2)}, u32[]{:S(2)}) collective-permute-start(bf16[4,320,128]{2,1,0:T(8,128)(2,1)S(1)} %get-tuple-element.225), channel_id=1, source_target_pairs={{0,8},{4,12},{8,0},{12,4},{1,9},{5,13},{9,1},{13,5},{2,10},{6,14},... | collective-permute-start | bytes 983048 | tf_op jit(solution)/shard_map/ppermute | solution.py:912
  54.7 11.4 %collective-permute-start.11 = (bf16[2,2,256,128]{3,2,1,0:T(8,128)(2,1)S(1)}, bf16[2,2,256,128]{3,2,1,0:T(8,128)(2,1)S(1)}, u32[]{:S(2)}, u32[]{:S(2)}) collective-permute-start(bf16[2,2,256,128]{3,2,1,0:T(8,128)(2,1)S(1)} %get-tuple-element.220), channel_id=1, source_target_pairs={{0,8},{4,12},{8,0},{12,4},{1,9},{5,13},{9,1},{13,5},{2,10},{6,14},... | collective-permute-start | bytes 786440 | tf_op jit(solution)/shard_map/ppermute | solution.py:912
  56.1 12.2 %collective-permute-start.15 = (bf16[4,704,128]{2,1,0:T(8,128)(2,1)S(1)}, bf16[4,704,128]{2,1,0:T(8,128)(2,1)S(1)}, u32[]{:S(2)}, u32[]{:S(2)}) collective-permute-start(bf16[4,704,128]{2,1,0:T(8,128)(2,1)S(1)} %get-tuple-element.221.refs_9_.refs_15_.refs_10_), channel_id=1, source_target_pairs={{0,4},{4,0},{8,12},{12,8},{1,5},{5,1},{9,13},{13,9},{2,6},{6,2},{1... | collective-permute-start | bytes 2162696 | tf_op jit(solution)/shard_map/ppermute | solution.py:912
  56.1 11.7 %collective-permute-start.10 = (bf16[2,256,128]{2,1,0:T(8,128)(2,1)S(1)}, bf16[2,256,128]{2,1,0:T(8,128)(2,1)S(1)}, u32[]{:S(2)}, u32[]{:S(2)}) collective-permute-start(bf16[2,256,128]{2,1,0:T(8,128)(2,1)S(1)} %get-tuple-element.219), channel_id=1, source_target_pairs={{0,4},{4,0},{8,12},{12,8},{1,5},{5,1},{9,13},{13,9},{2,6},{6,2},{1... | collective-permute-start | bytes 393224 | tf_op jit(solution)/shard_map/ppermute | solution.py:912
  56.6 11.0 %collective-permute-start.21 = (bf16[4,384,128]{2,1,0:T(8,128)(2,1)S(1)}, bf16[4,384,128]{2,1,0:T(8,128)(2,1)S(1)}, u32[]{:S(2)}, u32[]{:S(2)}) collective-permute-start(bf16[4,384,128]{2,1,0:T(8,128)(2,1)S(1)} %get-tuple-element.224), channel_id=1, source_target_pairs={{0,16},{16,0},{1,17},{17,1},{2,18},{18,2},{3,19},{19,3},{4,20},{20... | collective-permute-start | bytes 1179656 | tf_op jit(solution)/shard_map/ppermute | solution.py:912
  70.7 29.7 %collective-permute-start.33 = (bf16[4,704,128]{2,1,0:T(8,128)(2,1)S(1)}, bf16[4,704,128]{2,1,0:T(8,128)(2,1)S(1)}, u32[]{:S(2)}, u32[]{:S(2)}) collective-permute-start(bf16[4,704,128]{2,1,0:T(8,128)(2,1)S(1)} %get-tuple-element.235.refs_9_.refs_7_.refs_10_), channel_id=1, source_target_pairs={{0,16},{16,0},{1,17},{17,1},{2,18},{18,2},{3,19},{19,3},{4,20},{20... | collective-permute-start | bytes 2162696 | tf_op jit(solution)/shard_map/ppermute | solution.py:912
  71.3 29.7 %collective-permute-start.32 = (bf16[4,704,128]{2,1,0:T(8,128)(2,1)S(1)}, bf16[4,704,128]{2,1,0:T(8,128)(2,1)S(1)}, u32[]{:S(2)}, u32[]{:S(2)}) collective-permute-start(bf16[4,704,128]{2,1,0:T(8,128)(2,1)S(1)} %get-tuple-element.235.refs_9_.refs_7_.refs_10_), channel_id=1, source_target_pairs={{0,8},{4,12},{8,0},{12,4},{1,9},{5,13},{9,1},{13,5},{2,10},{6,14},... | collective-permute-start | bytes 2162696 | tf_op jit(solution)/shard_map/ppermute | solution.py:912
  84.8 11.1 %collective-permute-start.27 = (bf16[256,512]{1,0:T(8,128)(2,1)S(1)}, bf16[256,512]{1,0:T(8,128)(2,1)S(1)}, u32[]{:S(2)}, u32[]{:S(2)}) collective-permute-start(bf16[256,512]{1,0:T(8,128)(2,1)S(1)} %get-tuple-element.232.refs_3_.refs_8_.refs_9_), channel_id=1, source_target_pairs={{0,8},{4,12},{8,0},{12,4},{1,9},{5,13},{9,1},{13,5},{2,10},{6,14},... | collective-permute-start | bytes 786440 | tf_op jit(solution)/shard_map/ppermute | solution.py:912
  85.2 15.2 %collective-permute-start.28 = (bf16[256,512]{1,0:T(8,128)(2,1)S(1)}, bf16[256,512]{1,0:T(8,128)(2,1)S(1)}, u32[]{:S(2)}, u32[]{:S(2)}) collective-permute-start(bf16[256,512]{1,0:T(8,128)(2,1)S(1)} %get-tuple-element.233.refs_4_.refs_9_), channel_id=1, source_target_pairs={{0,8},{4,12},{8,0},{12,4},{1,9},{5,13},{9,1},{13,5},{2,10},{6,14},... | collective-permute-start | bytes 786440 | tf_op jit(solution)/shard_map/ppermute | solution.py:912
  93.1 25.9 %collective-permute-start.37 = (bf16[4,704,128]{2,1,0:T(8,128)(2,1)S(1)}, bf16[4,704,128]{2,1,0:T(8,128)(2,1)S(1)}, u32[]{:S(2)}, u32[]{:S(2)}) collective-permute-start(bf16[4,704,128]{2,1,0:T(8,128)(2,1)S(1)} %get-tuple-element.235.refs_9_.refs_7_.refs_10_), channel_id=1, source_target_pairs={{0,4},{4,0},{8,12},{12,8},{1,5},{5,1},{9,13},{13,9},{2,6},{6,2},{1... | collective-permute-start | bytes 2162696 | tf_op jit(solution)/shard_map/ppermute | solution.py:912
  101.1 16.4 %collective-permute-start.41 = (bf16[4,320,128]{2,1,0:T(8,128)(2,1)S(1)}, bf16[4,320,128]{2,1,0:T(8,128)(2,1)S(1)}, u32[]{:S(2)}, u32[]{:S(2)}) collective-permute-start(bf16[4,320,128]{2,1,0:T(8,128)(2,1)S(1)} %get-tuple-element.242), channel_id=1, source_target_pairs={{0,8},{4,12},{8,0},{12,4},{1,9},{5,13},{9,1},{13,5},{2,10},{6,14},... | collective-permute-start | bytes 983048 | tf_op jit(solution)/shard_map/ppermute | solution.py:912
  102.9 16.0 %collective-permute-start.40 = (bf16[4,384,128]{2,1,0:T(8,128)(2,1)S(1)}, bf16[4,384,128]{2,1,0:T(8,128)(2,1)S(1)}, u32[]{:S(2)}, u32[]{:S(2)}) collective-permute-start(bf16[4,384,128]{2,1,0:T(8,128)(2,1)S(1)} %get-tuple-element.241), channel_id=1, source_target_pairs={{0,16},{16,0},{1,17},{17,1},{2,18},{18,2},{3,19},{19,3},{4,20},{20... | collective-permute-start | bytes 1179656 | tf_op jit(solution)/shard_map/ppermute | solution.py:912
  103.4 24.2 %collective-permute-start.38 = (bf16[4,704,128]{2,1,0:T(8,128)(2,1)S(1)}, bf16[4,704,128]{2,1,0:T(8,128)(2,1)}, u32[]{:S(2)}, u32[]{:S(2)}) collective-permute-start(bf16[4,704,128]{2,1,0:T(8,128)(2,1)S(1)} %collective-permute-done.33.refs_0_.refs_1_.refs_10_.refs_8_.refs_11_), channel_id=1, source_target_pairs={{0,4},{4,0},{8,12},{12,8},{1,5},{5,1},{9,13},{13,9},{2,6},{6,2},{1... | collective-permute-start | bytes 2162696 | tf_op jit(solution)/shard_map/ppermute | solution.py:912
  103.5 24.1 %collective-permute-start.39 = (bf16[4,704,128]{2,1,0:T(8,128)(2,1)S(1)}, bf16[4,704,128]{2,1,0:T(8,128)(2,1)}, u32[]{:S(2)}, u32[]{:S(2)}) collective-permute-start(bf16[4,704,128]{2,1,0:T(8,128)(2,1)S(1)} %collective-permute-done.32.refs_1_.refs_0_.refs_11_.refs_9_.refs_12_), channel_id=1, source_target_pairs={{0,4},{4,0},{8,12},{12,8},{1,5},{5,1},{9,13},{13,9},{2,6},{6,2},{1... | collective-permute-start | bytes 2162696 | tf_op jit(solution)/shard_map/ppermute | solution.py:912
  117.6 8.5 %collective-permute-start.35 = (bf16[2,2,256,128]{3,2,1,0:T(8,128)(2,1)}, bf16[2,2,256,128]{3,2,1,0:T(8,128)(2,1)S(1)}, u32[]{:S(2)}, u32[]{:S(2)}) collective-permute-start(bf16[2,2,256,128]{3,2,1,0:T(8,128)(2,1)} %get-tuple-element.240), channel_id=1, source_target_pairs={{0,8},{4,12},{8,0},{12,4},{1,9},{5,13},{9,1},{13,5},{2,10},{6,14},... | collective-permute-start | bytes 786440 | tf_op jit(solution)/shard_map/ppermute | solution.py:912
  147.5 9.5 %collective-permute-start.44 = (bf16[2,256,128]{2,1,0:T(8,128)(2,1)S(1)}, bf16[2,256,128]{2,1,0:T(8,128)(2,1)S(1)}, u32[]{:S(2)}, u32[]{:S(2)}) collective-permute-start(bf16[2,256,128]{2,1,0:T(8,128)(2,1)S(1)} %get-tuple-element.267), channel_id=1, source_target_pairs={{0,4},{4,0},{8,12},{12,8},{1,5},{5,1},{9,13},{13,9},{2,6},{6,2},{1... | collective-permute-start | bytes 393224 | tf_op jit(solution)/shard_map/ppermute | solution.py:912
  147.7 9.2 %collective-permute-start.45 = (bf16[2,2,256,128]{3,2,1,0:T(8,128)(2,1)S(1)}, bf16[2,2,256,128]{3,2,1,0:T(8,128)(2,1)S(1)}, u32[]{:S(2)}, u32[]{:S(2)}) collective-permute-start(bf16[2,2,256,128]{3,2,1,0:T(8,128)(2,1)S(1)} %get-tuple-element.268), channel_id=1, source_target_pairs={{0,8},{4,12},{8,0},{12,4},{1,9},{5,13},{9,1},{13,5},{2,10},{6,14},... | collective-permute-start | bytes 786440 | tf_op jit(solution)/shard_map/ppermute | solution.py:912
  156.3 11.4 %collective-permute-start.48 = (bf16[16,320,128]{2,1,0:T(8,128)(2,1)S(1)}, bf16[16,320,128]{2,1,0:T(8,128)(2,1)S(1)}, u32[]{:S(2)}, u32[]{:S(2)}) collective-permute-start(bf16[16,320,128]{2,1,0:T(8,128)(2,1)S(1)} %get-tuple-element.273), channel_id=1, source_target_pairs={{0,4},{4,0},{8,12},{12,8},{1,5},{5,1},{9,13},{13,9},{2,6},{6,2},{1... | collective-permute-start | bytes 3932168 | tf_op jit(solution)/shard_map/ppermute | solution.py:912
  156.5 10.9 %collective-permute-start.49 = (bf16[16,384,128]{2,1,0:T(8,128)(2,1)S(1)}, bf16[16,384,128]{2,1,0:T(8,128)(2,1)S(1)}, u32[]{:S(2)}, u32[]{:S(2)}) collective-permute-start(bf16[16,384,128]{2,1,0:T(8,128)(2,1)S(1)} %get-tuple-element.275), channel_id=1, source_target_pairs={{0,4},{4,0},{8,12},{12,8},{1,5},{5,1},{9,13},{13,9},{2,6},{6,2},{1... | collective-permute-start | bytes 4718600 | tf_op jit(solution)/shard_map/ppermute | solution.py:912
  168.1 17.1 %collective-permute-start.51 = (bf16[8,320,128]{2,1,0:T(8,128)(2,1)S(1)}, bf16[8,320,128]{2,1,0:T(8,128)(2,1)S(1)}, u32[]{:S(2)}, u32[]{:S(2)}) collective-permute-start(bf16[8,320,128]{2,1,0:T(8,128)(2,1)S(1)} %get-tuple-element.285), channel_id=1, source_target_pairs={{0,16},{16,0},{1,17},{17,1},{2,18},{18,2},{3,19},{19,3},{4,20},{20... | collective-permute-start | bytes 1966088 | tf_op jit(solution)/shard_map/ppermute | solution.py:912
  179.1 10.9 %collective-permute-start.52 = (bf16[1,256,512]{2,1,0:T(8,128)(2,1)S(1)}, bf16[1,256,512]{2,1,0:T(8,128)(2,1)S(1)}, u32[]{:S(2)}, u32[]{:S(2)}) collective-permute-start(bf16[1,256,512]{2,1,0:T(8,128)(2,1)S(1)} %get-tuple-element.289), channel_id=1, source_target_pairs={{0,8},{4,12},{8,0},{12,4},{1,9},{5,13},{9,1},{13,5},{2,10},{6,14},... | collective-permute-start | bytes 786440 | tf_op jit(solution)/shard_map/ppermute | solution.py:912
  185.8 9.3 %collective-permute-start.53 = (bf16[1,256,512]{2,1,0:T(8,128)(2,1)S(1)}, bf16[1,256,512]{2,1,0:T(8,128)(2,1)S(1)}, u32[]{:S(2)}, u32[]{:S(2)}) collective-permute-start(bf16[1,256,512]{2,1,0:T(8,128)(2,1)S(1)} %get-tuple-element.290), channel_id=1, source_target_pairs={{0,8},{4,12},{8,0},{12,4},{1,9},{5,13},{9,1},{13,5},{2,10},{6,14},... | collective-permute-start | bytes 786440 | tf_op jit(solution)/shard_map/ppermute | solution.py:912
  186.7 18.1 %collective-permute-start.55 = (bf16[4,192,128]{2,1,0:T(8,128)(2,1)S(1)}, bf16[4,192,128]{2,1,0:T(8,128)(2,1)S(1)}, u32[]{:S(2)}, u32[]{:S(2)}) collective-permute-start(bf16[4,192,128]{2,1,0:T(8,128)(2,1)S(1)} %get-tuple-element.404), channel_id=1, source_target_pairs={{0,16},{16,0},{1,17},{17,1},{2,18},{18,2},{3,19},{19,3},{4,20},{20... | collective-permute-start | bytes 589832 | tf_op jit(solution)/shard_map/ppermute | solution.py:912
  188.2 21.5 %collective-permute-start.54 = (bf16[8,384,128]{2,1,0:T(8,128)(2,1)S(1)}, bf16[8,384,128]{2,1,0:T(8,128)(2,1)S(1)}, u32[]{:S(2)}, u32[]{:S(2)}) collective-permute-start(bf16[8,384,128]{2,1,0:T(8,128)(2,1)S(1)} %get-tuple-element.304), channel_id=1, source_target_pairs={{0,16},{16,0},{1,17},{17,1},{2,18},{18,2},{3,19},{19,3},{4,20},{20... | collective-permute-start | bytes 2359304 | tf_op jit(solution)/shard_map/ppermute | solution.py:912
  188.8 16.0 %collective-permute-start.56 = (bf16[4,320,128]{2,1,0:T(8,128)(2,1)S(1)}, bf16[4,320,128]{2,1,0:T(8,128)(2,1)S(1)}, u32[]{:S(2)}, u32[]{:S(2)}) collective-permute-start(bf16[4,320,128]{2,1,0:T(8,128)(2,1)S(1)} %get-tuple-element.307), channel_id=1, source_target_pairs={{0,8},{4,12},{8,0},{12,4},{1,9},{5,13},{9,1},{13,5},{2,10},{6,14},... | collective-permute-start | bytes 983048 | tf_op jit(solution)/shard_map/ppermute | solution.py:912
  203.8 14.6 %collective-permute-start.57 = (bf16[2,256,128]{2,1,0:T(8,128)(2,1)S(1)}, bf16[2,256,128]{2,1,0:T(8,128)(2,1)S(1)}, u32[]{:S(2)}, u32[]{:S(2)}) collective-permute-start(bf16[2,256,128]{2,1,0:T(8,128)(2,1)S(1)} %get-tuple-element.317), channel_id=1, source_target_pairs={{0,4},{4,0},{8,12},{12,8},{1,5},{5,1},{9,13},{13,9},{2,6},{6,2},{1... | collective-permute-start | bytes 393224 | tf_op jit(solution)/shard_map/ppermute | solution.py:912
  203.9 14.4 %collective-permute-start.58 = (bf16[2,2,256,128]{3,2,1,0:T(8,128)(2,1)S(1)}, bf16[2,2,256,128]{3,2,1,0:T(8,128)(2,1)S(1)}, u32[]{:S(2)}, u32[]{:S(2)}) collective-permute-start(bf16[2,2,256,128]{3,2,1,0:T(8,128)(2,1)S(1)} %get-tuple-element.318), channel_id=1, source_target_pairs={{0,8},{4,12},{8,0},{12,4},{1,9},{5,13},{9,1},{13,5},{2,10},{6,14},... | collective-permute-start | bytes 786440 | tf_op jit(solution)/shard_map/ppermute | solution.py:912
  205.5 25.6 %collective-permute-start.61 = (bf16[512,128]{1,0:T(8,128)(2,1)S(1)}, bf16[512,128]{1,0:T(8,128)(2,1)S(1)}, u32[]{:S(2)}, u32[]{:S(2)}) collective-permute-start(bf16[512,128]{1,0:T(8,128)(2,1)S(1)} %get-tuple-element.326), channel_id=1, source_target_pairs={{0,1},{1,0},{2,3},{3,2},{4,5},{5,4},{6,7},{7,6},{8,9},{9,8},{10,11... | collective-permute-start | bytes 393224 | tf_op jit(solution)/shard_map/ppermute | solution.py:912
  206.4 26.0 %collective-permute-start.62 = (bf16[512,128]{1,0:T(8,128)(2,1)S(1)}, bf16[512,128]{1,0:T(8,128)(2,1)S(1)}, u32[]{:S(2)}, u32[]{:S(2)}) collective-permute-start(bf16[512,128]{1,0:T(8,128)(2,1)S(1)} %get-tuple-element.327), channel_id=1, source_target_pairs={{0,2},{1,3},{2,0},{3,1},{4,6},{5,7},{6,4},{7,5},{8,10},{9,11},{10,... | collective-permute-start | bytes 393224 | tf_op jit(solution)/shard_map/ppermute | solution.py:912
  209.9 15.8 %collective-permute-start.66 = (bf16[4,384,128]{2,1,0:T(8,128)(2,1)S(1)}, bf16[4,384,128]{2,1,0:T(8,128)(2,1)S(1)}, u32[]{:S(2)}, u32[]{:S(2)}) collective-permute-start(bf16[4,384,128]{2,1,0:T(8,128)(2,1)S(1)} %get-tuple-element.334), channel_id=1, source_target_pairs={{0,8},{4,12},{8,0},{12,4},{1,9},{5,13},{9,1},{13,5},{2,10},{6,14},... | collective-permute-start | bytes 1179656 | tf_op jit(solution)/shard_map/ppermute | solution.py:912
  218.5 11.3 %collective-permute-start.64 = (bf16[16,320,128]{2,1,0:T(8,128)(2,1)S(1)}, bf16[16,320,128]{2,1,0:T(8,128)(2,1)S(1)}, u32[]{:S(2)}, u32[]{:S(2)}) collective-permute-start(bf16[16,320,128]{2,1,0:T(8,128)(2,1)S(1)} %get-tuple-element.330), channel_id=1, source_target_pairs={{0,4},{4,0},{8,12},{12,8},{1,5},{5,1},{9,13},{13,9},{2,6},{6,2},{1... | collective-permute-start | bytes 3932168 | tf_op jit(solution)/shard_map/ppermute | solution.py:912
  219.9 9.3 %collective-permute-start.65 = (bf16[16,384,128]{2,1,0:T(8,128)(2,1)S(1)}, bf16[16,384,128]{2,1,0:T(8,128)(2,1)S(1)}, u32[]{:S(2)}, u32[]{:S(2)}) collective-permute-start(bf16[16,384,128]{2,1,0:T(8,128)(2,1)S(1)} %get-tuple-element.332), channel_id=1, source_target_pairs={{0,4},{4,0},{8,12},{12,8},{1,5},{5,1},{9,13},{13,9},{2,6},{6,2},{1... | collective-permute-start | bytes 4718600 | tf_op jit(solution)/shard_map/ppermute | solution.py:912
  225.6 7.7 %collective-permute-start.63 = (bf16[512,128]{1,0:T(8,128)(2,1)S(1)}, bf16[512,128]{1,0:T(8,128)(2,1)S(1)}, u32[]{:S(2)}, u32[]{:S(2)}) collective-permute-start(bf16[512,128]{1,0:T(8,128)(2,1)S(1)} %get-tuple-element.328), channel_id=1, source_target_pairs={{0,3},{1,2},{2,1},{3,0},{4,7},{5,6},{6,5},{7,4},{8,11},{9,10},{10,... | collective-permute-start | bytes 393224 | tf_op jit(solution)/shard_map/ppermute | solution.py:912
  230.1 17.1 %collective-permute-start.69 = (bf16[8,320,128]{2,1,0:T(8,128)(2,1)S(1)}, bf16[8,320,128]{2,1,0:T(8,128)(2,1)S(1)}, u32[]{:S(2)}, u32[]{:S(2)}) collective-permute-start(bf16[8,320,128]{2,1,0:T(8,128)(2,1)S(1)} %get-tuple-element.351), channel_id=1, source_target_pairs={{0,8},{4,12},{8,0},{12,4},{1,9},{5,13},{9,1},{13,5},{2,10},{6,14},... | collective-permute-start | bytes 1966088 | tf_op jit(solution)/shard_map/ppermute | solution.py:912
  231.0 19.6 %collective-permute-start.68 = (bf16[8,384,128]{2,1,0:T(8,128)(2,1)S(1)}, bf16[8,384,128]{2,1,0:T(8,128)(2,1)S(1)}, u32[]{:S(2)}, u32[]{:S(2)}) collective-permute-start(bf16[8,384,128]{2,1,0:T(8,128)(2,1)S(1)} %get-tuple-element.349), channel_id=1, source_target_pairs={{0,16},{16,0},{1,17},{17,1},{2,18},{18,2},{3,19},{19,3},{4,20},{20... | collective-permute-start | bytes 2359304 | tf_op jit(solution)/shard_map/ppermute | solution.py:912
  243.2 8.8 %collective-permute-start.67 = (bf16[2,256,512]{2,1,0:T(8,128)(2,1)S(1)}, bf16[2,256,512]{2,1,0:T(8,128)(2,1)S(1)}, u32[]{:S(2)}, u32[]{:S(2)}) collective-permute-start(bf16[2,256,512]{2,1,0:T(8,128)(2,1)S(1)} %get-tuple-element.347), channel_id=1, source_target_pairs={{0,4},{4,0},{8,12},{12,8},{1,5},{5,1},{9,13},{13,9},{2,6},{6,2},{1... | collective-permute-start | bytes 1572872 | tf_op jit(solution)/shard_map/ppermute | solution.py:912
  243.3 10.4 %collective-permute-start.73 = (bf16[384,128]{1,0:T(8,128)(2,1)S(1)}, bf16[384,128]{1,0:T(8,128)(2,1)S(1)}, u32[]{:S(2)}, u32[]{:S(2)}) collective-permute-start(bf16[384,128]{1,0:T(8,128)(2,1)S(1)} %get-tuple-element.361), channel_id=1, source_target_pairs={{0,1},{1,0},{2,3},{3,2},{4,5},{5,4},{6,7},{7,6},{8,9},{9,8},{10,11... | collective-permute-start | bytes 294920 | tf_op jit(solution)/shard_map/ppermute | solution.py:912
  245.7 10.6 %collective-permute-start.74 = (bf16[384,128]{1,0:T(8,128)(2,1)S(1)}, bf16[384,128]{1,0:T(8,128)(2,1)S(1)}, u32[]{:S(2)}, u32[]{:S(2)}) collective-permute-start(bf16[384,128]{1,0:T(8,128)(2,1)S(1)} %get-tuple-element.362), channel_id=1, source_target_pairs={{0,2},{1,3},{2,0},{3,1},{4,6},{5,7},{6,4},{7,5},{8,10},{9,11},{10,... | collective-permute-start | bytes 294920 | tf_op jit(solution)/shard_map/ppermute | solution.py:912
  247.3 9.8 %collective-permute-start.75 = (bf16[384,128]{1,0:T(8,128)(2,1)S(1)}, bf16[384,128]{1,0:T(8,128)(2,1)S(1)}, u32[]{:S(2)}, u32[]{:S(2)}) collective-permute-start(bf16[384,128]{1,0:T(8,128)(2,1)S(1)} %get-tuple-element.363), channel_id=1, source_target_pairs={{0,3},{1,2},{2,1},{3,0},{4,7},{5,6},{6,5},{7,4},{8,11},{9,10},{10,... | collective-permute-start | bytes 294920 | tf_op jit(solution)/shard_map/ppermute | solution.py:912
  250.6 15.0 %collective-permute-start.70 = (bf16[1,256,512]{2,1,0:T(8,128)(2,1)S(1)}, bf16[1,256,512]{2,1,0:T(8,128)(2,1)S(1)}, u32[]{:S(2)}, u32[]{:S(2)}) collective-permute-start(bf16[1,256,512]{2,1,0:T(8,128)(2,1)S(1)} %get-tuple-element.356), channel_id=1, source_target_pairs={{0,8},{4,12},{8,0},{12,4},{1,9},{5,13},{9,1},{13,5},{2,10},{6,14},... | collective-permute-start | bytes 786440 | tf_op jit(solution)/shard_map/ppermute | solution.py:912
  252.0 28.5 %collective-permute-start.79 = (bf16[4,192,128]{2,1,0:T(8,128)(2,1)S(1)}, bf16[4,192,128]{2,1,0:T(8,128)(2,1)S(1)}, u32[]{:S(2)}, u32[]{:S(2)}) collective-permute-start(bf16[4,192,128]{2,1,0:T(8,128)(2,1)S(1)} %get-tuple-element.402), channel_id=1, source_target_pairs={{0,16},{16,0},{1,17},{17,1},{2,18},{18,2},{3,19},{19,3},{4,20},{20... | collective-permute-start | bytes 589832 | tf_op jit(solution)/shard_map/ppermute | solution.py:912
  253.7 11.2 %collective-permute-start.72 = (bf16[4,320,128]{2,1,0:T(8,128)(2,1)S(1)}, bf16[4,320,128]{2,1,0:T(8,128)(2,1)S(1)}, u32[]{:S(2)}, u32[]{:S(2)}) collective-permute-start(bf16[4,320,128]{2,1,0:T(8,128)(2,1)S(1)} %get-tuple-element.359), channel_id=1, source_target_pairs={{0,16},{16,0},{1,17},{17,1},{2,18},{18,2},{3,19},{19,3},{4,20},{20... | collective-permute-start | bytes 983048 | tf_op jit(solution)/shard_map/ppermute | solution.py:912
  256.3 9.4 %collective-permute-start.71 = (bf16[1,256,512]{2,1,0:T(8,128)(2,1)S(1)}, bf16[1,256,512]{2,1,0:T(8,128)(2,1)S(1)}, u32[]{:S(2)}, u32[]{:S(2)}) collective-permute-start(bf16[1,256,512]{2,1,0:T(8,128)(2,1)S(1)} %get-tuple-element.357), channel_id=1, source_target_pairs={{0,8},{4,12},{8,0},{12,4},{1,9},{5,13},{9,1},{13,5},{2,10},{6,14},... | collective-permute-start | bytes 786440 | tf_op jit(solution)/shard_map/ppermute | solution.py:912
  257.1 23.4 %collective-permute-start.80 = (bf16[4,384,128]{2,1,0:T(8,128)(2,1)S(1)}, bf16[4,384,128]{2,1,0:T(8,128)(2,1)S(1)}, u32[]{:S(2)}, u32[]{:S(2)}) collective-permute-start(bf16[4,384,128]{2,1,0:T(8,128)(2,1)S(1)} %get-tuple-element.376), channel_id=1, source_target_pairs={{0,8},{4,12},{8,0},{12,4},{1,9},{5,13},{9,1},{13,5},{2,10},{6,14},... | collective-permute-start | bytes 1179656 | tf_op jit(solution)/shard_map/ppermute | solution.py:912
  275.7 8.1 %collective-permute-start.76 = (bf16[320,128]{1,0:T(8,128)(2,1)S(1)}, bf16[320,128]{1,0:T(8,128)(2,1)S(1)}, u32[]{:S(2)}, u32[]{:S(2)}) collective-permute-start(bf16[320,128]{1,0:T(8,128)(2,1)S(1)} %get-tuple-element.371), channel_id=1, source_target_pairs={{0,1},{1,0},{2,3},{3,2},{4,5},{5,4},{6,7},{7,6},{8,9},{9,8},{10,11... | collective-permute-start | bytes 245768 | tf_op jit(solution)/shard_map/ppermute | solution.py:912
  276.0 9.7 %collective-permute-start.77 = (bf16[320,128]{1,0:T(8,128)(2,1)S(1)}, bf16[320,128]{1,0:T(8,128)(2,1)S(1)}, u32[]{:S(2)}, u32[]{:S(2)}) collective-permute-start(bf16[320,128]{1,0:T(8,128)(2,1)S(1)} %get-tuple-element.372), channel_id=1, source_target_pairs={{0,2},{1,3},{2,0},{3,1},{4,6},{5,7},{6,4},{7,5},{8,10},{9,11},{10,... | collective-permute-start | bytes 245768 | tf_op jit(solution)/shard_map/ppermute | solution.py:912
  281.2 17.0 %collective-permute-start.81 = (bf16[576,128]{1,0:T(8,128)(2,1)S(1)}, bf16[576,128]{1,0:T(8,128)(2,1)S(1)}, u32[]{:S(2)}, u32[]{:S(2)}) collective-permute-start(bf16[576,128]{1,0:T(8,128)(2,1)S(1)} %get-tuple-element.381), channel_id=1, source_target_pairs={{0,1},{1,0},{2,3},{3,2},{4,5},{5,4},{6,7},{7,6},{8,9},{9,8},{10,11... | collective-permute-start | bytes 442376 | tf_op jit(solution)/shard_map/ppermute | solution.py:912
  281.3 16.9 %collective-permute-start.82 = (bf16[576,128]{1,0:T(8,128)(2,1)S(1)}, bf16[576,128]{1,0:T(8,128)(2,1)S(1)}, u32[]{:S(2)}, u32[]{:S(2)}) collective-permute-start(bf16[576,128]{1,0:T(8,128)(2,1)S(1)} %get-tuple-element.382), channel_id=1, source_target_pairs={{0,2},{1,3},{2,0},{3,1},{4,6},{5,7},{6,4},{7,5},{8,10},{9,11},{10,... | collective-permute-start | bytes 442376 | tf_op jit(solution)/shard_map/ppermute | solution.py:912
  283.8 14.4 %collective-permute-start.83 = (bf16[576,128]{1,0:T(8,128)(2,1)S(1)}, bf16[576,128]{1,0:T(8,128)(2,1)S(1)}, u32[]{:S(2)}, u32[]{:S(2)}) collective-permute-start(bf16[576,128]{1,0:T(8,128)(2,1)S(1)} %get-tuple-element.383), channel_id=1, source_target_pairs={{0,3},{1,2},{2,1},{3,0},{4,7},{5,6},{6,5},{7,4},{8,11},{9,10},{10,... | collective-permute-start | bytes 442376 | tf_op jit(solution)/shard_map/ppermute | solution.py:912
  289.1 9.0 %collective-permute-start.88 = (bf16[16,128]{1,0:T(8,128)(2,1)S(1)}, bf16[16,128]{1,0:T(8,128)(2,1)S(1)}, u32[]{:S(2)}, u32[]{:S(2)}) collective-permute-start(bf16[16,128]{1,0:T(8,128)(2,1)S(1)} %get-tuple-element.389), channel_id=1, source_target_pairs={{0,2},{1,3},{2,0},{3,1},{4,6},{5,7},{6,4},{7,5},{8,10},{9,11},{10,... | collective-permute-start | bytes 12296 | tf_op jit(solution)/shard_map/ppermute | solution.py:912
  (82 other events, 662.8 us)
